TPU v7x, 128 devices: a whole 4x4x4 slice. The times are simulated.
128 devices in a mesh: dp: 4 (over z), ep: 32 (over x, y, core).
Axes of the slice: x: 4, y: 4, z: 4, core: 2. Of those that a mesh axis runs over, the one named last changes fastest.
Arguments:
- hidden_in: bfloat16 [2, 2048, 8, 1024], P(None, ('dp', 'ep')), parts along dimension 1, may hold values from -6 to 6
- expert_ids: int32 [2, 2048, 8], P(None, ('dp', 'ep')), parts along dimension 1, may hold values from 0 to 63, as said below
- gates: float32 [2, 2048, 8], P(None, ('dp', 'ep')), parts along dimension 1, may hold values from 0.1 to 1
- expert_weight: bfloat16 [64, 1024, 3584], P('ep'), may hold values from -0.1875 to 0.1875
- column_scale: bfloat16 [64, 3584], P('ep'), may hold values from 0.5 to 2
- replica_map: int32 [128], P('dp'), parts along dimension 0, may hold values from 0 to 63, as said below
Outputs:
- combined: bfloat16 [2, 2048, 3584], P(None, ('dp', 'ep')), parts along dimension 1
- replica_weight: bfloat16 [128, 1024, 3584], P(('dp', 'ep')), parts along dimension 0
- replica_scale: bfloat16 [128, 3584], P(('dp', 'ep')), parts along dimension 0
There are 4 independent parts, one for each index of `dp`. A program takes and returns all parts, laid end to end along the dimension named above; an argument that names none is the same for every part. Nothing has to cross between parts.
Inputs may be any that keep to these rules, and one draw needn't show every extreme that they name: `expert_ids`: each token names 8 different experts. Within one step, the 16 tokens of one device name exactly one expert 2 * 4 times, and that expert is listed in replica_map; they name every other expert at most 2 times. `replica_map`: entry d is one of the two experts owned by device (d + 16) mod 32, that is 2 * ((d + 16) mod 32) or one more; entries are distinct.
All inputs are finite; a program needn't handle non-finite values.
Results may differ from a plain program's by a relative error of at most 0.0049.
Values may be sent and summed in bfloat16 or wider, within the bound.
No kernel may reach another device: no remote copies, remote signals or barrier semaphores. Data moves between devices by JAX's collectives and lax.ppermute only.
A program may use at most 128 MiB of HBM per device.

v0:
```python
import jax
import jax.numpy as jnp
from jax import lax
from jax.sharding import PartitionSpec as P


def passed_along(block, axis, distance):
    devices = range(lax.axis_size(axis))
    route = [((i - distance) % len(devices), i) for i in devices]
    return lax.ppermute(block, axis, route)


def local(hidden_in, expert_ids, gates, expert_weight, column_scale, replica_map):
    device_total = lax.axis_size("ep")
    own_index = lax.axis_index("ep")
    half_axis = device_total // 2
    step_count, row_count, top_count, hidden_size = hidden_in.shape
    output_size = expert_weight.shape[2]
    experts = 2 * device_total
    capacity = max(4, (row_count * top_count + experts) // (experts + 1))
    item_total = row_count * top_count
    partner = replica_map[(own_index + half_axis) % device_total]
    local_pick = partner - 2 * own_index
    chosen_weight = lax.dynamic_index_in_dim(expert_weight, local_pick, 0, keepdims=True)
    chosen_scale = lax.dynamic_index_in_dim(column_scale, local_pick, 0, keepdims=True)
    replica_weight, replica_scale = passed_along((chosen_weight, chosen_scale), "ep", half_axis)
    sequence = jnp.arange(item_total, dtype=jnp.int32)
    results = []
    for step_index in range(step_count):
        activations = hidden_in[step_index].reshape(item_total, hidden_size)
        expert_list = expert_ids[step_index].reshape(item_total)
        matching = expert_list[:, None] == expert_list[None, :]
        earlier = jnp.sum(matching & (sequence[:, None] > sequence[None, :]), axis=1)
        home_device = expert_list // 2
        lane_index = expert_list % 2
        lane_count = 2
        depth_rows = 2 * capacity
        lane_weights = (expert_weight[0], expert_weight[1])
        lane_scales = (column_scale[0], column_scale[1])
        slot_index = (home_device * lane_count + lane_index) * depth_rows + earlier
        slot_total = device_total * lane_count * depth_rows
        selector = (jnp.arange(slot_total, dtype=jnp.int32)[:, None] == slot_index[None, :]).astype(
            jnp.bfloat16
        )
        outgoing = jnp.dot(selector, activations, preferred_element_type=jnp.float32).astype(
            jnp.bfloat16
        )
        outgoing = outgoing.reshape(device_total, lane_count, depth_rows, hidden_size)

        def run_experts(
            received, lane_weights=lane_weights, lane_scales=lane_scales, lane_count=lane_count
        ):
            sources = received.shape[0]
            depth_now = received.shape[2]
            pieces = []
            for lane_id in range(lane_count):
                flat_rows = received[:, lane_id].reshape(sources * depth_now, hidden_size)
                product = jnp.dot(
                    flat_rows, lane_weights[lane_id], preferred_element_type=jnp.float32
                )
                product = product * lane_scales[lane_id].astype(jnp.float32)[None, :]
                pieces.append(product.astype(jnp.bfloat16).reshape(sources, depth_now, output_size))
            stacked = jnp.stack(pieces, 1)
            return lax.all_to_all(stacked, "ep", split_axis=0, concat_axis=0, tiled=True)

        returned = run_experts(
            lax.all_to_all(outgoing, "ep", split_axis=0, concat_axis=0, tiled=True)
        )
        flat_back = returned.reshape(slot_total, output_size)
        gathered = jnp.einsum("si,sd->id", selector, flat_back, preferred_element_type=jnp.float32)
        weighted = (
            gathered.reshape(row_count, top_count, output_size) * gates[step_index][:, :, None]
        )
        results.append(jnp.sum(weighted, axis=1).astype(jnp.bfloat16))
    return (jnp.stack(results, 0), replica_weight, replica_scale)


def solution(mesh):
    in_specs = (
        P(None, ("dp", "ep"), None, None),
        P(None, ("dp", "ep"), None),
        P(None, ("dp", "ep"), None),
        P("ep", None, None),
        P("ep", None),
        P("dp"),
    )
    out_specs = (P(None, ("dp", "ep"), None), P(("dp", "ep"), None, None), P(("dp", "ep"), None))
    return jax.shard_map(local, mesh=mesh, in_specs=in_specs, out_specs=out_specs, check_vma=False)
```

profile of v0, /device:TPU:0, one launch (start us, length us, event | category | flops | bytes accessed | tf_op | source)
XLA Modules:
  0.0 321.3 jit_solution(12923866620632713222)
XLA Ops:
  2.1 2.3 convolution_convert_fusion.1
  4.5 7.4 %all-to-all-start = ((bf16[32,2,8,1024]{3,2,1,0:T(8,128)(2,1)}), bf16[32,2,8,1024]{3,2,1,0:T(8,128)(2,1)S(1)}, u32[]{:S(2)}, u32[]{:S(2)}) async-start(bf16[32,2,8,1024]{3,2,1,0:T(8,128)(2,1)} %bitcast.2), calls=%async_computation | async-start | bytes 2097152 | tf_op jit(solution)/shard_map/all_to_all | solution.py:67
  11.9 1.2 dynamic_slice.11
  13.8 0.9 convert_reduce_fusion.3
  14.7 1.4 convolution_convert_fusion
  16.1 12.6 %all-to-all-done = bf16[32,2,8,1024]{3,2,1,0:T(8,128)(2,1)S(1)} async-done(((bf16[32,2,8,1024]{3,2,1,0:T(8,128)(2,1)}), bf16[32,2,8,1024]{3,2,1,0:T(8,128)(2,1)S(1)}, u32[]{:S(2)}, u32[]{:S(2)}) %all-to-all-start) | async-done | bytes 1048608 | tf_op jit(solution)/shard_map/all_to_all | solution.py:67
  28.7 4.1 %all-to-all-start.2 = ((bf16[32,2,8,1024]{3,2,1,0:T(8,128)(2,1)}), bf16[32,2,8,1024]{3,2,1,0:T(8,128)(2,1)S(1)}, u32[]{:S(2)}, u32[]{:S(2)}) async-start(bf16[32,2,8,1024]{3,2,1,0:T(8,128)(2,1)} %bitcast.17), calls=%async_computation.2 | async-start | bytes 2097152 | tf_op jit(solution)/shard_map/all_to_all | solution.py:67
  32.8 5.1 %fusion.36 = bf16[32,1,8,3584]{3,2,1,0:T(8,128)(2,1)S(1)} fusion(bf16[2,1024,3584]{2,1,0:T(8,128)(2,1)} %param.9, f32[3584]{0:T(1024)S(1)} %get-tuple-element.3, bf16[32,2,8,1024]{3,2,1,0:T(8,128)(2,1)S(1)} %all-to-all-done), kind=kOutput, calls=%fused_computation.22 | convolution fusion | flops 1880883200 | bytes 9715712 | tf_op jit(solution)/shard_map/dot_general | solution.py:58
  37.9 5.2 %fusion.42 = bf16[32,1,8,3584]{3,2,1,0:T(8,128)(2,1)S(1)} fusion(bf16[2,1024,3584]{2,1,0:T(8,128)(2,1)} %param.9, f32[3584]{0:T(1024)S(1)} %get-tuple-element.4, bf16[32,2,8,1024]{3,2,1,0:T(8,128)(2,1)S(1)} %all-to-all-done), kind=kOutput, calls=%fused_computation.24 | convolution fusion | flops 1880883200 | bytes 9715712 | tf_op jit(solution)/shard_map/dot_general | solution.py:58
  43.1 2.1 pad_maximum_fusion
  45.2 4.4 %all-to-all-done.2 = bf16[32,2,8,1024]{3,2,1,0:T(8,128)(2,1)S(1)} async-done(((bf16[32,2,8,1024]{3,2,1,0:T(8,128)(2,1)}), bf16[32,2,8,1024]{3,2,1,0:T(8,128)(2,1)S(1)}, u32[]{:S(2)}, u32[]{:S(2)}) %all-to-all-start.2) | async-done | bytes 1048608 | tf_op jit(solution)/shard_map/all_to_all | solution.py:67
  49.6 4.8 %all-to-all-start.1 = ((bf16[32,2,8,3584]{3,2,1,0:T(8,128)(2,1)}), bf16[32,2,8,3584]{3,2,1,0:T(8,128)(2,1)}, u32[]{:S(2)}, u32[]{:S(2)}) async-start(bf16[32,2,8,3584]{3,2,1,0:T(8,128)(2,1)} %pad_maximum_fusion), calls=%async_computation.1 | async-start | bytes 7340032 | tf_op jit(solution)/shard_map/all_to_all | solution.py:64
  54.4 7.4 %constant_dynamic-slice_fusion.1 = bf16[1,1024,3584]{2,1,0:T(8,128)(2,1)} fusion(bf16[2,1024,3584]{2,1,0:T(8,128)(2,1)} %param.9, s32[]{:T(128)S(6)} %select_n.56), kind=kLoop, calls=%fused_computation.77 | loop fusion | bytes 14680068 | tf_op jit(solution)/shard_map/jit(dynamic_index_in_dim)/dynamic_slice | solution.py:24
  61.9 3.2 %collective-permute-start = (bf16[1,1024,3584]{2,1,0:T(8,128)(2,1)}, bf16[1,1024,3584]{2,1,0:T(8,128)(2,1)}, u32[]{:S(2)}, u32[]{:S(2)}) collective-permute-start(bf16[1,1024,3584]{2,1,0:T(8,128)(2,1)} %constant_dynamic-slice_fusion.1), channel_id=1, source_target_pairs={{16,0},{17,1},{18,2},{19,3},{20,4},{21,5},{22,6},{23,7},{24,8},{25... | collective-permute-start | bytes 22020104 | tf_op jit(solution)/shard_map/ppermute | solution.py:10
  65.1 5.1 %fusion.39 = bf16[32,1,8,3584]{3,2,1,0:T(8,128)(2,1)S(1)} fusion(bf16[2,1024,3584]{2,1,0:T(8,128)(2,1)} %param.9, f32[3584]{0:T(1024)S(1)} %get-tuple-element.3, bf16[32,2,8,1024]{3,2,1,0:T(8,128)(2,1)S(1)} %all-to-all-done.2), kind=kOutput, calls=%fused_computation.23 | convolution fusion | flops 1880883200 | bytes 9715712 | tf_op jit(solution)/shard_map/dot_general | solution.py:58
  70.3 2.1 fusion.45
  72.4 2.2 pad_maximum_fusion.1
  74.6 26.8 %all-to-all-done.1 = bf16[32,2,8,3584]{3,2,1,0:T(8,128)(2,1)} async-done(((bf16[32,2,8,3584]{3,2,1,0:T(8,128)(2,1)}), bf16[32,2,8,3584]{3,2,1,0:T(8,128)(2,1)}, u32[]{:S(2)}, u32[]{:S(2)}) %all-to-all-start.1) | async-done | bytes 3670048 | tf_op jit(solution)/shard_map/all_to_all | solution.py:64
  101.4 159.2 %all-to-all-start.3 = ((bf16[32,2,8,3584]{3,2,1,0:T(8,128)(2,1)}), bf16[32,2,8,3584]{3,2,1,0:T(8,128)(2,1)}, u32[]{:S(2)}, u32[]{:S(2)}) async-start(bf16[32,2,8,3584]{3,2,1,0:T(8,128)(2,1)} %pad_maximum_fusion.1), calls=%async_computation.3 | async-start | bytes 7340032 | tf_op jit(solution)/shard_map/all_to_all | solution.py:64
  260.6 3.3 %collective-permute-start.1 = (bf16[1,3584]{1,0:T(2,128)(2,1)S(1)}, bf16[1,3584]{1,0:T(2,128)(2,1)S(1)}, u32[]{:S(2)}, u32[]{:S(2)}) collective-permute-start(bf16[1,3584]{1,0:T(2,128)(2,1)S(1)} %constant_dynamic-slice_fusion), channel_id=1, source_target_pairs={{16,0},{17,1},{18,2},{19,3},{20,4},{21,5},{22,6},{23,7},{24,8},{25... | collective-permute-start | bytes 21512 | tf_op jit(solution)/shard_map/ppermute | solution.py:10
  264.1 43.2 %collective-permute-done.1 = bf16[1,3584]{1,0:T(2,128)(2,1)S(1)} collective-permute-done((bf16[1,3584]{1,0:T(2,128)(2,1)S(1)}, bf16[1,3584]{1,0:T(2,128)(2,1)S(1)}, u32[]{:S(2)}, u32[]{:S(2)}) %collective-permute-start.1) | collective-permute-done | bytes 7200 | tf_op jit(solution)/shard_map/ppermute | solution.py:10
  307.3 3.0 fusion.48
  310.4 3.0 fusion.49
  314.1 6.6 %copy.39 = bf16[1,1024,3584]{2,1,0:T(8,128)(2,1)} copy(bf16[1,1024,3584]{2,1,0:T(8,128)(2,1)} %collective-permute-done) | data formatting | bytes 14680064
  (31 shorter events, 3.0 us)
Async XLA Ops:
  0.6 14.0 %copy-start = (bf16[2,16,8,1024]{3,2,1,0:T(8,128)(2,1)S(1)}, bf16[2,16,8,1024]{3,2,1,0:T(8,128)(2,1)}, u32[]{:S(2)}) copy-start(bf16[2,16,8,1024]{3,2,1,0:T(8,128)(2,1)} %param.6) | copy-start | bytes 1572868
  4.5 24.2 %all-to-all-start = ((bf16[32,2,8,1024]{3,2,1,0:T(8,128)(2,1)}), bf16[32,2,8,1024]{3,2,1,0:T(8,128)(2,1)S(1)}, u32[]{:S(2)}, u32[]{:S(2)}) async-start(bf16[32,2,8,1024]{3,2,1,0:T(8,128)(2,1)} %bitcast.2), calls=%async_computation | async-start | bytes 2097152 | tf_op jit(solution)/shard_map/all_to_all | solution.py:67
  28.7 20.9 %all-to-all-start.2 = ((bf16[32,2,8,1024]{3,2,1,0:T(8,128)(2,1)}), bf16[32,2,8,1024]{3,2,1,0:T(8,128)(2,1)S(1)}, u32[]{:S(2)}, u32[]{:S(2)}) async-start(bf16[32,2,8,1024]{3,2,1,0:T(8,128)(2,1)} %bitcast.17), calls=%async_computation.2 | async-start | bytes 2097152 | tf_op jit(solution)/shard_map/all_to_all | solution.py:67
  49.6 51.8 %all-to-all-start.1 = ((bf16[32,2,8,3584]{3,2,1,0:T(8,128)(2,1)}), bf16[32,2,8,3584]{3,2,1,0:T(8,128)(2,1)}, u32[]{:S(2)}, u32[]{:S(2)}) async-start(bf16[32,2,8,3584]{3,2,1,0:T(8,128)(2,1)} %pad_maximum_fusion), calls=%async_computation.1 | async-start | bytes 7340032 | tf_op jit(solution)/shard_map/all_to_all | solution.py:64
  54.4 15.8 %slice-start = ((s8[14680064]{0:T(1024)(128)(4,1)}), s8[2097152]{0:T(1024)(128)(4,1)S(1)}, s32[]{:S(2)}) async-start(s8[14680064]{0:T(1024)(128)(4,1)} %bitcast.95), calls=%async_computation.4 | async-start | bytes 4194304
  54.4 15.8 %slice-start.1 = ((s8[14680064]{0:T(1024)(128)(4,1)}), s8[4194304]{0:T(1024)(128)(4,1)S(1)}, s32[]{:S(2)}) async-start(s8[14680064]{0:T(1024)(128)(4,1)} %bitcast.95), calls=%async_computation.5 | async-start | bytes 8388608
  54.4 15.8 %slice-start.2 = ((s8[14680064]{0:T(1024)(128)(4,1)}), s8[4194304]{0:T(1024)(128)(4,1)S(1)}, s32[]{:S(2)}) async-start(s8[14680064]{0:T(1024)(128)(4,1)} %bitcast.95), calls=%async_computation.6 | async-start | bytes 8388608
  61.9 8.4 %slice-start.3 = ((s8[14680064]{0:T(1024)(128)(4,1)}), s8[4194304]{0:T(1024)(128)(4,1)S(1)}, s32[]{:S(2)}) async-start(s8[14680064]{0:T(1024)(128)(4,1)} %bitcast.95), calls=%async_computation.7 | async-start | bytes 8388608
  61.9 252.2 %collective-permute-start = (bf16[1,1024,3584]{2,1,0:T(8,128)(2,1)}, bf16[1,1024,3584]{2,1,0:T(8,128)(2,1)}, u32[]{:S(2)}, u32[]{:S(2)}) collective-permute-start(bf16[1,1024,3584]{2,1,0:T(8,128)(2,1)} %constant_dynamic-slice_fusion.1), channel_id=1, source_target_pairs={{16,0},{17,1},{18,2},{19,3},{20,4},{21,5},{22,6},{23,7},{24,8},{25... | collective-permute-start | bytes 22020104 | tf_op jit(solution)/shard_map/ppermute | solution.py:10
  74.6 186.0 %copy-start.1 = (bf16[2,3584]{1,0:T(2,128)(2,1)S(1)}, bf16[2,3584]{1,0:T(2,128)(2,1)}, u32[]{:S(2)}) copy-start(bf16[2,3584]{1,0:T(2,128)(2,1)} %param.10) | copy-start | bytes 43012
  74.6 189.3 %copy-start.2 = (f32[2,16,8]{1,2,0:T(8,128)S(1)}, f32[2,16,8]{1,2,0:T(8,128)}, u32[]{:S(2)}) copy-start(f32[2,16,8]{1,2,0:T(8,128)} %param.8) | copy-start | bytes 3076
  101.4 209.0 %all-to-all-start.3 = ((bf16[32,2,8,3584]{3,2,1,0:T(8,128)(2,1)}), bf16[32,2,8,3584]{3,2,1,0:T(8,128)(2,1)}, u32[]{:S(2)}, u32[]{:S(2)}) async-start(bf16[32,2,8,3584]{3,2,1,0:T(8,128)(2,1)} %pad_maximum_fusion.1), calls=%async_computation.3 | async-start | bytes 7340032 | tf_op jit(solution)/shard_map/all_to_all | solution.py:64
  260.6 46.7 %collective-permute-start.1 = (bf16[1,3584]{1,0:T(2,128)(2,1)S(1)}, bf16[1,3584]{1,0:T(2,128)(2,1)S(1)}, u32[]{:S(2)}, u32[]{:S(2)}) collective-permute-start(bf16[1,3584]{1,0:T(2,128)(2,1)S(1)} %constant_dynamic-slice_fusion), channel_id=1, source_target_pairs={{16,0},{17,1},{18,2},{19,3},{20,4},{21,5},{22,6},{23,7},{24,8},{25... | collective-permute-start | bytes 21512 | tf_op jit(solution)/shard_map/ppermute | solution.py:10
where the time goes:
time: 323 us; the launch traced here: 321 us
  starting transfers between devices  182 us (56%)
  waiting for transfers between devices  87 us (27%)
  matrix products  27.3 us (8%)
  local copies, waits for them, and re-layouts  17.2 us (5%)
  other arithmetic  6.28 us (2%)
    all_to_all x2, starting transfers between devices, run_experts(): lax.all_to_all(stacked, 'ep', split_axis=0, concat_axis=0, tiled=True)  164 us
    ppermute x2, waiting for transfers between devices, passed_along(): return lax.ppermute(block, axis, route)  43.2 us
    all_to_all x2, waiting for transfers between devices, run_experts(): lax.all_to_all(stacked, 'ep', split_axis=0, concat_axis=0, tiled=True)  26.8 us
    dot_general x4, matrix products, run_experts(): jnp.dot(flat_rows, lane_weights[lane_id], preferred_element_type=jnp.floa...  17.5 us
    all_to_all x2, waiting for transfers between devices, local(): lax.all_to_all(outgoing, 'ep', split_axis=0, concat_axis=0, tiled=True)  17 us
    all_to_all x2, starting transfers between devices, local(): lax.all_to_all(outgoing, 'ep', split_axis=0, concat_axis=0, tiled=True)  11.5 us
    dynamic_slice x1, local copies, waits for them, and re-layouts, local(): lax.dynamic_index_in_dim(expert_weight, local_pick, 0, keepdims=True)  7.44 us
    unnamed x16, local copies, waits for them, and re-layouts  7.24 us
  transfers between devices with their start and end apart: 6, of which 4 were waited for; matrix products, arithmetic and copies ran while one was open for 12% of the time, Pallas kernels for 0%

commit v1 on v0

v1 whole, which is shorter than its diff:
```python
import jax
import jax.numpy as jnp
from jax import lax
from jax.sharding import Mesh, PartitionSpec as P

EP = ("x", "y", "c")
WEIGHT_ROWS = (64, 64, 64, 64)
HALVES = 2


def shifted(block, axis, distance):
    count = lax.axis_size(axis)
    return lax.ppermute(block, axis, [(i, (i + distance) % count) for i in range(count)])


def replica_update(expert_weight, column_scale, replica_map):
    part, parts = lax.axis_index("dp"), lax.axis_size("dp")
    me = lax.axis_index(EP)
    depth, width = expert_weight.shape[1:]
    quarter = depth // parts
    half_axis = lax.axis_size("x") // 2
    crossed, at = [], 0
    for rows in WEIGHT_ROWS:
        block = lax.dynamic_slice(expert_weight, (0, part * quarter + at, 0), (2, rows, width))
        crossed.append(shifted(block, "x", half_axis))
        at += rows
    partner = replica_map[(me + lax.axis_size(EP) // 2) % lax.axis_size(EP)]
    scale = lax.dynamic_index_in_dim(column_scale, partner - 2 * me, 0, keepdims=True)
    replica_scale = shifted(scale, "x", half_axis)
    picks = lax.all_gather(replica_map, "dp").reshape(parts, -1)[:, me] % 2
    pieces = []
    for block in crossed:
        chosen = jnp.where(picks[:, None, None] == 0, block[0][None], block[1][None])
        pieces.append(lax.all_to_all(chosen, "dp", 0, 0, tiled=True))
    return jnp.concatenate(pieces, 1).reshape(1, depth, width), replica_scale


def rank_of(expert_list):
    count = expert_list.shape[-1]
    order = jnp.arange(count, dtype=jnp.int32)
    same = expert_list[..., :, None] == expert_list[..., None, :]
    return jnp.sum(same & (order[:, None] > order[None, :]), axis=-1, dtype=jnp.int32)


def local(hidden_in, expert_ids, gates, expert_weight, column_scale, replica_map):
    steps, rows, top, depth = hidden_in.shape
    width = expert_weight.shape[2]
    items = rows * top
    n_x, n_yc, n_ep = lax.axis_size("x"), lax.axis_size("y") * lax.axis_size("c"), lax.axis_size(EP)
    my_x, my_yc, me = lax.axis_index("x"), lax.axis_index(("y", "c")), lax.axis_index(EP)

    replica_weight, replica_scale = replica_update(expert_weight, column_scale, replica_map)

    expert_list = expert_ids.reshape(steps, items)
    rank = rank_of(expert_list)
    step_of = jnp.arange(steps, dtype=jnp.int32)[:, None]
    place = jnp.where(
        rank < 2,
        (expert_list // 2) * 8 + (expert_list % 2) * 4 + step_of * 2 + rank,
        n_ep * 8 + step_of * 8 + rank - 2,
    ).reshape(steps * items)
    selector = (
        jnp.arange(n_ep * 8 + 16, dtype=jnp.int32)[:, None] == place[None, :]
    ).astype(jnp.bfloat16)
    outgoing = jnp.dot(
        selector, hidden_in.reshape(steps * items, depth), preferred_element_type=jnp.float32
    ).astype(jnp.bfloat16)
    hot_id = jnp.sum(jnp.where(rank == 7, expert_list, 0), axis=1)
    flat_gates = gates.reshape(steps * items)
    high = lax.reduce_precision(flat_gates, 8, 7)
    middle = lax.reduce_precision(flat_gates - high, 8, 7)
    low = flat_gates - high - middle
    told = jnp.concatenate(
        [expert_list.reshape(steps * items).astype(jnp.float32), high, middle, low]
    ).astype(jnp.bfloat16)
    line = jnp.arange(16, dtype=jnp.int32)[:, None]
    hot_line = jnp.where(line < 8, hot_id[0], hot_id[1]).astype(jnp.bfloat16)
    hot_block = jnp.where(line == 6, told[None, :], outgoing[n_ep * 8 :])
    hot_block = jnp.where(line % 8 == 7, hot_line, hot_block)
    received = lax.all_to_all(
        outgoing[: n_ep * 8].reshape(n_ep, 8, depth), EP, 0, 0, tiled=True
    )
    hot_all = lax.all_gather(hot_block, EP)

    normal = received.reshape(n_x, n_yc, 8, depth).transpose(1, 0, 2, 3).reshape(n_yc, n_x * 8, depth)
    normal_lane = jnp.broadcast_to((jnp.arange(n_x * 8, dtype=jnp.int32) % 8) // 4, (n_yc, n_x * 8))
    by_step = hot_all.reshape(n_x, n_yc, steps, 8, depth).transpose(1, 0, 2, 3, 4)
    hot = by_step[:, :, :, :6].reshape(n_yc, n_x * 12, depth)
    hot_lane = by_step[:, :, :, 7, 0].astype(jnp.int32) - 2 * me
    hot_lane = jnp.broadcast_to(hot_lane[..., None], (n_yc, n_x, steps, 6)).reshape(n_yc, n_x * 12)
    stack = n_x * 20
    served = jnp.concatenate([normal, hot], 1).reshape(n_yc * stack, depth)
    lane = jnp.concatenate([normal_lane, hot_lane], 1).reshape(n_yc * stack, 1)
    zero = jnp.zeros((), jnp.bfloat16)
    spread = jnp.concatenate(
        [jnp.where(lane == 0, served, zero), jnp.where(lane == 1, served, zero)], 1
    )

    told_all = hot_all.reshape(n_x, n_yc, 16, depth)[:, :, 6]
    told_here = lax.dynamic_index_in_dim(told_all, my_yc, 1, keepdims=False)
    told_here = told_here.astype(jnp.float32).reshape(n_x, 4, steps, items)
    ids_here = told_here[:, 0].astype(jnp.int32)
    gates_here = told_here[:, 1] + told_here[:, 2] + told_here[:, 3]
    rank_here = rank_of(ids_here)
    who = jnp.arange(n_x * steps, dtype=jnp.int32).reshape(n_x, steps, 1) * 256
    code = jnp.where(rank_here < 2, ids_here * 2 + rank_here, 128 + rank_here - 2) + who
    source = jnp.arange(n_yc, dtype=jnp.int32)[:, None]
    row = jnp.arange(n_x * 8, dtype=jnp.int32)[None, :]
    normal_code = ((n_yc * my_x + source) * 2 + (row % 8) // 4) * 2 + row % 2
    normal_code = normal_code + ((row // 8) * steps + (row % 4) // 2) * 256
    row = jnp.arange(n_x * 12, dtype=jnp.int32)[None, :]
    hot_code = 128 + row % 6 + ((row // 12) * steps + (row % 12) // 6) * 256
    hot_code = jnp.broadcast_to(hot_code, (n_yc, n_x * 12))
    column_code = jnp.concatenate([normal_code, hot_code], 1).reshape(n_yc * stack)
    code = code.reshape(n_x * steps * rows, top)
    gates_here = gates_here.reshape(n_x * steps * rows, top)
    mix = jnp.sum(
        jnp.where(code[:, :, None] == column_code[None, None, :], gates_here[:, :, None], 0.0), axis=1
    )
    mix_high = lax.reduce_precision(mix, 8, 7)
    mixes = jnp.concatenate([mix_high, mix - mix_high], 0).astype(jnp.bfloat16)

    flat_weight = expert_weight.reshape(2 * depth, width)
    scales = column_scale.astype(jnp.float32)
    piece = width // HALVES
    results = []
    for half in range(HALVES):
        columns = slice(half * piece, (half + 1) * piece)
        product = jnp.dot(spread, flat_weight[:, columns], preferred_element_type=jnp.float32)
        product = product * jnp.where(lane == 0, scales[0:1, columns], scales[1:2, columns])
        product = product.astype(jnp.bfloat16).reshape(n_yc, stack, piece)
        returned = lax.all_to_all(product, ("y", "c"), 0, 0, tiled=True)
        partial = jnp.dot(
            mixes, returned.reshape(n_yc * stack, piece), preferred_element_type=jnp.float32
        )
        many = n_x * steps * rows
        partial = (partial[:many] + partial[many:]).astype(jnp.bfloat16)
        partial = lax.all_to_all(partial.reshape(n_x, steps * rows, piece), "x", 0, 0, tiled=True)
        total = jnp.sum(partial.astype(jnp.float32), axis=0).astype(jnp.bfloat16)
        results.append(total.reshape(steps, rows, piece))
    return jnp.concatenate(results, 2), replica_weight, replica_scale


def solution(mesh):
    n_dp = mesh.shape["dp"]
    grid = Mesh(mesh.devices.reshape(n_dp, 4, 4, 2), ("dp", "x", "y", "c"))
    everywhere = ("dp",) + EP
    in_specs = (
        P(None, everywhere, None, None),
        P(None, everywhere, None),
        P(None, everywhere, None),
        P(EP, None, None),
        P(EP, None),
        P("dp"),
    )
    out_specs = (P(None, everywhere, None), P(everywhere, None, None), P(everywhere, None))
    return jax.shard_map(local, mesh=grid, in_specs=in_specs, out_specs=out_specs, check_vma=False)
```

time: 323 us -> 365 us (1.13)
  starting transfers between devices: 182 us -> 50.9 us
  waiting for transfers between devices: 87 us -> 181 us
  local copies, waits for them, and re-layouts: 17.2 us -> 61.5 us
  between operations: 1.52 us -> 15.8 us
  other arithmetic: 6.28 us -> 19.6 us
  blocking collectives: 0 us -> 9.72 us
    all_to_all x4 -> x9, starting transfers between devices: 176 us -> 41.2 us  [the longest x4 18.6 us: replica_update(): pieces.append(lax.all_to_all(chosen, 'dp', 0, 0, tiled=True))]
    all_to_all x4 -> x9, waiting for transfers between devices: 43.8 us -> 99.5 us  [the longest x4 51.1 us: replica_update(): pieces.append(lax.all_to_all(chosen, 'dp', 0, 0, tiled=True))]
    slice x3 -> x5, local copies, waits for them, and re-layouts: 0.91 us -> 28.7 us  [the longest x2 26.9 us: local(): hot = by_step[:, :, :, :6].reshape(n_yc, n_x * 12, depth)]
    ppermute x2 -> x5, waiting for transfers between devices: 43.2 us -> 62.5 us  [shifted(): lax.ppermute(block, axis, [(i, (i + distance) % count) for i in range(cou...]
    all_gather x0 -> x1, waiting for transfers between devices: none -> 18.5 us  [local(): hot_all = lax.all_gather(hot_block, EP)]
    reshape x0 -> x5, local copies, waits for them, and re-layouts: none -> 17.1 us  [the longest x1 15.8 us: local(): hot_all.reshape(n_x, n_yc, steps, 8, depth).transpose(1, 0, 2, 3, 4)]
    unnamed x0 -> x1, blocking collectives: none -> 9.72 us
    concatenate x0 -> x5, other arithmetic: none -> 6.78 us  [the longest x1 5.94 us: replica_update(): return (jnp.concatenate(pieces, 1).reshape(1, depth, width), replica_scale)]
  transfers between devices with their start and end apart: 6 -> 15, of which waited for: 4 -> 12; matrix products, arithmetic and copies ran while one was open for 12% -> 27% of each run, Pallas kernels for 0% -> 0%
where the time goes in v1:
time: 365 us; the launch traced here: 362 us
  waiting for transfers between devices  181 us (50%)
  local copies, waits for them, and re-layouts  61.5 us (17%)
  starting transfers between devices  50.9 us (14%)
  matrix products  24.3 us (7%)
  other arithmetic  19.6 us (5%)
  between operations  15.8 us (4%)
  blocking collectives  9.72 us (3%)
    ppermute x5, waiting for transfers between devices, shifted(): lax.ppermute(block, axis, [(i, (i + distance) % count) for i in range(cou...  62.5 us
    all_to_all x4, waiting for transfers between devices, replica_update(): pieces.append(lax.all_to_all(chosen, 'dp', 0, 0, tiled=True))  51.1 us
    all_to_all x2, waiting for transfers between devices, local(): returned = lax.all_to_all(product, ('y', 'c'), 0, 0, tiled=True)  41.2 us
    slice x2, local copies, waits for them, and re-layouts, local(): hot = by_step[:, :, :, :6].reshape(n_yc, n_x * 12, depth)  26.9 us
    dot_general x2, matrix products, local(): jnp.dot(spread, flat_weight[:, columns], preferred_element_type=jnp.float32)  19.4 us
    all_to_all x4, starting transfers between devices, replica_update(): pieces.append(lax.all_to_all(chosen, 'dp', 0, 0, tiled=True))  18.6 us
    all_gather x1, waiting for transfers between devices, local(): hot_all = lax.all_gather(hot_block, EP)  18.5 us
    reshape x1, local copies, waits for them, and re-layouts, local(): hot_all.reshape(n_x, n_yc, steps, 8, depth).transpose(1, 0, 2, 3, 4)  15.8 us
  transfers between devices with their start and end apart: 15, of which 12 were waited for; matrix products, arithmetic and copies ran while one was open for 27% of the time, Pallas kernels for 0%

profile of v1, /device:TPU:0, one launch (start us, length us, event | category | flops | bytes accessed | tf_op | source)
XLA Modules:
  0.0 362.4 jit_solution(1058791144733687998)
XLA Ops:
  9.7 7.4 %all-to-all-start = ((bf16[32,8,1024]{2,1,0:T(8,128)(2,1)}), bf16[32,8,1024]{2,1,0:T(8,128)(2,1)S(1)}, u32[]{:S(2)}, u32[]{:S(2)}) async-start(bf16[32,8,1024]{2,1,0:T(8,128)(2,1)} %slice_bitcast_fusion), calls=%async_computation | async-start | bytes 1048576 | tf_op jit(solution)/shard_map/all_to_all | solution.py:80
  30.1 9.7 %all-reduce.1 = s32[4,32]{1,0:T(4,128)S(1)} all-reduce(s32[4,32]{1,0:T(4,128)S(1)} %reshape.640), channel_id=3, replica_groups=mesh['dp'=4,'x'=4,'y'=4,'c'=2] {'dp'}, use_global_device_ids=true, to_apply=%add | all-reduce | flops 128 | bytes 1024
  40.7 6.6 %collective-permute-done = bf16[2,64,3584]{2,1,0:T(8,128)(2,1)} collective-permute-done((bf16[2,64,3584]{2,1,0:T(8,128)(2,1)}, bf16[2,64,3584]{2,1,0:T(8,128)(2,1)}, u32[]{:S(2)}, u32[]{:S(2)}) %collective-permute-start) | collective-permute-done | bytes 917536 | tf_op jit(solution)/shard_map/ppermute | solution.py:13
  48.6 18.4 %collective-permute-done.1 = bf16[2,64,3584]{2,1,0:T(8,128)(2,1)} collective-permute-done((bf16[2,64,3584]{2,1,0:T(8,128)(2,1)}, bf16[2,64,3584]{2,1,0:T(8,128)(2,1)}, u32[]{:S(2)}, u32[]{:S(2)}) %collective-permute-start.1) | collective-permute-done | bytes 917536 | tf_op jit(solution)/shard_map/ppermute | solution.py:13
  68.2 18.3 %collective-permute-done.2 = bf16[2,64,3584]{2,1,0:T(8,128)(2,1)S(1)} collective-permute-done((bf16[2,64,3584]{2,1,0:T(8,128)(2,1)}, bf16[2,64,3584]{2,1,0:T(8,128)(2,1)S(1)}, u32[]{:S(2)}, u32[]{:S(2)}) %collective-permute-start.2) | collective-permute-done | bytes 917536 | tf_op jit(solution)/shard_map/ppermute | solution.py:13
  86.6 19.1 %collective-permute-done.3 = bf16[2,64,3584]{2,1,0:T(8,128)(2,1)S(1)} collective-permute-done((bf16[2,64,3584]{2,1,0:T(8,128)(2,1)}, bf16[2,64,3584]{2,1,0:T(8,128)(2,1)S(1)}, u32[]{:S(2)}, u32[]{:S(2)}) %collective-permute-start.3) | collective-permute-done | bytes 917536 | tf_op jit(solution)/shard_map/ppermute | solution.py:13
  109.1 5.3 %all-to-all-start.8 = ((bf16[4,64,3584]{2,1,0:T(8,128)(2,1)}), bf16[4,64,3584]{2,1,0:T(8,128)(2,1)S(1)}, u32[]{:S(2)}, u32[]{:S(2)}) async-start(bf16[4,64,3584]{2,1,0:T(8,128)(2,1)} %get-tuple-element.35), calls=%async_computation.8 | async-start | bytes 3670016 | tf_op jit(solution)/shard_map/all_to_all | solution.py:34
  116.5 21.3 %all-to-all-done.8 = bf16[4,64,3584]{2,1,0:T(8,128)(2,1)S(1)} async-done(((bf16[4,64,3584]{2,1,0:T(8,128)(2,1)}), bf16[4,64,3584]{2,1,0:T(8,128)(2,1)S(1)}, u32[]{:S(2)}, u32[]{:S(2)}) %all-to-all-start.8) | async-done | bytes 1835040 | tf_op jit(solution)/shard_map/all_to_all | solution.py:34
  137.8 4.4 %all-to-all-start.7 = ((bf16[4,64,3584]{2,1,0:T(8,128)(2,1)}), bf16[4,64,3584]{2,1,0:T(8,128)(2,1)}, u32[]{:S(2)}, u32[]{:S(2)}) async-start(bf16[4,64,3584]{2,1,0:T(8,128)(2,1)} %get-tuple-element.34), calls=%async_computation.7 | async-start | bytes 3670016 | tf_op jit(solution)/shard_map/all_to_all | solution.py:34
  142.7 18.5 %all-gather.4.cloned.1.call-done = bf16[512,1024]{1,0:T(8,128)(2,1)} async-done(((bf16[16,1024]{1,0:T(8,128)(2,1)}), bf16[512,1024]{1,0:T(8,128)(2,1)}) %all-gather.4.cloned.1.call-update) | async-done | bytes 1048592 | tf_op jit(solution)/shard_map/all_gather | solution.py:83
  161.2 15.8 %copy.56 = bf16[4,8,2,8,1024]{1,0,4,3,2:T(4,128)(2,1)} copy(bf16[4,8,2,8,1024]{4,3,2,1,0:T(8,128)(2,1)} %bitcast.80) | data formatting | bytes 2097152 | tf_op jit(solution)/shard_map/reshape | solution.py:87
  176.9 10.9 %slice.124 = bf16[8,4,2,6,1024]{0,1,4,3,2:T(4,128)(2,1)} slice(bf16[8,4,2,8,1024]{0,1,4,3,2:T(4,128)(2,1)} %bitcast.71), slice={[0:8], [0:4], [0:2], [0:6], [0:1024]} | slice | bytes 1572864 | tf_op jit(solution)/shard_map/slice | solution.py:88
  189.0 16.0 %copy.59 = bf16[8,4,2,6,1024]{4,0,3,2,1:T(8,128)(2,1)S(1)} copy(bf16[8,4,2,6,1024]{0,1,4,3,2:T(4,128)(2,1)} %slice.124) | data formatting | bytes 1572864 | tf_op jit(solution)/shard_map/slice | solution.py:88
  207.0 4.4 %all-to-all-start.6 = ((bf16[4,64,3584]{2,1,0:T(8,128)(2,1)}), bf16[4,64,3584]{2,1,0:T(8,128)(2,1)S(1)}, u32[]{:S(2)}, u32[]{:S(2)}) async-start(bf16[4,64,3584]{2,1,0:T(8,128)(2,1)} %get-tuple-element.33), calls=%async_computation.6 | async-start | bytes 3670016 | tf_op jit(solution)/shard_map/all_to_all | solution.py:34
  214.5 9.2 %multiply_convert_fusion = bf16[640,1792]{1,0:T(8,128)(2,1)} fusion(bf16[2048,3584]{1,0:T(8,128)(2,1)} %bitcast.82, f32[1792]{0:T(1024)S(1)} %get-tuple-element.4, f32[1792]{0:T(1024)S(1)} %get-tuple-element.5, pred[640]{0:T(1024)(128)(4,1)S(1)} %eq.157, bf16[640,1024]{1,0:T(8,128)(2,1)S(1)} %get-tuple-element.12, bf16[640,1024]{1,0:T(8,128)(2,1)S(1)} %get-tuple-element.11), kind=kOutput, calls=%fused_computation.5 | convolution fusion | flops 4706304000 | bytes 12270208 | tf_op jit(solution)/shard_map/dot_general | solution.py:129
  223.7 11.8 %all-to-all-done.6 = bf16[4,64,3584]{2,1,0:T(8,128)(2,1)S(1)} async-done(((bf16[4,64,3584]{2,1,0:T(8,128)(2,1)}), bf16[4,64,3584]{2,1,0:T(8,128)(2,1)S(1)}, u32[]{:S(2)}, u32[]{:S(2)}) %all-to-all-start.6) | async-done | bytes 1835040 | tf_op jit(solution)/shard_map/all_to_all | solution.py:34
  244.5 10.2 %multiply_convert_fusion.1 = bf16[640,1792]{1,0:T(8,128)(2,1)} fusion(bf16[2048,3584]{1,0:T(8,128)(2,1)} %bitcast.83, f32[1792]{0:T(1024)S(1)} %get-tuple-element.6, f32[1792]{0:T(1024)S(1)} %get-tuple-element.3, pred[640]{0:T(1024)(128)(4,1)S(1)} %eq.157, bf16[640,1024]{1,0:T(8,128)(2,1)} %copy-done.6, bf16[640,1024]{1,0:T(8,128)(2,1)} %copy-done.5), kind=kOutput, calls=%fused_computation.6 | convolution fusion | flops 4706304000 | bytes 12270208 | tf_op jit(solution)/shard_map/dot_general | solution.py:129
  254.7 15.1 %all-to-all-done.3 = bf16[8,80,1792]{2,1,0:T(8,128)(2,1)S(1)} async-done(((bf16[8,80,1792]{2,1,0:T(8,128)(2,1)}), bf16[8,80,1792]{2,1,0:T(8,128)(2,1)S(1)}, u32[]{:S(2)}, u32[]{:S(2)}) %all-to-all-start.3) | async-done | bytes 2293792 | tf_op jit(solution)/shard_map/all_to_all | solution.py:132
  269.9 4.4 %all-to-all-start.1 = ((bf16[8,80,1792]{2,1,0:T(8,128)(2,1)}), bf16[8,80,1792]{2,1,0:T(8,128)(2,1)}, u32[]{:S(2)}, u32[]{:S(2)}) async-start(bf16[8,80,1792]{2,1,0:T(8,128)(2,1)} %bitcast.76), calls=%async_computation.1 | async-start | bytes 4587520 | tf_op jit(solution)/shard_map/all_to_all | solution.py:132
  277.5 26.0 %all-to-all-done.1 = bf16[8,80,1792]{2,1,0:T(8,128)(2,1)} async-done(((bf16[8,80,1792]{2,1,0:T(8,128)(2,1)}), bf16[8,80,1792]{2,1,0:T(8,128)(2,1)}, u32[]{:S(2)}, u32[]{:S(2)}) %all-to-all-start.1) | async-done | bytes 2293792 | tf_op jit(solution)/shard_map/all_to_all | solution.py:132
  303.5 4.4 %all-to-all-start.5 = ((bf16[4,64,3584]{2,1,0:T(8,128)(2,1)}), bf16[4,64,3584]{2,1,0:T(8,128)(2,1)}, u32[]{:S(2)}, u32[]{:S(2)}) async-start(bf16[4,64,3584]{2,1,0:T(8,128)(2,1)} %get-tuple-element.32), calls=%async_computation.5 | async-start | bytes 3670016 | tf_op jit(solution)/shard_map/all_to_all | solution.py:34
  313.5 18.1 %all-to-all-done.5 = bf16[4,64,3584]{2,1,0:T(8,128)(2,1)} async-done(((bf16[4,64,3584]{2,1,0:T(8,128)(2,1)}), bf16[4,64,3584]{2,1,0:T(8,128)(2,1)}, u32[]{:S(2)}, u32[]{:S(2)}) %all-to-all-start.5) | async-done | bytes 1835040 | tf_op jit(solution)/shard_map/all_to_all | solution.py:34
  337.5 5.5 %all-to-all-done.4 = bf16[4,32,1792]{2,1,0:T(8,128)(2,1)S(1)} async-done(((bf16[4,32,1792]{2,1,0:T(8,128)(2,1)}), bf16[4,32,1792]{2,1,0:T(8,128)(2,1)S(1)}, u32[]{:S(2)}, u32[]{:S(2)}) %all-to-all-start.4) | async-done | bytes 458784 | tf_op jit(solution)/shard_map/all_to_all | solution.py:138
  346.5 5.9 %pad_maximum_fusion = bf16[4,256,3584]{2,1,0:T(8,128)(2,1)} fusion(bf16[4,64,3584]{2,1,0:T(8,128)(2,1)S(1)} %copy-done.3, bf16[4,64,3584]{2,1,0:T(8,128)(2,1)} %all-to-all-done.7, bf16[4,64,3584]{2,1,0:T(8,128)(2,1)} %copy-done.4, bf16[4,64,3584]{2,1,0:T(8,128)(2,1)} %all-to-all-done.5), kind=kLoop, calls=%fused_computation.4 | loop fusion | flops 29360128 | bytes 14680064 | tf_op jit(solution)/shard_map/concatenate | solution.py:35
  (117 shorter events, 59.7 us)
Async XLA Ops:
  7.2 1.3 copy-start
  9.7 99.5 %all-to-all-start = ((bf16[32,8,1024]{2,1,0:T(8,128)(2,1)}), bf16[32,8,1024]{2,1,0:T(8,128)(2,1)S(1)}, u32[]{:S(2)}, u32[]{:S(2)}) async-start(bf16[32,8,1024]{2,1,0:T(8,128)(2,1)} %slice_bitcast_fusion), calls=%async_computation | async-start | bytes 1048576 | tf_op jit(solution)/shard_map/all_to_all | solution.py:80
  17.1 11.1 %copy-start.8 = (f32[2,16,8]{1,2,0:T(8,128)S(1)}, f32[2,16,8]{1,2,0:T(8,128)}, u32[]{:S(2)}) copy-start(f32[2,16,8]{1,2,0:T(8,128)} %param.8) | copy-start | bytes 3076
  17.1 11.3 %copy-start.10 = (u32[128]{0:T(128)S(1)}, u32[128]{0:T(128)}, u32[]{:S(2)}) copy-start(u32[128]{0:T(128)} %constant.247) | copy-start | bytes 1540
  17.1 12.6 %copy-start.9 = (s32[32]{0:T(128)S(1)}, s32[32]{0:T(128)}, u32[]{:S(2)}) copy-start(s32[32]{0:T(128)} %param.11) | copy-start | bytes 388
  21.1 26.2 %collective-permute-start = (bf16[2,64,3584]{2,1,0:T(8,128)(2,1)}, bf16[2,64,3584]{2,1,0:T(8,128)(2,1)}, u32[]{:S(2)}, u32[]{:S(2)}) collective-permute-start(bf16[2,64,3584]{2,1,0:T(8,128)(2,1)} %get-tuple-element.7), channel_id=1, source_target_pairs={{0,16},{8,24},{16,0},{24,8},{1,17},{9,25},{17,1},{25,9},{2,18},{10... | collective-permute-start | bytes 2752520 | tf_op jit(solution)/shard_map/ppermute | solution.py:13
  24.4 42.6 %collective-permute-start.1 = (bf16[2,64,3584]{2,1,0:T(8,128)(2,1)}, bf16[2,64,3584]{2,1,0:T(8,128)(2,1)}, u32[]{:S(2)}, u32[]{:S(2)}) collective-permute-start(bf16[2,64,3584]{2,1,0:T(8,128)(2,1)} %get-tuple-element.8), channel_id=1, source_target_pairs={{0,16},{8,24},{16,0},{24,8},{1,17},{9,25},{17,1},{25,9},{2,18},{10... | collective-permute-start | bytes 2752520 | tf_op jit(solution)/shard_map/ppermute | solution.py:13
  24.6 61.9 %collective-permute-start.2 = (bf16[2,64,3584]{2,1,0:T(8,128)(2,1)}, bf16[2,64,3584]{2,1,0:T(8,128)(2,1)S(1)}, u32[]{:S(2)}, u32[]{:S(2)}) collective-permute-start(bf16[2,64,3584]{2,1,0:T(8,128)(2,1)} %get-tuple-element.10), channel_id=1, source_target_pairs={{0,16},{8,24},{16,0},{24,8},{1,17},{9,25},{17,1},{25,9},{2,18},{10... | collective-permute-start | bytes 2752520 | tf_op jit(solution)/shard_map/ppermute | solution.py:13
  28.0 77.8 %collective-permute-start.3 = (bf16[2,64,3584]{2,1,0:T(8,128)(2,1)}, bf16[2,64,3584]{2,1,0:T(8,128)(2,1)S(1)}, u32[]{:S(2)}, u32[]{:S(2)}) collective-permute-start(bf16[2,64,3584]{2,1,0:T(8,128)(2,1)} %get-tuple-element.9), channel_id=1, source_target_pairs={{0,16},{8,24},{16,0},{24,8},{1,17},{9,25},{17,1},{25,9},{2,18},{10... | collective-permute-start | bytes 2752520 | tf_op jit(solution)/shard_map/ppermute | solution.py:13
  109.1 28.6 %all-to-all-start.8 = ((bf16[4,64,3584]{2,1,0:T(8,128)(2,1)}), bf16[4,64,3584]{2,1,0:T(8,128)(2,1)S(1)}, u32[]{:S(2)}, u32[]{:S(2)}) async-start(bf16[4,64,3584]{2,1,0:T(8,128)(2,1)} %get-tuple-element.35), calls=%async_computation.8 | async-start | bytes 3670016 | tf_op jit(solution)/shard_map/all_to_all | solution.py:34
  114.4 27.8 %copy-start.7 = (bf16[2,3584]{1,0:T(2,128)(2,1)S(1)}, bf16[2,3584]{1,0:T(2,128)(2,1)}, u32[]{:S(2)}) copy-start(bf16[2,3584]{1,0:T(2,128)(2,1)} %param.10) | copy-start | bytes 43012
  114.5 46.7 %all-gather.4.cloned.1.call-start = ((), (), s32[]{:S(2)}) async-start(), calls=%async_computation.9 | async-start | bytes 1081344 | tf_op jit(solution)/shard_map/all_gather | solution.py:83
  137.8 4.6 %copy-start.2 = (bf16[4,64,3584]{2,1,0:T(8,128)(2,1)}, bf16[4,64,3584]{2,1,0:T(8,128)(2,1)S(1)}, u32[]{:S(2)}) copy-start(bf16[4,64,3584]{2,1,0:T(8,128)(2,1)S(1)} %all-to-all-done.8) | copy-start | bytes 5505028
  137.8 69.3 %all-to-all-start.7 = ((bf16[4,64,3584]{2,1,0:T(8,128)(2,1)}), bf16[4,64,3584]{2,1,0:T(8,128)(2,1)}, u32[]{:S(2)}, u32[]{:S(2)}) async-start(bf16[4,64,3584]{2,1,0:T(8,128)(2,1)} %get-tuple-element.34), calls=%async_computation.7 | async-start | bytes 3670016 | tf_op jit(solution)/shard_map/all_to_all | solution.py:34
  207.0 28.4 %all-to-all-start.6 = ((bf16[4,64,3584]{2,1,0:T(8,128)(2,1)}), bf16[4,64,3584]{2,1,0:T(8,128)(2,1)S(1)}, u32[]{:S(2)}, u32[]{:S(2)}) async-start(bf16[4,64,3584]{2,1,0:T(8,128)(2,1)} %get-tuple-element.33), calls=%async_computation.6 | async-start | bytes 3670016 | tf_op jit(solution)/shard_map/all_to_all | solution.py:34
  213.1 1.5 copy-start.6
  236.7 33.1 %all-to-all-start.3 = ((bf16[8,80,1792]{2,1,0:T(8,128)(2,1)}), bf16[8,80,1792]{2,1,0:T(8,128)(2,1)S(1)}, u32[]{:S(2)}, u32[]{:S(2)}) async-start(bf16[8,80,1792]{2,1,0:T(8,128)(2,1)} %bitcast.77), calls=%async_computation.3 | async-start | bytes 4587520 | tf_op jit(solution)/shard_map/all_to_all | solution.py:132
  241.8 32.9 %collective-permute-start.4 = (bf16[1,3584]{1,0:T(2,128)(2,1)S(1)}, bf16[1,3584]{1,0:T(2,128)(2,1)S(1)}, u32[]{:S(2)}, u32[]{:S(2)}) collective-permute-start(bf16[1,3584]{1,0:T(2,128)(2,1)S(1)} %constant_dynamic-slice_fusion), channel_id=1, source_target_pairs={{0,16},{8,24},{16,0},{24,8},{1,17},{9,25},{17,1},{25,9},{2,18},{10... | collective-permute-start | bytes 21512 | tf_op jit(solution)/shard_map/ppermute | solution.py:13
  269.9 33.7 %all-to-all-start.1 = ((bf16[8,80,1792]{2,1,0:T(8,128)(2,1)}), bf16[8,80,1792]{2,1,0:T(8,128)(2,1)}, u32[]{:S(2)}, u32[]{:S(2)}) async-start(bf16[8,80,1792]{2,1,0:T(8,128)(2,1)} %bitcast.76), calls=%async_computation.1 | async-start | bytes 4587520 | tf_op jit(solution)/shard_map/all_to_all | solution.py:132
  303.5 28.1 %all-to-all-start.5 = ((bf16[4,64,3584]{2,1,0:T(8,128)(2,1)}), bf16[4,64,3584]{2,1,0:T(8,128)(2,1)}, u32[]{:S(2)}, u32[]{:S(2)}) async-start(bf16[4,64,3584]{2,1,0:T(8,128)(2,1)} %get-tuple-element.32), calls=%async_computation.5 | async-start | bytes 3670016 | tf_op jit(solution)/shard_map/all_to_all | solution.py:34
  313.5 33.0 %copy-start.3 = (bf16[4,64,3584]{2,1,0:T(8,128)(2,1)S(1)}, bf16[4,64,3584]{2,1,0:T(8,128)(2,1)}, u32[]{:S(2)}) copy-start(bf16[4,64,3584]{2,1,0:T(8,128)(2,1)} %copy-done.2) | copy-start | bytes 5505028
  331.6 11.4 %all-to-all-start.4 = ((bf16[4,32,1792]{2,1,0:T(8,128)(2,1)}), bf16[4,32,1792]{2,1,0:T(8,128)(2,1)S(1)}, u32[]{:S(2)}, u32[]{:S(2)}) async-start(bf16[4,32,1792]{2,1,0:T(8,128)(2,1)} %bitcast.24), calls=%async_computation.4 | async-start | bytes 917504 | tf_op jit(solution)/shard_map/all_to_all | solution.py:138
  343.0 11.2 %all-to-all-start.2 = ((bf16[4,32,1792]{2,1,0:T(8,128)(2,1)}), bf16[4,32,1792]{2,1,0:T(8,128)(2,1)S(1)}, u32[]{:S(2)}, u32[]{:S(2)}) async-start(bf16[4,32,1792]{2,1,0:T(8,128)(2,1)} %bitcast.20), calls=%async_computation.2 | async-start | bytes 917504 | tf_op jit(solution)/shard_map/all_to_all | solution.py:138
  346.5 9.1 %copy-start.1 = (bf16[2,16,8,1024]{3,2,1,0:T(8,128)(2,1)S(1)}, bf16[2,16,8,1024]{3,2,1,0:T(8,128)(2,1)}, u32[]{:S(2)}) copy-start(bf16[2,16,8,1024]{3,2,1,0:T(8,128)(2,1)} %param.6) | copy-start | bytes 1572868
  (2 other events, 2.3 us)
Sparse Core Ops, SparseCore 0:
  118.1 43.0 all-gather.3

commit v2 on v1

v2 whole, which is shorter than its diff:
```python
import functools

import jax
import jax.numpy as jnp
import numpy as np
from jax import lax
from jax.experimental import pallas as pl
from jax.experimental.pallas import tpu as pltpu
from jax.sharding import Mesh, PartitionSpec as P

X = ("xh", "xl")
EP = X + ("y", "c")
N_X, N_Y, N_C = 4, 4, 2
N_YC = N_Y * N_C
N_EP = N_X * N_YC
BLOCK = 24
TRADED = (80, 112)
COLUMNS = 512
VMEM_LIMIT = 60 << 20
CHEAP = pl.CostEstimate(flops=1000, bytes_accessed=1000, transcendentals=0)
HBM = pl.BlockSpec(memory_space=pltpu.HBM)
SMEM = pl.BlockSpec(memory_space=pltpu.SMEM)
WHOLE = pl.BlockSpec(memory_space=pltpu.VMEM)


def shifted(block, axis, distance):
    count = lax.axis_size(axis)
    return lax.ppermute(block, axis, [(i, (i + distance) % count) for i in range(count)])


TOKEN = jax.ShapeDtypeStruct((8, 128), jnp.float32)


def ordered_call(kernel, operands, after, out_shape, out_specs, scratch, in_specs=None, aliases=None):
    after = [t for t in after if t is not None]
    in_specs = in_specs or [HBM] * len(operands)

    def body(*refs):
        ins, rest = refs[: len(operands)], refs[len(operands) + len(after) :]
        kernel(*ins, *rest[: len(out_shape)], *rest[len(out_shape) + 1 :])

    *outs, token = pl.pallas_call(
        body,
        out_shape=list(out_shape) + [TOKEN],
        in_specs=list(in_specs) + [HBM] * len(after),
        out_specs=list(out_specs) + [HBM],
        scratch_shapes=scratch,
        input_output_aliases=aliases or {},
        compiler_params=pltpu.CompilerParams(vmem_limit_bytes=VMEM_LIMIT),
        cost_estimate=CHEAP,
    )(*operands, *after)
    return outs, token


def through(moves, reads, writes):
    reading = [pltpu.make_async_copy(m[0], m[1], reads.at[i]) for i, m in enumerate(moves)]
    writing = [pltpu.make_async_copy(m[1], m[2], writes.at[i]) for i, m in enumerate(moves)]
    for copy in reading:
        copy.start()
    for read, write in zip(reading, writing):
        read.wait()
        write.start()
    for copy in writing:
        copy.wait()


def cut_kernel(ranges, quarter, part, weight, *refs):
    count = len(ranges)
    outs, held, (reads, writes) = refs[:count], refs[count : 2 * count], refs[2 * count :]
    moves = []
    for out, stop, (at, rows) in zip(outs, held, ranges):
        start = pl.multiple_of(part[0] * quarter + at, 16)
        moves.append((weight.at[:, pl.ds(start, rows)], stop, out))
    through(moves, reads, writes)


def cut(part, weight, ranges, quarter, after):
    shapes = [(2, rows, weight.shape[2]) for _, rows in ranges]
    return ordered_call(
        functools.partial(cut_kernel, ranges, quarter),
        [part, weight],
        after,
        [jax.ShapeDtypeStruct(shape, weight.dtype) for shape in shapes],
        [HBM] * len(shapes),
        [pltpu.VMEM(shape, weight.dtype) for shape in shapes]
        + [pltpu.SemaphoreType.DMA((len(shapes),))] * 2,
        in_specs=[SMEM, HBM],
    )


def last_kernel(partner, weight, *refs):
    *refs, held, reads, writes = refs
    out = refs[(len(refs) - 1) // 2]
    rows = held.shape[1]
    first = weight.shape[1] - out.shape[0]
    moves = []
    for i in range(held.shape[0]):
        source = weight.at[partner[0], pl.ds(first + i * rows, rows)]
        moves.append((source, held.at[i], out.at[pl.ds(i * rows, rows)]))
    through(moves, reads, writes)


def last_rows(partner, weight, count, after, passed):
    shape = (count, weight.shape[2])
    return ordered_call(
        last_kernel,
        [partner, weight, *passed],
        after,
        [jax.ShapeDtypeStruct(shape, weight.dtype)]
        + [jax.ShapeDtypeStruct(p.shape, p.dtype) for p in passed],
        [HBM] * (1 + len(passed)),
        [pltpu.VMEM((4, count // 4, shape[1]), weight.dtype)]
        + [pltpu.SemaphoreType.DMA((4,))] * 2,
        in_specs=[SMEM, HBM] + [HBM] * len(passed),
        aliases={2 + i: 1 + i for i in range(len(passed))},
    )


def pick_kernel(others, picks, block, *refs):
    *refs, held, reads, writes = refs
    passed = (len(refs) - others) // 2
    outs = refs[passed : passed + others]
    through([(block.at[picks[i + 1]], held.at[i], o) for i, o in enumerate(outs)], reads, writes)


def pick(picks, block, parts, after, passed=()):
    others = parts - 1
    operands = [picks, block, *passed]
    return ordered_call(
        functools.partial(pick_kernel, others),
        operands,
        after,
        [jax.ShapeDtypeStruct(block.shape[1:], block.dtype)] * others
        + [jax.ShapeDtypeStruct(p.shape, p.dtype) for p in passed],
        [HBM] * (others + len(passed)),
        [pltpu.VMEM((others,) + block.shape[1:], block.dtype)]
        + [pltpu.SemaphoreType.DMA((others,))] * 2,
        in_specs=[SMEM] + [HBM] * (1 + len(passed)),
        aliases={2 + i: others + i for i in range(len(passed))},
    )


def place_kernel(at, quarter, parts, picks, part, block, *refs):
    *refs, held, reads, writes = refs
    arrived, out = refs[: parts - 1], refs[-1]
    rows = arrived[0].shape[0]
    moves = []
    for i, source in enumerate([block.at[picks[0]], *arrived]):
        origin = lax.rem(part[0] - i + parts, parts)
        start = pl.multiple_of(origin * quarter + at, 16)
        moves.append((source, held.at[i], out.at[0, pl.ds(start, rows)]))
    through(moves, reads, writes)


def placed(picks, part, block, arrived, at, quarter, depth, whole, after):
    parts = len(arrived) + 1
    rows, width = arrived[0].shape
    chained = whole is not None
    operands = [picks, part, block, *arrived] + ([whole] if chained else [])
    (whole,), token = ordered_call(
        functools.partial(place_kernel, at, quarter, parts),
        operands,
        after,
        [jax.ShapeDtypeStruct((1, depth, width), block.dtype)],
        [HBM],
        [pltpu.VMEM((parts, rows, width), block.dtype)]
        + [pltpu.SemaphoreType.DMA((parts,))] * 2,
        in_specs=[SMEM, SMEM] + [HBM] * (len(operands) - 2),
        aliases={len(operands) - 1: 0} if chained else {},
    )
    return whole, token


def direct_kernel(block, _, out, held, reads, writes):
    rows = block.shape[0] // 4
    through(
        [
            (
                block.at[pl.ds(i * rows, rows)],
                held.at[i],
                out.at[0, pl.ds(out.shape[1] - (4 - i) * rows, rows)],
            )
            for i in range(4)
        ],
        reads,
        writes,
    )


def placed_direct(block, whole, after):
    (whole,), token = ordered_call(
        direct_kernel,
        [block, whole],
        after,
        [jax.ShapeDtypeStruct(whole.shape, whole.dtype)],
        [HBM],
        [pltpu.VMEM((4, block.shape[0] // 4, block.shape[1]), block.dtype)]
        + [pltpu.SemaphoreType.DMA((4,))] * 2,
        aliases={1: 0},
    )
    return whole, token


def rank_of(expert_list):
    count = expert_list.shape[-1]
    order = jnp.arange(count, dtype=jnp.int32)
    same = expert_list[..., :, None] == expert_list[..., None, :]
    return jnp.sum(same & (order[:, None] > order[None, :]), axis=-1, dtype=jnp.int32)


def one_hot_rows(sources, count):
    table = np.zeros((len(sources), count), np.float32)
    table[np.arange(len(sources)), sources] = 1.0
    return table


STACK = N_X * 20


def return_order():
    rows, names = [], []
    for yc in range(N_YC):
        bases = [(x * N_YC + yc) * BLOCK for x in range(N_X)]
        for base in bases:
            rows += [base + r for r in range(8)]
            names += [base + 15] * 8
        for base in bases:
            for at in (base + 8, base + 16):
                rows += [at + r for r in range(6)]
                names += [at + 7] * 6
    return one_hot_rows(rows, N_EP * BLOCK), one_hot_rows(names, N_EP * BLOCK)


def scale_kernel(partner, scale, out):
    first = scale[0:1].astype(jnp.float32)
    second = scale[1:2].astype(jnp.float32)
    out[...] = jnp.where(partner[0] == 0, first, second).astype(out.dtype)


def chosen_scale(partner, scale, after):
    (chosen,), token = ordered_call(
        scale_kernel,
        [partner, scale],
        after,
        [jax.ShapeDtypeStruct((1, scale.shape[1]), scale.dtype)],
        [WHOLE],
        [],
        in_specs=[SMEM, WHOLE],
    )
    return chosen, token


def serve_kernel(me, received, order, naming, weight, scale, *refs):
    out, _, spread, held, product, reads, writes = refs[-7:]
    depth = received.shape[1]
    tiles = held.shape[0]
    columns = [pl.ds(i * COLUMNS, COLUMNS) for i in range(tiles)]
    reading = [
        pltpu.make_async_copy(weight.at[:, :, columns[i]], held.at[i], reads.at[i])
        for i in range(tiles)
    ]
    writing = [
        pltpu.make_async_copy(product.at[i], out.at[:, columns[i]], writes.at[i])
        for i in range(tiles)
    ]
    for copy in reading:
        copy.start()
    ordered = jnp.dot(order[...], received[...], preferred_element_type=jnp.float32)
    named = jnp.dot(naming[...], received[:, :128], preferred_element_type=jnp.float32)
    row = lax.broadcasted_iota(jnp.int32, named.shape, 0)
    lane = jnp.where(
        row % STACK < N_X * 8,
        ((row // 4) % 2).astype(jnp.float32),
        named - (2 * me[0]).astype(jnp.float32),
    )[:, 0:1]
    spread[:, :depth] = jnp.where(lane == 0.0, ordered, 0.0).astype(jnp.bfloat16)
    spread[:, depth:] = jnp.where(lane == 1.0, ordered, 0.0).astype(jnp.bfloat16)
    for i in range(tiles):
        reading[i].wait()
        both = held[i].reshape(2 * depth, COLUMNS)
        scales = scale[:, i * COLUMNS : (i + 1) * COLUMNS].astype(jnp.float32)
        total = jnp.dot(spread[...], both, preferred_element_type=jnp.float32)
        total = total * jnp.where(lane == 0.0, scales[0:1], scales[1:2])
        product[i] = total.astype(jnp.bfloat16)
        writing[i].start()
    for copy in writing:
        copy.wait()


def serve(me, received, weight, scale, after):
    order, naming = (jnp.asarray(table, jnp.bfloat16) for table in return_order())
    rows = order.shape[0]
    _, depth, width = weight.shape
    tiles = width // COLUMNS
    return pl.pallas_call(
        serve_kernel,
        in_specs=[SMEM, WHOLE, WHOLE, WHOLE, HBM, WHOLE] + [HBM] * len(after),
        out_specs=[HBM, HBM],
        scratch_shapes=[
            pltpu.VMEM((rows, 2 * depth), jnp.bfloat16),
            pltpu.VMEM((tiles, 2, depth, COLUMNS), jnp.bfloat16),
            pltpu.VMEM((tiles, rows, COLUMNS), jnp.bfloat16),
            pltpu.SemaphoreType.DMA((tiles,)),
            pltpu.SemaphoreType.DMA((tiles,)),
        ],
        out_shape=[jax.ShapeDtypeStruct((rows, width), jnp.bfloat16), TOKEN],
        compiler_params=pltpu.CompilerParams(vmem_limit_bytes=VMEM_LIMIT),
        cost_estimate=CHEAP,
    )(me, received, order, naming, weight, scale, *after)


def mixing(told, my_x, steps, rows, top):
    items = rows * top
    told = told.astype(jnp.float32).reshape(N_X, 4, steps, items)
    ids = told[:, 0].astype(jnp.int32)
    gates = told[:, 1] + told[:, 2] + told[:, 3]
    rank = rank_of(ids)
    who = jnp.arange(N_X * steps, dtype=jnp.int32).reshape(N_X, steps, 1) * 256
    code = jnp.where(rank < 2, ids * 2 + rank, 128 + rank - 2) + who
    source = jnp.arange(N_YC, dtype=jnp.int32)[:, None]
    row = jnp.arange(N_X * 8, dtype=jnp.int32)[None, :]
    slot_code = ((N_YC * my_x + source) * 2 + (row % 8) // 4) * 2 + row % 2
    slot_code = slot_code + ((row // 8) * steps + (row % 4) // 2) * 256
    row = jnp.arange(N_X * 12, dtype=jnp.int32)[None, :]
    hot_code = 128 + row % 6 + ((row // 12) * steps + (row % 12) // 6) * 256
    hot_code = jnp.broadcast_to(hot_code, (N_YC, N_X * 12))
    column_code = jnp.concatenate([slot_code, hot_code], 1).reshape(-1)
    code = code.reshape(N_X * steps * rows, top)
    gates = gates.reshape(N_X * steps * rows, top)
    mix = jnp.sum(
        jnp.where(code[:, :, None] == column_code[None, None, :], gates[:, :, None], 0.0), axis=1
    )
    high = lax.reduce_precision(mix, 8, 7)
    return jnp.concatenate([high, mix - high], 0).astype(jnp.bfloat16)


def mix_kernel(mixes, returned, out, held, product, reads, writes):
    tiles = held.shape[0]
    columns = [pl.ds(i * COLUMNS, COLUMNS) for i in range(tiles)]
    reading = [
        pltpu.make_async_copy(returned.at[:, columns[i]], held.at[i], reads.at[i])
        for i in range(tiles)
    ]
    writing = [
        pltpu.make_async_copy(product.at[i], out.at[:, columns[i]], writes.at[i])
        for i in range(tiles)
    ]
    for copy in reading:
        copy.start()
    many = out.shape[0]
    for i in range(tiles):
        reading[i].wait()
        total = jnp.dot(mixes[...], held[i], preferred_element_type=jnp.float32)
        product[i] = (total[:many] + total[many:]).astype(out.dtype)
        writing[i].start()
    for copy in writing:
        copy.wait()


def mixed(mixes, returned):
    rows, (many, width) = mixes.shape[0] // 2, returned.shape
    tiles = width // COLUMNS
    return pl.pallas_call(
        mix_kernel,
        in_specs=[WHOLE, HBM],
        out_specs=HBM,
        out_shape=jax.ShapeDtypeStruct((rows, width), jnp.bfloat16),
        scratch_shapes=[
            pltpu.VMEM((tiles, many, COLUMNS), jnp.bfloat16),
            pltpu.VMEM((tiles, rows, COLUMNS), jnp.bfloat16),
            pltpu.SemaphoreType.DMA((tiles,)),
            pltpu.SemaphoreType.DMA((tiles,)),
        ],
        compiler_params=pltpu.CompilerParams(vmem_limit_bytes=VMEM_LIMIT),
        cost_estimate=CHEAP,
    )(mixes, returned)


def local(hidden_in, expert_ids, gates, expert_weight, column_scale, replica_map):
    steps, rows, top, depth = hidden_in.shape
    width = expert_weight.shape[2]
    items = rows * top
    my_x, my_yc, me = lax.axis_index(X), lax.axis_index(("y", "c")), lax.axis_index(EP)

    expert_list = expert_ids.reshape(steps, items)
    rank = rank_of(expert_list)
    step_of = jnp.arange(steps, dtype=jnp.int32)[:, None]
    place = jnp.where(
        rank < 2,
        (expert_list // 2) * BLOCK + (expert_list % 2) * 4 + step_of * 2 + rank,
        1000 + step_of * 8 + rank - 2,
    ).reshape(steps * items)
    place = jnp.concatenate([place, jnp.array([1006, 1007, 1015, -1, -1, -1, -1, -1], jnp.int32)])
    line = jnp.arange(N_EP * BLOCK, dtype=jnp.int32)
    line = jnp.where(line % BLOCK < 8, line, 1000 + line % BLOCK - 8)
    selector = (line[:, None] == place[None, :]).astype(jnp.bfloat16)
    hot_id = jnp.sum(jnp.where(rank == 7, expert_list, 0), axis=1).astype(jnp.float32)
    flat_gates = gates.reshape(steps * items)
    high = lax.reduce_precision(flat_gates, 8, 7)
    middle = lax.reduce_precision(flat_gates - high, 8, 7)
    low = flat_gates - high - middle
    told = jnp.concatenate([expert_list.reshape(steps * items).astype(jnp.float32), high, middle, low])
    further = jnp.concatenate(
        [told[None], jnp.broadcast_to(hot_id[:, None], (steps, depth)), jnp.zeros((5, depth), jnp.float32)]
    ).astype(jnp.bfloat16)
    hidden = jnp.concatenate([hidden_in.reshape(steps * items, depth), further])
    part, parts = lax.axis_index("dp"), lax.axis_size("dp")
    here = part.reshape(1).astype(jnp.int32)
    quarter = sum(TRADED)
    starts = [sum(TRADED[:i]) for i in range(len(TRADED))]
    ranges = list(zip(starts, TRADED))
    partner = lax.dynamic_slice(replica_map, ((me + N_EP // 2) % N_EP,), (1,)) % 2
    blocks, token = cut(here, expert_weight, ranges, quarter, [])
    crossed = [shifted(block, "xh", 1) for block in blocks]

    outgoing = jnp.dot(selector, hidden, preferred_element_type=jnp.float32).astype(jnp.bfloat16)
    received = lax.all_to_all(outgoing.reshape(N_EP, BLOCK, depth), EP, 0, 0, tiled=True)
    mine = lax.dynamic_slice(replica_map, (me,), (1,)) % 2
    picks = lax.psum(jnp.where(jnp.arange(parts) == part, mine, 0), "dp")
    picks = jnp.roll(picks, -part)
    scale, _ = chosen_scale(partner, column_scale, [])
    replica_scale = shifted(scale, "xh", 1)

    def traded(j, after, passed=()):
        (*sent, last), token = pick(picks, crossed[j], parts, after, passed)
        if not passed:
            sent, last = sent + [last], None
        return [shifted(piece, "dp", d + 1) for d, piece in enumerate(sent)], last, token

    def put(j, pieces, whole, after):
        return placed(picks, here, crossed[j], pieces, starts[j], quarter, depth, whole, after)

    received = received.reshape(N_EP * BLOCK, depth)
    where = me.reshape(1).astype(jnp.int32)
    returned, token = serve(where, received, expert_weight, column_scale, [token, picks])
    told = received.reshape(N_X, N_YC, BLOCK, depth)[:, :, 14]
    told = lax.dynamic_index_in_dim(told, my_yc, 1, keepdims=False)
    first, returned, token = traded(0, [token, replica_scale], [returned])
    returned = lax.all_to_all(returned.reshape(N_YC, -1, width), ("y", "c"), 0, 0, tiled=True)
    whole, token = put(0, first, None, [token])
    (direct, told), token = last_rows(
        partner, expert_weight, depth - parts * quarter, [token], [told]
    )
    direct = shifted(direct, "xh", 1)
    second, _, token = traded(1, [token])
    whole, token = put(1, second, whole, [token])
    replica_weight, token = placed_direct(direct, whole, [token])

    mixes = mixing(told, my_x, steps, rows, top)
    partial = mixed(mixes, returned.reshape(-1, width))
    partial = lax.all_to_all(partial.reshape(N_X, steps * rows, width), X, 0, 0, tiled=True)
    combined = jnp.sum(partial.astype(jnp.float32), axis=0).astype(jnp.bfloat16)
    return combined.reshape(steps, rows, width), replica_weight, replica_scale


def solution(mesh):
    grid = Mesh(mesh.devices.reshape(-1, 2, N_X // 2, N_Y, N_C), ("dp",) + EP)
    everywhere = ("dp",) + EP
    in_specs = (
        P(None, everywhere, None, None),
        P(None, everywhere, None),
        P(None, everywhere, None),
        P(EP, None, None),
        P(EP, None),
        P("dp"),
    )
    out_specs = (P(None, everywhere, None), P(everywhere, None, None), P(everywhere, None))
    return jax.shard_map(local, mesh=grid, in_specs=in_specs, out_specs=out_specs, check_vma=False)
```

time: 365 us -> 180 us (0.49)
  waiting for transfers between devices: 181 us -> 52.5 us
  local copies, waits for them, and re-layouts: 61.5 us -> 12.6 us
  Pallas kernels: 0 us -> 43.5 us
  matrix products: 24.3 us -> 3.33 us
  other arithmetic: 19.6 us -> 4.26 us
  between operations: 15.8 us -> 4.79 us
    all_to_all x9 -> x3, waiting for transfers between devices: 99.5 us -> 1.11 us  [the longest x1 0.94 us: local(): lax.all_to_all(partial.reshape(N_X, steps * rows, width), X, 0, 0, tiled=...]
    pallas_call x0 -> x10, Pallas kernels: none -> 43.5 us  [the longest x8 22.9 us: ordered_call(): pl.pallas_call(body, out_shape=list(out_shape) + [TOKEN], in_specs=list(i...]
    slice x5 -> x1, local copies, waits for them, and re-layouts: 28.7 us -> 1.18 us  [local(): told = received.reshape(N_X, N_YC, BLOCK, depth)[:, :, 14]]
    all_to_all x9 -> x3, starting transfers between devices: 41.2 us -> 16.9 us  [the longest x1 7.4 us: local(): lax.all_to_all(outgoing.reshape(N_EP, BLOCK, depth), EP, 0, 0, tiled=True)]
    ppermute x5 -> x10, starting transfers between devices: 9.74 us -> 31.7 us  [shifted(): lax.ppermute(block, axis, [(i, (i + distance) % count) for i in range(cou...]
    dot_general x5 -> x1, matrix products: 24.3 us -> 3.33 us  [local(): jnp.dot(selector, hidden, preferred_element_type=jnp.float32)]
    all_gather x1 -> x0, waiting for transfers between devices: 18.5 us -> none  [local(): hot_all = lax.all_gather(hot_block, EP)]
    reshape x4 -> x2, local copies, waits for them, and re-layouts: 17 us -> 0.81 us  [the longest x1 0.72 us: mixing(): told = told.astype(jnp.float32).reshape(N_X, 4, steps, items)]
  transfers between devices with their start and end apart: 15 -> 13, of which waited for: 12 -> 7; matrix products, arithmetic and copies ran while one was open for 27% -> 4% of each run, Pallas kernels for 0% -> 22%
where the time goes in v2:
time: 180 us; the launch traced here: 179 us
  waiting for transfers between devices  52.5 us (29%)
  starting transfers between devices  48.7 us (27%)
  Pallas kernels  43.5 us (24%)
  local copies, waits for them, and re-layouts  12.6 us (7%)
  blocking collectives  9.73 us (5%)
  between operations  4.79 us (3%)
  other arithmetic  4.26 us (2%)
  matrix products  3.33 us (2%)
    ppermute x10, waiting for transfers between devices, shifted(): lax.ppermute(block, axis, [(i, (i + distance) % count) for i in range(cou...  51.4 us
    ppermute x10, starting transfers between devices, shifted(): lax.ppermute(block, axis, [(i, (i + distance) % count) for i in range(cou...  31.7 us
    pallas_call x8, Pallas kernels, ordered_call(): pl.pallas_call(body, out_shape=list(out_shape) + [TOKEN], in_specs=list(i...  22.9 us
    pallas_call x1, Pallas kernels, serve(): pl.pallas_call(serve_kernel, in_specs=[SMEM, WHOLE, WHOLE, WHOLE, HBM, WH...  15.2 us
    psum x1, blocking collectives, local(): picks = lax.psum(jnp.where(jnp.arange(parts) == part, mine, 0), 'dp')  9.73 us
    unnamed x24, local copies, waits for them, and re-layouts  8.37 us
    all_to_all x1, starting transfers between devices, local(): lax.all_to_all(outgoing.reshape(N_EP, BLOCK, depth), EP, 0, 0, tiled=True)  7.4 us
    pallas_call x1, Pallas kernels, mixed(): pl.pallas_call(mix_kernel, in_specs=[WHOLE, HBM], out_specs=HBM, out_shap...  5.45 us
  transfers between devices with their start and end apart: 13, of which 7 were waited for; matrix products, arithmetic and copies ran while one was open for 4% of the time, Pallas kernels for 22%

profile of v2, /device:TPU:0, one launch (start us, length us, event | category | flops | bytes accessed | tf_op | source)
XLA Modules:
  0.0 179.4 jit_solution(17918027162871457269)
XLA Ops:
  3.9 3.3 %convolution_convert_fusion = bf16[768,1024]{1,0:T(8,128)(2,1)} fusion(s32[264]{0:T(512)S(1)} %pad_add_fusion.1, s32[768]{0:T(1024)S(1)} %iota_select_fusion, bf16[1,1024]{1,0:T(2,128)(2,1)S(1)} %broadcast_in_dim.33, bf16[256,1024]{1,0:T(8,128)(2,1)} %bitcast.63, bf16[264]{0:T(512)(128)(2,1)S(1)} %pad.9.clone, bf16[264]{0:T(512)(128)(2,1)S(1)} %pad.8.clone), kind=kOutput, calls=%fused_computation.1 | convolution fusion | flops 418387968 | bytes 2104384 | tf_op jit(solution)/shard_map/dot_general | solution.py:416
  7.2 7.4 %all-to-all-start = ((bf16[32,24,1024]{2,1,0:T(8,128)(2,1)}), bf16[32,24,1024]{2,1,0:T(8,128)(2,1)S(1)}, u32[]{:S(2)}, u32[]{:S(2)}) async-start(bf16[32,24,1024]{2,1,0:T(8,128)(2,1)} %bitcast.4), calls=%async_computation | async-start | bytes 3145728 | tf_op jit(solution)/shard_map/all_to_all | solution.py:417
  14.6 3.0 %shard_map.112 = (bf16[2,80,3584]{2,1,0:T(8,128)(2,1)}, bf16[2,112,3584]{2,1,0:T(8,128)(2,1)}, f32[8,128]{1,0:T(8,128)}) custom-call(s32[1]{0:T(128)} %bitcast.7.refs_0_.refs_1_, bf16[2,1024,3584]{2,1,0:T(8,128)(2,1)} %refs_1_.5), custom_call_target="tpu_custom_call" | custom-call | flops 1000 | bytes 1000 | tf_op jit(solution)/shard_map/pallas_call | solution.py:42
  17.6 3.4 %collective-permute-start = (bf16[2,80,3584]{2,1,0:T(8,128)(2,1)}, bf16[2,80,3584]{2,1,0:T(8,128)(2,1)S(1)}, u32[]{:S(2)}, u32[]{:S(2)}) collective-permute-start(bf16[2,80,3584]{2,1,0:T(8,128)(2,1)} %get-tuple-element.26), channel_id=1, source_target_pairs={{0,16},{16,0},{1,17},{17,1},{2,18},{18,2},{3,19},{19,3},{4,20},{20... | collective-permute-start | bytes 3440648 | tf_op jit(solution)/shard_map/ppermute | solution.py:28
  27.2 9.7 %psum.7 = s32[4]{0:T(128)S(1)} all-reduce(s32[4]{0:T(128)S(1)} %compare_select_fusion), channel_id=1, replica_groups=mesh['dp'=4,'xh'=2,'xl'=2,'y'=4,'c'=2] {'dp'}, use_global_device_ids=true, to_apply=%region_2.3 | all-reduce | flops 4 | bytes 32 | tf_op jit(solution)/shard_map/psum | solution.py:419
  38.9 15.2 %shard_map.113 = (bf16[640,3584]{1,0:T(8,128)(2,1)}, f32[8,128]{1,0:T(8,128)}) custom-call(s32[1]{0:T(128)} %bitcast.8.me, bf16[768,1024]{1,0:T(8,128)(2,1)} %bitcast.58, bf16[640,768]{1,0:T(8,128)(2,1)} %constant.249.clone.order, bf16[640,768]{1,0:T(8,128)(2,1)} %constant.250.clone.naming, bf16[2,1024,3584]{2,1,0:T(8,128)(2,1)} %refs_1_.5, ...), custom_call_target="tpu_custom_call" | custom-call | flops 1000 | bytes 1000 | tf_op jit(solution)/shard_map/pallas_call | solution.py:295
  54.1 6.8 %collective-permute-done.1.refs_4_ = bf16[1,3584]{1,0:T(2,128)(2,1)S(1)} collective-permute-done((bf16[1,3584]{1,0:T(2,128)(2,1)}, bf16[1,3584]{1,0:T(2,128)(2,1)S(1)}, u32[]{:S(2)}, u32[]{:S(2)}) %collective-permute-start.1) | collective-permute-done | bytes 7200 | tf_op jit(solution)/shard_map/ppermute | solution.py:28
  61.8 3.3 %shard_map.115 = (bf16[80,3584]{1,0:T(8,128)(2,1)}, bf16[80,3584]{1,0:T(8,128)(2,1)}, bf16[80,3584]{1,0:T(8,128)(2,1)}, bf16[640,3584]{1,0:T(8,128)(2,1)}, f32[8,128]{1,0:T(8,128)}) custom-call(s32[4]{0:T(128)} %dynamic_slice.17.refs_1_.refs_0_, bf16[2,80,3584]{2,1,0:T(8,128)(2,1)} %copy-done.2, ...), custom_call_target="tpu_custom_call", output_to_operand_aliasing={{3}: (2, {})} | custom-call | flops 1000 | bytes 1000 | tf_op jit(solution)/shard_map/pallas_call | solution.py:42
  65.2 4.6 %all-to-all-start.1 = ((bf16[8,80,3584]{2,1,0:T(8,128)(2,1)}), bf16[8,80,3584]{2,1,0:T(8,128)(2,1)}, u32[]{:S(2)}, u32[]{:S(2)}) async-start(bf16[8,80,3584]{2,1,0:T(8,128)(2,1)} %bitcast.57), calls=%async_computation.1 | async-start | bytes 9175040 | tf_op jit(solution)/shard_map/all_to_all | solution.py:439
  69.8 16.8 %collective-permute-start.6 = (bf16[2,112,3584]{2,1,0:T(8,128)(2,1)}, bf16[2,112,3584]{2,1,0:T(8,128)(2,1)S(1)}, u32[]{:S(2)}, u32[]{:S(2)}) collective-permute-start(bf16[2,112,3584]{2,1,0:T(8,128)(2,1)} %get-tuple-element.39), channel_id=1, source_target_pairs={{0,16},{16,0},{1,17},{17,1},{2,18},{18,2},{3,19},{19,3},{4,20},{20... | collective-permute-start | bytes 4816904 | tf_op jit(solution)/shard_map/ppermute | solution.py:28
  86.7 1.7 collective-permute-start.2
  88.5 3.9 %collective-permute-start.3 = (bf16[80,3584]{1,0:T(8,128)(2,1)}, bf16[80,3584]{1,0:T(8,128)(2,1)S(1)}, u32[]{:S(2)}, u32[]{:S(2)}) collective-permute-start(bf16[80,3584]{1,0:T(8,128)(2,1)} %get-tuple-element.32), channel_id=1, source_target_pairs={{0,64},{32,96},{64,0},{96,32},{1,65},{33,97},{65,1},{97,33},{2,66}... | collective-permute-start | bytes 1720328 | tf_op jit(solution)/shard_map/ppermute | solution.py:28
  95.5 8.7 %collective-permute-done.2.refs_3_ = bf16[80,3584]{1,0:T(8,128)(2,1)S(1)} collective-permute-done((bf16[80,3584]{1,0:T(8,128)(2,1)}, bf16[80,3584]{1,0:T(8,128)(2,1)S(1)}, u32[]{:S(2)}, u32[]{:S(2)}) %collective-permute-start.2) | collective-permute-done | bytes 573472 | tf_op jit(solution)/shard_map/ppermute | solution.py:28
  104.2 13.5 %collective-permute-done.3.refs_4_ = bf16[80,3584]{1,0:T(8,128)(2,1)S(1)} collective-permute-done((bf16[80,3584]{1,0:T(8,128)(2,1)}, bf16[80,3584]{1,0:T(8,128)(2,1)S(1)}, u32[]{:S(2)}, u32[]{:S(2)}) %collective-permute-start.3) | collective-permute-done | bytes 573472 | tf_op jit(solution)/shard_map/ppermute | solution.py:28
  118.7 3.2 %shard_map.116 = (bf16[1,1024,3584]{2,1,0:T(8,128)(2,1)}, f32[8,128]{1,0:T(8,128)}) custom-call(s32[4]{0:T(128)} %dynamic_slice.17.refs_1_.refs_0_, s32[1]{0:T(128)} %bitcast.7.refs_0_.refs_1_, bf16[2,80,3584]{2,1,0:T(8,128)(2,1)} %copy-done.2, bf16[80,3584]{1,0:T(8,128)(2,1)} %copy-done.4, bf16[80,3584]{1,0:T(8,128)(2,1)} %copy-done.5, ...), custom_call_target="tpu_custom_call" | custom-call | flops 1000 | bytes 1000 | tf_op jit(solution)/shard_map/pallas_call | solution.py:42
  121.9 2.3 %shard_map.117 = (bf16[256,3584]{1,0:T(8,128)(2,1)}, bf16[4,1024]{1,0:T(4,128)(2,1)}, f32[8,128]{1,0:T(8,128)}) custom-call(s32[1]{0:T(128)S(6)} %select_n.192.refs_0_, bf16[2,1024,3584]{2,1,0:T(8,128)(2,1)} %refs_1_.5, bf16[4,1024]{1,0:T(4,128)(2,1)} %bitcast.62, f32[8,128]{1,0:T(8,128)} %get-tuple-element.35.refs_3_), custom_call_target="tpu_custom_call", output_to_operand_aliasing={{1}: (2, {})} | custom-call | flops 1000 | bytes 1000 | tf_op jit(solution)/shard_map/pallas_call | solution.py:42
  126.7 3.9 %shard_map.119 = (bf16[112,3584]{1,0:T(8,128)(2,1)}, bf16[112,3584]{1,0:T(8,128)(2,1)}, bf16[112,3584]{1,0:T(8,128)(2,1)}, f32[8,128]{1,0:T(8,128)}) custom-call(s32[4]{0:T(128)} %dynamic_slice.17.refs_1_.refs_0_, bf16[2,112,3584]{2,1,0:T(8,128)(2,1)} %copy-done.1, f32[8,128]{1,0:T(8,128)} %get-tuple-element.40.refs_2_), custom_call_target="tpu_custom_call" | custom-call | flops 1000 | bytes 1000 | tf_op jit(solution)/shard_map/pallas_call | solution.py:42
  132.2 1.9 %collective-permute-start.8 = (bf16[112,3584]{1,0:T(8,128)(2,1)}, bf16[112,3584]{1,0:T(8,128)(2,1)}, u32[]{:S(2)}, u32[]{:S(2)}) collective-permute-start(bf16[112,3584]{1,0:T(8,128)(2,1)} %get-tuple-element.42), channel_id=1, source_target_pairs={{0,64},{32,96},{64,0},{96,32},{1,65},{33,97},{65,1},{97,33},{2,66}... | collective-permute-start | bytes 2408456 | tf_op jit(solution)/shard_map/ppermute | solution.py:28
  137.1 5.5 %shard_map.118 = bf16[128,3584]{1,0:T(8,128)(2,1)} custom-call(bf16[256,640]{1,0:T(8,128)(2,1)} %pad_maximum_fusion.mixes, bf16[640,3584]{1,0:T(8,128)(2,1)} %bitcast.12.returned), custom_call_target="tpu_custom_call" | custom-call | flops 1000 | bytes 1000 | tf_op jit(solution)/shard_map/pallas_call | solution.py:363
  142.5 4.9 %all-to-all-start.2 = ((bf16[4,32,3584]{2,1,0:T(8,128)(2,1)}), bf16[4,32,3584]{2,1,0:T(8,128)(2,1)S(1)}, u32[]{:S(2)}, u32[]{:S(2)}) async-start(bf16[4,32,3584]{2,1,0:T(8,128)(2,1)} %bitcast.60), calls=%async_computation.2 | async-start | bytes 1835008 | tf_op jit(solution)/shard_map/all_to_all | solution.py:451
  147.5 4.2 %collective-permute-done.7.refs_3_ = bf16[112,3584]{1,0:T(8,128)(2,1)} collective-permute-done((bf16[112,3584]{1,0:T(8,128)(2,1)}, bf16[112,3584]{1,0:T(8,128)(2,1)}, u32[]{:S(2)}, u32[]{:S(2)}) %collective-permute-start.7) | collective-permute-done | bytes 802848 | tf_op jit(solution)/shard_map/ppermute | solution.py:28
  151.7 18.2 %collective-permute-done.8.refs_4_ = bf16[112,3584]{1,0:T(8,128)(2,1)} collective-permute-done((bf16[112,3584]{1,0:T(8,128)(2,1)}, bf16[112,3584]{1,0:T(8,128)(2,1)}, u32[]{:S(2)}, u32[]{:S(2)}) %collective-permute-start.8) | collective-permute-done | bytes 802848 | tf_op jit(solution)/shard_map/ppermute | solution.py:28
  169.9 3.6 %shard_map.120 = (bf16[1,1024,3584]{2,1,0:T(8,128)(2,1)}, f32[8,128]{1,0:T(8,128)}) custom-call(s32[4]{0:T(128)} %dynamic_slice.17.refs_1_.refs_0_, s32[1]{0:T(128)} %bitcast.7.refs_0_.refs_1_, bf16[2,112,3584]{2,1,0:T(8,128)(2,1)} %copy-done.1, bf16[112,3584]{1,0:T(8,128)(2,1)} %collective-permute-done.7.refs_3_, ...), custom_call_target="tpu_custom_call", output_to_operand_aliasing={{0}: (6, {})} | custom-call | flops 1000 | bytes 1000 | tf_op jit(solution)/shard_map/pallas_call | solution.py:42
  174.7 2.3 %shard_map.121 = (bf16[1,1024,3584]{2,1,0:T(8,128)(2,1)}, f32[8,128]{1,0:T(8,128)}) custom-call(bf16[256,3584]{1,0:T(8,128)(2,1)} %copy-done.3, bf16[1,1024,3584]{2,1,0:T(8,128)(2,1)} %get-tuple-element.46.refs_1_, f32[8,128]{1,0:T(8,128)} %get-tuple-element.47.refs_2_), custom_call_target="tpu_custom_call", output_to_operand_aliasing={{0}: (1, {})} | custom-call | flops 1000 | bytes 1000 | tf_op jit(solution)/shard_map/pallas_call | solution.py:42
  (87 shorter events, 23.4 us)
Async XLA Ops:
  7.2 30.5 %all-to-all-start = ((bf16[32,24,1024]{2,1,0:T(8,128)(2,1)}), bf16[32,24,1024]{2,1,0:T(8,128)(2,1)S(1)}, u32[]{:S(2)}, u32[]{:S(2)}) async-start(bf16[32,24,1024]{2,1,0:T(8,128)(2,1)} %bitcast.4), calls=%async_computation | async-start | bytes 3145728 | tf_op jit(solution)/shard_map/all_to_all | solution.py:417
  14.6 6.4 %copy-start.9 = (s32[32]{0:T(128)S(1)}, s32[32]{0:T(128)}, u32[]{:S(2)}) copy-start(s32[32]{0:T(128)} %param.14) | copy-start | bytes 388
  17.6 43.2 %collective-permute-start = (bf16[2,80,3584]{2,1,0:T(8,128)(2,1)}, bf16[2,80,3584]{2,1,0:T(8,128)(2,1)S(1)}, u32[]{:S(2)}, u32[]{:S(2)}) collective-permute-start(bf16[2,80,3584]{2,1,0:T(8,128)(2,1)} %get-tuple-element.26), channel_id=1, source_target_pairs={{0,16},{16,0},{1,17},{17,1},{2,18},{18,2},{3,19},{19,3},{4,20},{20... | collective-permute-start | bytes 3440648 | tf_op jit(solution)/shard_map/ppermute | solution.py:28
  26.9 34.0 %collective-permute-start.1 = (bf16[1,3584]{1,0:T(2,128)(2,1)}, bf16[1,3584]{1,0:T(2,128)(2,1)S(1)}, u32[]{:S(2)}, u32[]{:S(2)}) collective-permute-start(bf16[1,3584]{1,0:T(2,128)(2,1)} %get-tuple-element.30), channel_id=1, source_target_pairs={{0,16},{16,0},{1,17},{17,1},{2,18},{18,2},{3,19},{19,3},{4,20},{20... | collective-permute-start | bytes 21512 | tf_op jit(solution)/shard_map/ppermute | solution.py:28
  37.7 1.1 copy-start
  60.8 0.6 copy-start.7
  60.8 1.0 copy-start.2
  65.2 71.9 %all-to-all-start.1 = ((bf16[8,80,3584]{2,1,0:T(8,128)(2,1)}), bf16[8,80,3584]{2,1,0:T(8,128)(2,1)}, u32[]{:S(2)}, u32[]{:S(2)}) async-start(bf16[8,80,3584]{2,1,0:T(8,128)(2,1)} %bitcast.57), calls=%async_computation.1 | async-start | bytes 9175040 | tf_op jit(solution)/shard_map/all_to_all | solution.py:439
  69.8 55.7 %collective-permute-start.6 = (bf16[2,112,3584]{2,1,0:T(8,128)(2,1)}, bf16[2,112,3584]{2,1,0:T(8,128)(2,1)S(1)}, u32[]{:S(2)}, u32[]{:S(2)}) collective-permute-start(bf16[2,112,3584]{2,1,0:T(8,128)(2,1)} %get-tuple-element.39), channel_id=1, source_target_pairs={{0,16},{16,0},{1,17},{17,1},{2,18},{18,2},{3,19},{19,3},{4,20},{20... | collective-permute-start | bytes 4816904 | tf_op jit(solution)/shard_map/ppermute | solution.py:28
  86.7 17.5 %collective-permute-start.2 = (bf16[80,3584]{1,0:T(8,128)(2,1)}, bf16[80,3584]{1,0:T(8,128)(2,1)S(1)}, u32[]{:S(2)}, u32[]{:S(2)}) collective-permute-start(bf16[80,3584]{1,0:T(8,128)(2,1)} %get-tuple-element.31), channel_id=1, source_target_pairs={{0,32},{32,64},{64,96},{96,0},{1,33},{33,65},{65,97},{97,1},{2,34}... | collective-permute-start | bytes 1720328 | tf_op jit(solution)/shard_map/ppermute | solution.py:28
  88.5 29.2 %collective-permute-start.3 = (bf16[80,3584]{1,0:T(8,128)(2,1)}, bf16[80,3584]{1,0:T(8,128)(2,1)S(1)}, u32[]{:S(2)}, u32[]{:S(2)}) collective-permute-start(bf16[80,3584]{1,0:T(8,128)(2,1)} %get-tuple-element.32), channel_id=1, source_target_pairs={{0,64},{32,96},{64,0},{96,32},{1,65},{33,97},{65,1},{97,33},{2,66}... | collective-permute-start | bytes 1720328 | tf_op jit(solution)/shard_map/ppermute | solution.py:28
  92.3 25.4 %collective-permute-start.4 = (bf16[80,3584]{1,0:T(8,128)(2,1)}, bf16[80,3584]{1,0:T(8,128)(2,1)S(1)}, u32[]{:S(2)}, u32[]{:S(2)}) collective-permute-start(bf16[80,3584]{1,0:T(8,128)(2,1)} %get-tuple-element.33), channel_id=1, source_target_pairs={{0,96},{32,0},{64,32},{96,64},{1,97},{33,1},{65,33},{97,65},{2,98}... | collective-permute-start | bytes 1720328 | tf_op jit(solution)/shard_map/ppermute | solution.py:28
  104.2 13.5 %copy-start.4 = (bf16[80,3584]{1,0:T(8,128)(2,1)}, bf16[80,3584]{1,0:T(8,128)(2,1)S(1)}, u32[]{:S(2)}) copy-start(bf16[80,3584]{1,0:T(8,128)(2,1)S(1)} %collective-permute-done.2.refs_3_) | copy-start | bytes 1720324
  117.7 0.9 copy-start.5
  117.7 1.0 copy-start.6
  124.9 48.5 %collective-permute-start.5 = (bf16[256,3584]{1,0:T(8,128)(2,1)}, bf16[256,3584]{1,0:T(8,128)(2,1)S(1)}, u32[]{:S(2)}, u32[]{:S(2)}) collective-permute-start(bf16[256,3584]{1,0:T(8,128)(2,1)} %get-tuple-element.38), channel_id=1, source_target_pairs={{0,16},{16,0},{1,17},{17,1},{2,18},{18,2},{3,19},{19,3},{4,20},{20... | collective-permute-start | bytes 5505032 | tf_op jit(solution)/shard_map/ppermute | solution.py:28
  125.5 1.2 copy-start.1
  131.3 20.4 %collective-permute-start.7 = (bf16[112,3584]{1,0:T(8,128)(2,1)}, bf16[112,3584]{1,0:T(8,128)(2,1)}, u32[]{:S(2)}, u32[]{:S(2)}) collective-permute-start(bf16[112,3584]{1,0:T(8,128)(2,1)} %get-tuple-element.41), channel_id=1, source_target_pairs={{0,32},{32,64},{64,96},{96,0},{1,33},{33,65},{65,97},{97,1},{2,34}... | collective-permute-start | bytes 2408456 | tf_op jit(solution)/shard_map/ppermute | solution.py:28
  132.2 37.7 %collective-permute-start.8 = (bf16[112,3584]{1,0:T(8,128)(2,1)}, bf16[112,3584]{1,0:T(8,128)(2,1)}, u32[]{:S(2)}, u32[]{:S(2)}) collective-permute-start(bf16[112,3584]{1,0:T(8,128)(2,1)} %get-tuple-element.42), channel_id=1, source_target_pairs={{0,64},{32,96},{64,0},{96,32},{1,65},{33,97},{65,1},{97,33},{2,66}... | collective-permute-start | bytes 2408456 | tf_op jit(solution)/shard_map/ppermute | solution.py:28
  134.1 35.7 %collective-permute-start.9 = (bf16[112,3584]{1,0:T(8,128)(2,1)}, bf16[112,3584]{1,0:T(8,128)(2,1)}, u32[]{:S(2)}, u32[]{:S(2)}) collective-permute-start(bf16[112,3584]{1,0:T(8,128)(2,1)} %get-tuple-element.43), channel_id=1, source_target_pairs={{0,96},{32,0},{64,32},{96,64},{1,97},{33,1},{65,33},{97,65},{2,98}... | collective-permute-start | bytes 2408456 | tf_op jit(solution)/shard_map/ppermute | solution.py:28
  142.5 35.5 %all-to-all-start.2 = ((bf16[4,32,3584]{2,1,0:T(8,128)(2,1)}), bf16[4,32,3584]{2,1,0:T(8,128)(2,1)S(1)}, u32[]{:S(2)}, u32[]{:S(2)}) async-start(bf16[4,32,3584]{2,1,0:T(8,128)(2,1)} %bitcast.60), calls=%async_computation.2 | async-start | bytes 1835008 | tf_op jit(solution)/shard_map/all_to_all | solution.py:451
  173.4 1.3 copy-start.3
  174.7 4.1 %copy-start.8 = (bf16[1,3584]{1,0:T(2,128)(2,1)S(1)}, bf16[1,3584]{1,0:T(2,128)(2,1)}, u32[]{:S(2)}) copy-start(bf16[1,3584]{1,0:T(2,128)(2,1)} %copy-done.7) | copy-start | bytes 21508

commit v3 on v2

--- a/solution.py
+++ b/solution.py
@@ -13,12 +13,14 @@
 N_X, N_Y, N_C = 4, 4, 2
 N_YC = N_Y * N_C
 N_EP = N_X * N_YC
-BLOCK = 24
-TRADED = (80, 112)
+BLOCK = 16
+TRADED = (64, 128)
 COLUMNS = 512
 VMEM_LIMIT = 60 << 20
+AHEAD = 3
 CHEAP = pl.CostEstimate(flops=1000, bytes_accessed=1000, transcendentals=0)
 HBM = pl.BlockSpec(memory_space=pltpu.HBM)
+ANY = pl.BlockSpec(memory_space=pl.ANY)
 SMEM = pl.BlockSpec(memory_space=pltpu.SMEM)
 WHOLE = pl.BlockSpec(memory_space=pltpu.VMEM)
 
@@ -31,7 +33,7 @@
 TOKEN = jax.ShapeDtypeStruct((8, 128), jnp.float32)
 
 
-def ordered_call(kernel, operands, after, out_shape, out_specs, scratch, in_specs=None, aliases=None):
+def ordered_call(kernel, operands, after, out_shape, out_specs, scratch, in_specs=None, aliases=None, limit=60):
     after = [t for t in after if t is not None]
     in_specs = in_specs or [HBM] * len(operands)
 
@@ -46,7 +48,7 @@
         out_specs=list(out_specs) + [HBM],
         scratch_shapes=scratch,
         input_output_aliases=aliases or {},
-        compiler_params=pltpu.CompilerParams(vmem_limit_bytes=VMEM_LIMIT),
+        compiler_params=pltpu.CompilerParams(vmem_limit_bytes=limit << 20),
         cost_estimate=CHEAP,
     )(*operands, *after)
     return outs, token
@@ -88,9 +90,7 @@
     )
 
 
-def last_kernel(partner, weight, *refs):
-    *refs, held, reads, writes = refs
-    out = refs[(len(refs) - 1) // 2]
+def last_kernel(partner, weight, out, held, reads, writes):
     rows = held.shape[1]
     first = weight.shape[1] - out.shape[0]
     moves = []
@@ -100,49 +100,61 @@
     through(moves, reads, writes)
 
 
-def last_rows(partner, weight, count, after, passed):
+def last_rows(partner, weight, count, after):
     shape = (count, weight.shape[2])
-    return ordered_call(
+    (rows,), token = ordered_call(
         last_kernel,
-        [partner, weight, *passed],
-        after,
-        [jax.ShapeDtypeStruct(shape, weight.dtype)]
-        + [jax.ShapeDtypeStruct(p.shape, p.dtype) for p in passed],
-        [HBM] * (1 + len(passed)),
+        [partner, weight],
+        after,
+        [jax.ShapeDtypeStruct(shape, weight.dtype)],
+        [HBM],
         [pltpu.VMEM((4, count // 4, shape[1]), weight.dtype)]
         + [pltpu.SemaphoreType.DMA((4,))] * 2,
-        in_specs=[SMEM, HBM] + [HBM] * len(passed),
-        aliases={2 + i: 1 + i for i in range(len(passed))},
-    )
-
-
-def pick_kernel(others, picks, block, *refs):
-    *refs, held, reads, writes = refs
-    passed = (len(refs) - others) // 2
-    outs = refs[passed : passed + others]
+        in_specs=[SMEM, HBM],
+    )
+    return rows, token
+
+
+def pick_kernel(picks, block, *refs):
+    *outs, held, reads, writes = refs
     through([(block.at[picks[i + 1]], held.at[i], o) for i, o in enumerate(outs)], reads, writes)
 
 
-def pick(picks, block, parts, after, passed=()):
+def pick(picks, block, parts, after):
     others = parts - 1
-    operands = [picks, block, *passed]
     return ordered_call(
-        functools.partial(pick_kernel, others),
-        operands,
-        after,
-        [jax.ShapeDtypeStruct(block.shape[1:], block.dtype)] * others
-        + [jax.ShapeDtypeStruct(p.shape, p.dtype) for p in passed],
-        [HBM] * (others + len(passed)),
+        pick_kernel,
+        [picks, block],
+        after,
+        [jax.ShapeDtypeStruct(block.shape[1:], block.dtype)] * others,
+        [HBM] * others,
         [pltpu.VMEM((others,) + block.shape[1:], block.dtype)]
         + [pltpu.SemaphoreType.DMA((others,))] * 2,
-        in_specs=[SMEM] + [HBM] * (1 + len(passed)),
-        aliases={2 + i: others + i for i in range(len(passed))},
-    )
+        in_specs=[SMEM, ANY],
+        limit=12,
+    )
+
+
+def gate_kernel(*_):
+    pass
+
+
+def gated(passed, after):
+    (passed,), _ = ordered_call(
+        gate_kernel,
+        [passed],
+        after,
+        [jax.ShapeDtypeStruct(passed.shape, passed.dtype)],
+        [HBM],
+        [],
+        aliases={0: 0},
+    )
+    return passed
 
 
 def place_kernel(at, quarter, parts, picks, part, block, *refs):
-    *refs, held, reads, writes = refs
-    arrived, out = refs[: parts - 1], refs[-1]
+    *refs, out, held, reads, writes = refs
+    arrived = refs[: parts - 1]
     rows = arrived[0].shape[0]
     moves = []
     for i, source in enumerate([block.at[picks[0]], *arrived]):
@@ -165,40 +177,50 @@
         [HBM],
         [pltpu.VMEM((parts, rows, width), block.dtype)]
         + [pltpu.SemaphoreType.DMA((parts,))] * 2,
-        in_specs=[SMEM, SMEM] + [HBM] * (len(operands) - 2),
+        in_specs=[SMEM, SMEM] + [ANY] * parts + [HBM] * chained,
         aliases={len(operands) - 1: 0} if chained else {},
+        limit=12,
     )
     return whole, token
 
 
-def direct_kernel(block, _, out, held, reads, writes):
-    rows = block.shape[0] // 4
-    through(
+def finish_kernel(at, quarter, parts, picks, part, block, *refs):
+    arrived, (straight, _, out, held, rest, reads, writes) = refs[: parts - 1], refs[parts - 1 :]
+    rows = arrived[0].shape[0]
+    moves = []
+    share = rest.shape[1]
+    for i in range(parts):
+        first = out.shape[1] - (parts - i) * share
+        moves.append(
+            (straight.at[pl.ds(i * share, share)], rest.at[i], out.at[0, pl.ds(first, share)])
+        )
+    for i, source in enumerate([block.at[picks[0]], *arrived]):
+        origin = lax.rem(part[0] - i + parts, parts)
+        start = pl.multiple_of(origin * quarter + at, 16)
+        moves.append((source, held.at[i], out.at[0, pl.ds(start, rows)]))
+    through(moves, reads, writes)
+
+
+def finished(picks, part, block, arrived, straight, at, quarter, whole, after):
+    parts = len(arrived) + 1
+    rows, width = arrived[0].shape
+    operands = [picks, part, block, *arrived, straight, whole]
+    (whole,), _ = ordered_call(
+        functools.partial(finish_kernel, at, quarter, parts),
+        operands,
+        after,
+        [jax.ShapeDtypeStruct(whole.shape, block.dtype)],
+        [HBM],
         [
-            (
-                block.at[pl.ds(i * rows, rows)],
-                held.at[i],
-                out.at[0, pl.ds(out.shape[1] - (4 - i) * rows, rows)],
-            )
-            for i in range(4)
-        ],
-        reads,
-        writes,
-    )
-
-
-def placed_direct(block, whole, after):
-    (whole,), token = ordered_call(
-        direct_kernel,
-        [block, whole],
-        after,
-        [jax.ShapeDtypeStruct(whole.shape, whole.dtype)],
-        [HBM],
-        [pltpu.VMEM((4, block.shape[0] // 4, block.shape[1]), block.dtype)]
-        + [pltpu.SemaphoreType.DMA((4,))] * 2,
-        aliases={1: 0},
-    )
-    return whole, token
+            pltpu.VMEM((parts, rows, width), block.dtype),
+            pltpu.VMEM((parts, straight.shape[0] // parts, width), block.dtype),
+        ]
+        + [pltpu.SemaphoreType.DMA((2 * parts,))] * 2,
+        in_specs=[SMEM, SMEM] + [ANY] * (parts + 1) + [HBM],
+        aliases={len(operands) - 1: 0},
+        limit=16,
+    )
+    return whole
 
 
 def rank_of(expert_list):
@@ -208,27 +230,32 @@
     return jnp.sum(same & (order[:, None] > order[None, :]), axis=-1, dtype=jnp.int32)
 
 
-def one_hot_rows(sources, count):
-    table = np.zeros((len(sources), count), np.float32)
+STACK = N_X * 20
+
+
+def one_hot_rows(sources):
+    table = np.zeros((len(sources), N_EP * (BLOCK + 8)), np.float32)
     table[np.arange(len(sources)), sources] = 1.0
     return table
 
 
-STACK = N_X * 20
-
-
 def return_order():
-    rows, names = [], []
-    for yc in range(N_YC):
-        bases = [(x * N_YC + yc) * BLOCK for x in range(N_X)]
-        for base in bases:
-            rows += [base + r for r in range(8)]
-            names += [base + 15] * 8
-        for base in bases:
-            for at in (base + 8, base + 16):
-                rows += [at + r for r in range(6)]
-                names += [at + 7] * 6
-    return one_hot_rows(rows, N_EP * BLOCK), one_hot_rows(names, N_EP * BLOCK)
+    orders, namings = [], []
+    for core in range(N_C):
+        rows, names = [], []
+        for yc in range(N_YC):
+            clients = [x * N_YC + yc for x in range(N_X)]
+            for client in clients:
+                rows += [client * BLOCK + r for r in range(8)]
+                names += [client * BLOCK + 15] * 8
+            for client in clients:
+                for step in range(2):
+                    at = client * BLOCK + 8 if step == core else N_EP * BLOCK + client * 8
+                    rows += [at + r for r in range(6)]
+                    names += [at + 7] * 6
+        orders.append(one_hot_rows(rows))
+        namings.append(one_hot_rows(names))
+    return np.stack([np.stack(orders), np.stack(namings)], 1)
 
 
 def scale_kernel(partner, scale, out):
@@ -250,11 +277,12 @@
     return chosen, token
 
 
-def serve_kernel(me, received, order, naming, weight, scale, *refs):
-    out, _, spread, held, product, reads, writes = refs[-7:]
-    depth = received.shape[1]
+def serve_kernel(me, received, far, order, weight, scale, *refs):
+    out, _, table, spread, held, product, table_read, reads, writes = refs[-9:]
+    near, depth = received.shape
     tiles = held.shape[0]
     columns = [pl.ds(i * COLUMNS, COLUMNS) for i in range(tiles)]
+    table_reading = pltpu.make_async_copy(order.at[me[1]], table, table_read)
     reading = [
         pltpu.make_async_copy(weight.at[:, :, columns[i]], held.at[i], reads.at[i])
         for i in range(tiles)
@@ -263,10 +291,17 @@
         pltpu.make_async_copy(product.at[i], out.at[:, columns[i]], writes.at[i])
         for i in range(tiles)
     ]
-    for copy in reading:
+    table_reading.start()
+    table_reading.wait()
+    for copy in reading[:AHEAD]:
         copy.start()
-    ordered = jnp.dot(order[...], received[...], preferred_element_type=jnp.float32)
-    named = jnp.dot(naming[...], received[:, :128], preferred_element_type=jnp.float32)
+
+    def gather(which, first, second):
+        rows = jnp.dot(table[which, :, :near], first, preferred_element_type=jnp.float32)
+        return rows + jnp.dot(table[which, :, near:], second, preferred_element_type=jnp.float32)
+
+    ordered = gather(0, received[...], far[...])
+    named = gather(1, received[:, :128], far[:, :128])
     row = lax.broadcasted_iota(jnp.int32, named.shape, 0)
     lane = jnp.where(
         row % STACK < N_X * 8,
@@ -277,6 +312,8 @@
     spread[:, depth:] = jnp.where(lane == 1.0, ordered, 0.0).astype(jnp.bfloat16)
     for i in range(tiles):
         reading[i].wait()
+        if i + AHEAD < tiles:
+            reading[i + AHEAD].start()
         both = held[i].reshape(2 * depth, COLUMNS)
         scales = scale[:, i * COLUMNS : (i + 1) * COLUMNS].astype(jnp.float32)
         total = jnp.dot(spread[...], both, preferred_element_type=jnp.float32)
@@ -287,51 +324,85 @@
         copy.wait()
 
 
-def serve(me, received, weight, scale, after):
-    order, naming = (jnp.asarray(table, jnp.bfloat16) for table in return_order())
-    rows = order.shape[0]
+def serve(me, received, far, weight, scale, after):
+    order = jnp.asarray(return_order(), jnp.bfloat16)
+    rows = order.shape[2]
     _, depth, width = weight.shape
     tiles = width // COLUMNS
     return pl.pallas_call(
         serve_kernel,
-        in_specs=[SMEM, WHOLE, WHOLE, WHOLE, HBM, WHOLE] + [HBM] * len(after),
+        in_specs=[SMEM, WHOLE, WHOLE, HBM, HBM, WHOLE] + [HBM] * len(after),
         out_specs=[HBM, HBM],
         scratch_shapes=[
+            pltpu.VMEM(order.shape[1:], jnp.bfloat16),
             pltpu.VMEM((rows, 2 * depth), jnp.bfloat16),
             pltpu.VMEM((tiles, 2, depth, COLUMNS), jnp.bfloat16),
             pltpu.VMEM((tiles, rows, COLUMNS), jnp.bfloat16),
+            pltpu.SemaphoreType.DMA,
             pltpu.SemaphoreType.DMA((tiles,)),
             pltpu.SemaphoreType.DMA((tiles,)),
         ],
         out_shape=[jax.ShapeDtypeStruct((rows, width), jnp.bfloat16), TOKEN],
         compiler_params=pltpu.CompilerParams(vmem_limit_bytes=VMEM_LIMIT),
         cost_estimate=CHEAP,
-    )(me, received, order, naming, weight, scale, *after)
-
-
-def mixing(told, my_x, steps, rows, top):
-    items = rows * top
-    told = told.astype(jnp.float32).reshape(N_X, 4, steps, items)
-    ids = told[:, 0].astype(jnp.int32)
-    gates = told[:, 1] + told[:, 2] + told[:, 3]
-    rank = rank_of(ids)
-    who = jnp.arange(N_X * steps, dtype=jnp.int32).reshape(N_X, steps, 1) * 256
-    code = jnp.where(rank < 2, ids * 2 + rank, 128 + rank - 2) + who
-    source = jnp.arange(N_YC, dtype=jnp.int32)[:, None]
-    row = jnp.arange(N_X * 8, dtype=jnp.int32)[None, :]
-    slot_code = ((N_YC * my_x + source) * 2 + (row % 8) // 4) * 2 + row % 2
-    slot_code = slot_code + ((row // 8) * steps + (row % 4) // 2) * 256
-    row = jnp.arange(N_X * 12, dtype=jnp.int32)[None, :]
-    hot_code = 128 + row % 6 + ((row // 12) * steps + (row % 12) // 6) * 256
-    hot_code = jnp.broadcast_to(hot_code, (N_YC, N_X * 12))
-    column_code = jnp.concatenate([slot_code, hot_code], 1).reshape(-1)
-    code = code.reshape(N_X * steps * rows, top)
-    gates = gates.reshape(N_X * steps * rows, top)
-    mix = jnp.sum(
-        jnp.where(code[:, :, None] == column_code[None, None, :], gates[:, :, None], 0.0), axis=1
-    )
-    high = lax.reduce_precision(mix, 8, 7)
-    return jnp.concatenate([high, mix - high], 0).astype(jnp.bfloat16)
+    )(me, received, far, order, weight, scale, *after)
+
+
+def column_codes():
+    codes, slots = [], []
+    for source in range(N_YC):
+        for x in range(N_X):
+            for r in range(8):
+                slot = (source * 2 + r // 4) * 2 + r % 2
+                codes.append((x * 2 + r % 4 // 2) * 256 + slot)
+                slots.append(1)
+        for x in range(N_X):
+            for r in range(12):
+                codes.append((x * 2 + r // 6) * 256 + 128 + r % 6)
+                slots.append(0)
+    return np.array([codes], np.float32), np.array([slots], np.float32)
+
+
+def mixing_kernel(told, columns, out):
+    count = told.shape[2]
+    tokens = out.shape[0] // 2 // (N_X * 2)
+    row = lax.broadcasted_iota(jnp.int32, (count, count), 0)
+    line = lax.broadcasted_iota(jnp.int32, (count, count), 1)
+    token = lax.broadcasted_iota(jnp.int32, (tokens, count), 0)
+    item = lax.broadcasted_iota(jnp.int32, (tokens, count), 1)
+    mine = item // (count // tokens) == token
+    for x in range(N_X):
+        for step in range(2):
+            ids = told[x, step : step + 1, :]
+            down = jnp.sum(jnp.where(row == line, ids, 0.0), axis=1, keepdims=True)
+            before = jnp.where((down == ids) & (line < row), 1.0, 0.0)
+            rank = jnp.sum(before, axis=1, keepdims=True)
+            code = jnp.where(rank < 2.0, down * 2.0 + rank, 126.0 + rank)
+            code = code + float((x * 2 + step) * 256)
+            slot = jnp.where(code == columns[...], 1.0, 0.0).astype(jnp.bfloat16)
+            high = told[x, 2 + step : 3 + step, :]
+            rest = told[x, 4 + step : 5 + step, :] + told[x, 6 + step : 7 + step, :]
+            at = (x * 2 + step) * tokens
+            for first, part in ((0, high), (out.shape[0] // 2, rest)):
+                gate = jnp.where(mine, part, 0.0).astype(jnp.bfloat16)
+                mix = jnp.dot(gate, slot, preferred_element_type=jnp.float32)
+                out[first + at : first + at + tokens] = mix.astype(jnp.bfloat16)
+
+
+def mixing(told, my_x, steps, rows, after):
+    codes, slots = column_codes()
+    columns = jnp.asarray(codes) + jnp.asarray(slots) * (my_x * N_YC * 4).astype(jnp.float32)
+    told = told.astype(jnp.float32).reshape(N_X, 4 * steps, -1)
+    (mixes,), token = ordered_call(
+        mixing_kernel,
+        [told, columns],
+        after,
+        [jax.ShapeDtypeStruct((2 * N_X * steps * rows, codes.shape[1]), jnp.bfloat16)],
+        [WHOLE],
+        [],
+        in_specs=[WHOLE, WHOLE],
+    )
+    return mixes, token
 
 
 def mix_kernel(mixes, returned, out, held, product, reads, writes):
@@ -390,9 +461,11 @@
         (expert_list // 2) * BLOCK + (expert_list % 2) * 4 + step_of * 2 + rank,
         1000 + step_of * 8 + rank - 2,
     ).reshape(steps * items)
-    place = jnp.concatenate([place, jnp.array([1006, 1007, 1015, -1, -1, -1, -1, -1], jnp.int32)])
+    extra = jnp.array([2006, 1007, 1015, -1, -1, -1, -1, -1], jnp.int32)
+    place = jnp.concatenate([place, extra])
     line = jnp.arange(N_EP * BLOCK, dtype=jnp.int32)
-    line = jnp.where(line % BLOCK < 8, line, 1000 + line % BLOCK - 8)
+    of_step = (line // BLOCK) % N_C * 8 + line % 8
+    line = jnp.where(line % BLOCK < 8, line, jnp.where(line % 8 == 6, 2006, 1000 + of_step))
     selector = (line[:, None] == place[None, :]).astype(jnp.bfloat16)
     hot_id = jnp.sum(jnp.where(rank == 7, expert_list, 0), axis=1).astype(jnp.float32)
     flat_gates = gates.reshape(steps * items)
@@ -410,43 +483,43 @@
     starts = [sum(TRADED[:i]) for i in range(len(TRADED))]
     ranges = list(zip(starts, TRADED))
     partner = lax.dynamic_slice(replica_map, ((me + N_EP // 2) % N_EP,), (1,)) % 2
-    blocks, token = cut(here, expert_weight, ranges, quarter, [])
-    crossed = [shifted(block, "xh", 1) for block in blocks]
-
     outgoing = jnp.dot(selector, hidden, preferred_element_type=jnp.float32).astype(jnp.bfloat16)
     received = lax.all_to_all(outgoing.reshape(N_EP, BLOCK, depth), EP, 0, 0, tiled=True)
     mine = lax.dynamic_slice(replica_map, (me,), (1,)) % 2
     picks = lax.psum(jnp.where(jnp.arange(parts) == part, mine, 0), "dp")
     picks = jnp.roll(picks, -part)
-    scale, _ = chosen_scale(partner, column_scale, [])
+    scale, token = chosen_scale(partner, column_scale, [picks])
+    blocks, token = cut(here, expert_weight, ranges, quarter, [picks, token])
     replica_scale = shifted(scale, "xh", 1)
 
-    def traded(j, after, passed=()):
-        (*sent, last), token = pick(picks, crossed[j], parts, after, passed)
-        if not passed:
-            sent, last = sent + [last], None
-        return [shifted(piece, "dp", d + 1) for d, piece in enumerate(sent)], last, token
-
-    def put(j, pieces, whole, after):
-        return placed(picks, here, crossed[j], pieces, starts[j], quarter, depth, whole, after)
-
+    def traded(j, after):
+        sent, token = pick(picks, crossed[j], parts, after)
+        return [shifted(piece, "dp", d + 1) for d, piece in enumerate(sent)], token
+
+    far = shifted(received[:, 8:].reshape(N_EP * 8, depth), "c", 1)
     received = received.reshape(N_EP * BLOCK, depth)
-    where = me.reshape(1).astype(jnp.int32)
-    returned, token = serve(where, received, expert_weight, column_scale, [token, picks])
+    blocks[0] = gated(blocks[0], [received])
+    crossed = [shifted(block, "xh", 1) for block in blocks]
+    where = jnp.stack([me, lax.axis_index("c")]).astype(jnp.int32)
+    returned, token = serve(where, received, far, expert_weight, column_scale, [token, picks])
     told = received.reshape(N_X, N_YC, BLOCK, depth)[:, :, 14]
     told = lax.dynamic_index_in_dim(told, my_yc, 1, keepdims=False)
-    first, returned, token = traded(0, [token, replica_scale], [returned])
+    returned = gated(returned, [crossed[0], replica_scale])
     returned = lax.all_to_all(returned.reshape(N_YC, -1, width), ("y", "c"), 0, 0, tiled=True)
-    whole, token = put(0, first, None, [token])
-    (direct, told), token = last_rows(
-        partner, expert_weight, depth - parts * quarter, [token], [told]
-    )
-    direct = shifted(direct, "xh", 1)
-    second, _, token = traded(1, [token])
-    whole, token = put(1, second, whole, [token])
-    replica_weight, token = placed_direct(direct, whole, [token])
-
-    mixes = mixing(told, my_x, steps, rows, top)
+    first, token = traded(0, [token])
+    mixes, token = mixing(told, my_x, steps, rows, [token])
+    straight, token = last_rows(
+        partner, expert_weight, depth - parts * quarter, [token, *first]
+    )
+    straight = shifted(straight, "xh", 1)
+    whole, token = placed(
+        picks, here, crossed[0], first, starts[0], quarter, depth, None, [token]
+    )
+    second, token = traded(1, [token])
+    replica_weight = finished(
+        picks, here, crossed[1], second, straight, starts[1], quarter, whole, [token]
+    )
+
     partial = mixed(mixes, returned.reshape(-1, width))
     partial = lax.all_to_all(partial.reshape(N_X, steps * rows, width), X, 0, 0, tiled=True)
     combined = jnp.sum(partial.astype(jnp.float32), axis=0).astype(jnp.bfloat16)

time: 180 us -> 162 us (0.900)
  starting transfers between devices: 48.7 us -> 33.1 us
    ppermute x10 -> x11, starting transfers between devices: 31.7 us -> 16.8 us  [shifted(): lax.ppermute(block, axis, [(i, (i + distance) % count) for i in range(cou...]
    ppermute x10 -> x11, waiting for transfers between devices: 51.4 us -> 49.4 us  [shifted(): lax.ppermute(block, axis, [(i, (i + distance) % count) for i in range(cou...]
    unnamed x24 -> x35, local copies, waits for them, and re-layouts: 8.37 us -> 7.18 us
    pallas_call x8 -> x10, Pallas kernels: 22.9 us -> 22.2 us  [ordered_call(): pl.pallas_call(body, out_shape=list(out_shape) + [TOKEN], in_specs=list(i...]
  transfers between devices with their start and end apart: 13 -> 14, of which waited for: 7 -> 7; matrix products, arithmetic and copies ran while one was open for 4% -> 3% of each run, Pallas kernels for 22% -> 27%
where the time goes in v3:
time: 162 us; the launch traced here: 161 us
  waiting for transfers between devices  50.7 us (31%)
  Pallas kernels  43.9 us (27%)
  starting transfers between devices  33.1 us (20%)
  local copies, waits for them, and re-layouts  11.1 us (7%)
  blocking collectives  9.76 us (6%)
  other arithmetic  5.02 us (3%)
  between operations  4.89 us (3%)
  matrix products  2.9 us (2%)
    ppermute x11, waiting for transfers between devices, shifted(): lax.ppermute(block, axis, [(i, (i + distance) % count) for i in range(cou...  49.4 us
    pallas_call x10, Pallas kernels, ordered_call(): pl.pallas_call(body, out_shape=list(out_shape) + [TOKEN], in_specs=list(i...  22.2 us
    ppermute x11, starting transfers between devices, shifted(): lax.ppermute(block, axis, [(i, (i + distance) % count) for i in range(cou...  16.8 us
    pallas_call x1, Pallas kernels, serve(): pl.pallas_call(serve_kernel, in_specs=[SMEM, WHOLE, WHOLE, HBM, HBM, WHOL...  16.2 us
    psum x1, blocking collectives, local(): picks = lax.psum(jnp.where(jnp.arange(parts) == part, mine, 0), 'dp')  9.76 us
    all_to_all x1, starting transfers between devices, local(): lax.all_to_all(outgoing.reshape(N_EP, BLOCK, depth), EP, 0, 0, tiled=True)  7.4 us
    unnamed x35, local copies, waits for them, and re-layouts  7.18 us
    pallas_call x1, Pallas kernels, mixed(): pl.pallas_call(mix_kernel, in_specs=[WHOLE, HBM], out_specs=HBM, out_shap...  5.47 us
  transfers between devices with their start and end apart: 14, of which 7 were waited for; matrix products, arithmetic and copies ran while one was open for 3% of the time, Pallas kernels for 27%

profile of v3, /device:TPU:0, one launch (start us, length us, event | category | flops | bytes accessed | tf_op | source)
XLA Modules:
  0.0 161.3 jit_solution(5158644811817767539)
XLA Ops:
  3.9 2.9 %convolution_convert_fusion = bf16[512,1024]{1,0:T(8,128)(2,1)} fusion(bf16[1,1024]{1,0:T(2,128)(2,1)S(1)} %broadcast_in_dim.40, bf16[256,1024]{1,0:T(8,128)(2,1)} %bitcast.37, s32[264]{0:T(512)S(1)} %pad_add_fusion, s32[512]{0:T(512)S(1)} %iota_select_fusion, bf16[264]{0:T(512)(128)(2,1)S(1)} %pad.7.clone, bf16[264]{0:T(512)(128)(2,1)S(1)} %pad.6.clone), kind=kOutput, calls=%fused_computation | convolution fusion | flops 279646208 | bytes 1579072 | tf_op jit(solution)/shard_map/dot_general | solution.py:486
  6.8 7.4 %all-to-all-start = ((bf16[32,16,1024]{2,1,0:T(8,128)(2,1)}), bf16[32,16,1024]{2,1,0:T(8,128)(2,1)S(1)}, u32[]{:S(2)}, u32[]{:S(2)}) async-start(bf16[32,16,1024]{2,1,0:T(8,128)(2,1)} %bitcast.4), calls=%async_computation | async-start | bytes 2097152 | tf_op jit(solution)/shard_map/all_to_all | solution.py:487
  16.8 9.8 %psum.7 = s32[4]{0:T(128)S(1)} all-reduce(s32[4]{0:T(128)S(1)} %compare_select_fusion), channel_id=1, replica_groups=mesh['dp'=4,'xh'=2,'xl'=2,'y'=4,'c'=2] {'dp'}, use_global_device_ids=true, to_apply=%region_2.3 | all-reduce | flops 4 | bytes 32 | tf_op jit(solution)/shard_map/psum | solution.py:489
  29.2 1.3 shard_map.121
  30.5 3.0 %shard_map.122 = (bf16[2,64,3584]{2,1,0:T(8,128)(2,1)}, bf16[2,128,3584]{2,1,0:T(8,128)(2,1)}, f32[8,128]{1,0:T(8,128)}) custom-call(s32[1]{0:T(128)} %bitcast.8.refs_0_.refs_1_, bf16[2,1024,3584]{2,1,0:T(8,128)(2,1)} %refs_1_.5, s32[4]{0:T(128)} %dynamic_slice.16.refs_2_.refs_1_.refs_0_, f32[8,128]{1,0:T(8,128)} %get-tuple-element.27.refs_3_), custom_call_target="tpu_custom_call" | custom-call | flops 1000 | bytes 1000 | tf_op jit(solution)/shard_map/pallas_call | solution.py:44
  34.5 3.3 %collective-permute-start = (bf16[2,64,3584]{2,1,0:T(8,128)(2,1)}, bf16[2,64,3584]{2,1,0:T(8,128)(2,1)S(1)}, u32[]{:S(2)}, u32[]{:S(2)}) collective-permute-start(bf16[2,64,3584]{2,1,0:T(8,128)(2,1)} %get-tuple-element.29), channel_id=1, source_target_pairs={{0,16},{16,0},{1,17},{17,1},{2,18},{18,2},{3,19},{19,3},{4,20},{20... | collective-permute-start | bytes 2752520 | tf_op jit(solution)/shard_map/ppermute | solution.py:30
  41.7 16.2 %shard_map.124 = (bf16[640,3584]{1,0:T(8,128)(2,1)}, f32[8,128]{1,0:T(8,128)}) custom-call(s32[2]{0:T(128)} %pad_add_fusion.2.me, bf16[512,1024]{1,0:T(8,128)(2,1)} %bitcast.32, bf16[256,1024]{1,0:T(8,128)(2,1)} %copy-done.9, bf16[2,2,640,768]{3,2,1,0:T(8,128)(2,1)} %constant.185.clone.order, bf16[2,1024,3584]{2,1,0:T(8,128)(2,1)} %refs_1_.5, ...), custom_call_target="tpu_custom_call" | custom-call | flops 1000 | bytes 1000 | tf_op jit(solution)/shard_map/pallas_call | solution.py:332
  58.9 4.7 %all-to-all-start.1 = ((bf16[8,80,3584]{2,1,0:T(8,128)(2,1)}), bf16[8,80,3584]{2,1,0:T(8,128)(2,1)}, u32[]{:S(2)}, u32[]{:S(2)}) async-start(bf16[8,80,3584]{2,1,0:T(8,128)(2,1)} %bitcast.30), calls=%async_computation.1 | async-start | bytes 9175040 | tf_op jit(solution)/shard_map/all_to_all | solution.py:508
  63.6 3.0 %collective-permute-start.3 = (bf16[2,128,3584]{2,1,0:T(8,128)(2,1)}, bf16[2,128,3584]{2,1,0:T(8,128)(2,1)S(1)}, u32[]{:S(2)}, u32[]{:S(2)}) collective-permute-start(bf16[2,128,3584]{2,1,0:T(8,128)(2,1)} %get-tuple-element.37), channel_id=1, source_target_pairs={{0,16},{16,0},{1,17},{17,1},{2,18},{18,2},{3,19},{19,3},{4,20},{20... | collective-permute-start | bytes 5505032 | tf_op jit(solution)/shard_map/ppermute | solution.py:30
  66.6 2.5 %shard_map.125 = (bf16[64,3584]{1,0:T(8,128)(2,1)}, bf16[64,3584]{1,0:T(8,128)(2,1)}, bf16[64,3584]{1,0:T(8,128)(2,1)}, f32[8,128]{1,0:T(8,128)S(1)}) custom-call(s32[4]{0:T(128)S(1)} %copy-done.4, bf16[2,64,3584]{2,1,0:T(8,128)(2,1)S(1)} %copy-done.1, f32[8,128]{1,0:T(8,128)S(1)} %copy-done.5), custom_call_target="tpu_custom_call" | custom-call | flops 1000 | bytes 1000 | tf_op jit(solution)/shard_map/pallas_call | solution.py:44
  70.8 1.8 %collective-permute-start.5 = (bf16[64,3584]{1,0:T(8,128)(2,1)}, bf16[64,3584]{1,0:T(8,128)(2,1)}, u32[]{:S(2)}, u32[]{:S(2)}) collective-permute-start(bf16[64,3584]{1,0:T(8,128)(2,1)} %get-tuple-element.39), channel_id=1, source_target_pairs={{0,64},{32,96},{64,0},{96,32},{1,65},{33,97},{65,1},{97,33},{2,66}... | collective-permute-start | bytes 1376264 | tf_op jit(solution)/shard_map/ppermute | solution.py:30
  75.9 2.5 %shard_map.126 = (bf16[256,640]{1,0:T(8,128)(2,1)}, f32[8,128]{1,0:T(8,128)}) custom-call(f32[4,8,128]{2,1,0:T(8,128)} %bitcast.36, f32[1,640]{1,0:T(1,128)} %multiply_add_fusion.refs_1_, f32[8,128]{1,0:T(8,128)} %copy-done.7), custom_call_target="tpu_custom_call" | custom-call | flops 1000 | bytes 1000 | tf_op jit(solution)/shard_map/pallas_call | solution.py:44
  78.5 15.0 %collective-permute-done.4.refs_3_ = bf16[64,3584]{1,0:T(8,128)(2,1)S(1)} collective-permute-done((bf16[64,3584]{1,0:T(8,128)(2,1)}, bf16[64,3584]{1,0:T(8,128)(2,1)S(1)}, u32[]{:S(2)}, u32[]{:S(2)}) %collective-permute-start.4) | collective-permute-done | bytes 458784 | tf_op jit(solution)/shard_map/ppermute | solution.py:30
  94.2 2.4 %shard_map.129 = (bf16[256,3584]{1,0:T(8,128)(2,1)}, f32[8,128]{1,0:T(8,128)}) custom-call(s32[1]{0:T(128)S(6)} %select_n.135.refs_0_, bf16[2,1024,3584]{2,1,0:T(8,128)(2,1)} %refs_1_.5, f32[8,128]{1,0:T(8,128)} %get-tuple-element.41.refs_2_, bf16[64,3584]{1,0:T(8,128)(2,1)} %copy-done.2, bf16[64,3584]{1,0:T(8,128)(2,1)} %collective-permute-done.5.refs_4_, ...), custom_call_target="tpu_custom_call" | custom-call | flops 1000 | bytes 1000 | tf_op jit(solution)/shard_map/pallas_call | solution.py:44
  99.3 3.4 %shard_map.130 = (bf16[1,1024,3584]{2,1,0:T(8,128)(2,1)}, f32[8,128]{1,0:T(8,128)S(1)}) custom-call(s32[4]{0:T(128)S(1)} %copy-done.4, s32[1]{0:T(128)} %bitcast.8.refs_0_.refs_1_, bf16[2,64,3584]{2,1,0:T(8,128)(2,1)S(1)} %copy-done.1, bf16[64,3584]{1,0:T(8,128)(2,1)S(1)} %copy-done.3, bf16[64,3584]{1,0:T(8,128)(2,1)} %collective-permute-done.5.refs_4_, ...), custom_call_target="tpu_custom_call" | custom-call | flops 1000 | bytes 1000 | tf_op jit(solution)/shard_map/pallas_call | solution.py:44
  102.8 5.5 %collective-permute-done.3.refs_1_.refs_2_ = bf16[2,128,3584]{2,1,0:T(8,128)(2,1)S(1)} collective-permute-done((bf16[2,128,3584]{2,1,0:T(8,128)(2,1)}, bf16[2,128,3584]{2,1,0:T(8,128)(2,1)S(1)}, u32[]{:S(2)}, u32[]{:S(2)}) %collective-permute-start.3) | collective-permute-done | bytes 1835040 | tf_op jit(solution)/shard_map/ppermute | solution.py:30
  108.3 2.8 %shard_map.131 = (bf16[128,3584]{1,0:T(8,128)(2,1)}, bf16[128,3584]{1,0:T(8,128)(2,1)}, bf16[128,3584]{1,0:T(8,128)(2,1)}, f32[8,128]{1,0:T(8,128)S(1)}) custom-call(s32[4]{0:T(128)S(1)} %copy-done.4, bf16[2,128,3584]{2,1,0:T(8,128)(2,1)S(1)} %collective-permute-done.3.refs_1_.refs_2_, f32[8,128]{1,0:T(8,128)S(1)} %get-tuple-element.43.refs_2_), custom_call_target="tpu_custom_call" | custom-call | flops 1000 | bytes 1000 | tf_op jit(solution)/shard_map/pallas_call | solution.py:44
  112.1 3.2 %collective-permute-start.8 = (bf16[128,3584]{1,0:T(8,128)(2,1)}, bf16[128,3584]{1,0:T(8,128)(2,1)}, u32[]{:S(2)}, u32[]{:S(2)}) collective-permute-start(bf16[128,3584]{1,0:T(8,128)(2,1)} %get-tuple-element.45), channel_id=1, source_target_pairs={{0,64},{32,96},{64,0},{96,32},{1,65},{33,97},{65,1},{97,33},{2,66}... | collective-permute-start | bytes 2752520 | tf_op jit(solution)/shard_map/ppermute | solution.py:30
  117.5 5.5 %shard_map.128 = bf16[128,3584]{1,0:T(8,128)(2,1)} custom-call(bf16[256,640]{1,0:T(8,128)(2,1)} %get-tuple-element.33.mixes, bf16[640,3584]{1,0:T(8,128)(2,1)} %bitcast.14.returned), custom_call_target="tpu_custom_call" | custom-call | flops 1000 | bytes 1000 | tf_op jit(solution)/shard_map/pallas_call | solution.py:434
  123.0 4.2 %all-to-all-start.2 = ((bf16[4,32,3584]{2,1,0:T(8,128)(2,1)}), bf16[4,32,3584]{2,1,0:T(8,128)(2,1)}, u32[]{:S(2)}, u32[]{:S(2)}) async-start(bf16[4,32,3584]{2,1,0:T(8,128)(2,1)} %bitcast.34), calls=%async_computation.2 | async-start | bytes 1835008 | tf_op jit(solution)/shard_map/all_to_all | solution.py:524
  127.2 7.7 %collective-permute-done.7.refs_3_ = bf16[128,3584]{1,0:T(8,128)(2,1)S(1)} collective-permute-done((bf16[128,3584]{1,0:T(8,128)(2,1)}, bf16[128,3584]{1,0:T(8,128)(2,1)S(1)}, u32[]{:S(2)}, u32[]{:S(2)}) %collective-permute-start.7) | collective-permute-done | bytes 917536 | tf_op jit(solution)/shard_map/ppermute | solution.py:30
  134.9 19.6 %collective-permute-done.8.refs_4_ = bf16[128,3584]{1,0:T(8,128)(2,1)} collective-permute-done((bf16[128,3584]{1,0:T(8,128)(2,1)}, bf16[128,3584]{1,0:T(8,128)(2,1)}, u32[]{:S(2)}, u32[]{:S(2)}) %collective-permute-start.8) | collective-permute-done | bytes 917536 | tf_op jit(solution)/shard_map/ppermute | solution.py:30
  154.5 4.1 %shard_map.132 = (bf16[1,1024,3584]{2,1,0:T(8,128)(2,1)}, f32[8,128]{1,0:T(8,128)}) custom-call(s32[4]{0:T(128)S(1)} %copy-done.4, s32[1]{0:T(128)} %bitcast.8.refs_0_.refs_1_, bf16[2,128,3584]{2,1,0:T(8,128)(2,1)S(1)} %collective-permute-done.3.refs_1_.refs_2_, ...), custom_call_target="tpu_custom_call", output_to_operand_aliasing={{0}: (7, {})} | custom-call | flops 1000 | bytes 1000 | tf_op jit(solution)/shard_map/pallas_call | solution.py:44
  158.7 2.1 %reduce_sum.35 = bf16[32,3584]{1,0:T(8,128)(2,1)} reduce(bf16[4,32,3584]{2,1,0:T(8,128)(2,1)} %all-to-all-done.2, bf16[]{:T(256)} %constant.172.clone.1), dimensions={0}, to_apply=%region_3.4 | reduce | flops 344064 | bytes 1146882 | tf_op jit(solution)/shard_map/reduce_sum | solution.py:525
  (82 shorter events, 22.5 us)
Async XLA Ops:
  3.9 10.3 %copy-start.14 = (s32[32]{0:T(128)S(1)}, s32[32]{0:T(128)}, u32[]{:S(2)}) copy-start(s32[32]{0:T(128)} %param.15) | copy-start | bytes 388
  6.8 26.8 %all-to-all-start = ((bf16[32,16,1024]{2,1,0:T(8,128)(2,1)}), bf16[32,16,1024]{2,1,0:T(8,128)(2,1)S(1)}, u32[]{:S(2)}, u32[]{:S(2)}) async-start(bf16[32,16,1024]{2,1,0:T(8,128)(2,1)} %bitcast.4), calls=%async_computation | async-start | bytes 2097152 | tf_op jit(solution)/shard_map/all_to_all | solution.py:487
  33.6 5.5 %copy-start.15 = (bf16[1,3584]{1,0:T(2,128)(2,1)S(1)}, bf16[1,3584]{1,0:T(2,128)(2,1)}, u32[]{:S(2)}) copy-start(bf16[1,3584]{1,0:T(2,128)(2,1)} %get-tuple-element.35) | copy-start | bytes 21508
  33.6 1.0 copy-start.8
  34.5 23.4 %collective-permute-start = (bf16[2,64,3584]{2,1,0:T(8,128)(2,1)}, bf16[2,64,3584]{2,1,0:T(8,128)(2,1)S(1)}, u32[]{:S(2)}, u32[]{:S(2)}) collective-permute-start(bf16[2,64,3584]{2,1,0:T(8,128)(2,1)} %get-tuple-element.29), channel_id=1, source_target_pairs={{0,16},{16,0},{1,17},{17,1},{2,18},{18,2},{3,19},{19,3},{4,20},{20... | collective-permute-start | bytes 2752520 | tf_op jit(solution)/shard_map/ppermute | solution.py:30
  38.9 2.0 %collective-permute-start.1 = (bf16[256,1024]{1,0:T(8,128)(2,1)S(1)}, bf16[256,1024]{1,0:T(8,128)(2,1)S(1)}, u32[]{:S(2)}, u32[]{:S(2)}) collective-permute-start(bf16[256,1024]{1,0:T(8,128)(2,1)S(1)} %slice_bitcast_fusion), channel_id=1, source_target_pairs={{0,1},{1,0},{2,3},{3,2},{4,5},{5,4},{6,7},{7,6},{8,9},{9,8},{10,11... | collective-permute-start | bytes 1572872 | tf_op jit(solution)/shard_map/ppermute | solution.py:30
  39.0 18.9 %collective-permute-start.2 = (bf16[1,3584]{1,0:T(2,128)(2,1)S(1)}, bf16[1,3584]{1,0:T(2,128)(2,1)S(1)}, u32[]{:S(2)}, u32[]{:S(2)}) collective-permute-start(bf16[1,3584]{1,0:T(2,128)(2,1)S(1)} %copy-done.15), channel_id=1, source_target_pairs={{0,16},{16,0},{1,17},{17,1},{2,18},{18,2},{3,19},{19,3},{4,20},{20... | collective-permute-start | bytes 21512 | tf_op jit(solution)/shard_map/ppermute | solution.py:30
  58.9 7.7 %copy-start.1 = (bf16[2,64,3584]{2,1,0:T(8,128)(2,1)S(1)}, bf16[2,64,3584]{2,1,0:T(8,128)(2,1)}, u32[]{:S(2)}) copy-start(bf16[2,64,3584]{2,1,0:T(8,128)(2,1)} %copy-done) | copy-start | bytes 2752516
  58.9 7.7 %copy-start.4 = (s32[4]{0:T(128)S(1)}, s32[4]{0:T(128)}, u32[]{:S(2)}) copy-start(s32[4]{0:T(128)} %dynamic_slice.16.refs_2_.refs_1_.refs_0_) | copy-start | bytes 52
  58.9 7.7 %copy-start.5 = (f32[8,128]{1,0:T(8,128)S(1)}, f32[8,128]{1,0:T(8,128)}, u32[]{:S(2)}) copy-start(f32[8,128]{1,0:T(8,128)} %get-tuple-element.31.refs_2_) | copy-start | bytes 12292
  58.9 14.7 %copy-start.12 = (f32[1,640]{1,0:T(1,128)S(1)}, f32[1,640]{1,0:T(1,128)}, u32[]{:S(2)}) copy-start(f32[1,640]{1,0:T(1,128)} %constant.187.clone) | copy-start | bytes 7684
  58.9 14.7 %copy-start.13 = (f32[1,640]{1,0:T(1,128)S(1)}, f32[1,640]{1,0:T(1,128)}, u32[]{:S(2)}) copy-start(f32[1,640]{1,0:T(1,128)} %constant.186.clone) | copy-start | bytes 7684
  58.9 58.6 %all-to-all-start.1 = ((bf16[8,80,3584]{2,1,0:T(8,128)(2,1)}), bf16[8,80,3584]{2,1,0:T(8,128)(2,1)}, u32[]{:S(2)}, u32[]{:S(2)}) async-start(bf16[8,80,3584]{2,1,0:T(8,128)(2,1)} %bitcast.30), calls=%async_computation.1 | async-start | bytes 9175040 | tf_op jit(solution)/shard_map/all_to_all | solution.py:508
  63.6 44.6 %collective-permute-start.3 = (bf16[2,128,3584]{2,1,0:T(8,128)(2,1)}, bf16[2,128,3584]{2,1,0:T(8,128)(2,1)S(1)}, u32[]{:S(2)}, u32[]{:S(2)}) collective-permute-start(bf16[2,128,3584]{2,1,0:T(8,128)(2,1)} %get-tuple-element.37), channel_id=1, source_target_pairs={{0,16},{16,0},{1,17},{17,1},{2,18},{18,2},{3,19},{19,3},{4,20},{20... | collective-permute-start | bytes 5505032 | tf_op jit(solution)/shard_map/ppermute | solution.py:30
  69.8 23.7 %collective-permute-start.4 = (bf16[64,3584]{1,0:T(8,128)(2,1)}, bf16[64,3584]{1,0:T(8,128)(2,1)S(1)}, u32[]{:S(2)}, u32[]{:S(2)}) collective-permute-start(bf16[64,3584]{1,0:T(8,128)(2,1)} %get-tuple-element.38), channel_id=1, source_target_pairs={{0,32},{32,64},{64,96},{96,0},{1,33},{33,65},{65,97},{97,1},{2,34}... | collective-permute-start | bytes 1376264 | tf_op jit(solution)/shard_map/ppermute | solution.py:30
  70.8 22.7 %collective-permute-start.5 = (bf16[64,3584]{1,0:T(8,128)(2,1)}, bf16[64,3584]{1,0:T(8,128)(2,1)}, u32[]{:S(2)}, u32[]{:S(2)}) collective-permute-start(bf16[64,3584]{1,0:T(8,128)(2,1)} %get-tuple-element.39), channel_id=1, source_target_pairs={{0,64},{32,96},{64,0},{96,32},{1,65},{33,97},{65,1},{97,33},{2,66}... | collective-permute-start | bytes 1376264 | tf_op jit(solution)/shard_map/ppermute | solution.py:30
  72.6 21.6 %collective-permute-start.6 = (bf16[64,3584]{1,0:T(8,128)(2,1)}, bf16[64,3584]{1,0:T(8,128)(2,1)}, u32[]{:S(2)}, u32[]{:S(2)}) collective-permute-start(bf16[64,3584]{1,0:T(8,128)(2,1)} %get-tuple-element.40), channel_id=1, source_target_pairs={{0,96},{32,0},{64,32},{96,64},{1,97},{33,1},{65,33},{97,65},{2,98}... | collective-permute-start | bytes 1376264 | tf_op jit(solution)/shard_map/ppermute | solution.py:30
  96.6 57.9 %collective-permute-start.10 = (bf16[256,3584]{1,0:T(8,128)(2,1)}, bf16[256,3584]{1,0:T(8,128)(2,1)}, u32[]{:S(2)}, u32[]{:S(2)}) collective-permute-start(bf16[256,3584]{1,0:T(8,128)(2,1)} %get-tuple-element.47), channel_id=1, source_target_pairs={{0,16},{16,0},{1,17},{17,1},{2,18},{18,2},{3,19},{19,3},{4,20},{20... | collective-permute-start | bytes 5505032 | tf_op jit(solution)/shard_map/ppermute | solution.py:30
  97.6 1.0 copy-start.3
  111.1 23.8 %collective-permute-start.7 = (bf16[128,3584]{1,0:T(8,128)(2,1)}, bf16[128,3584]{1,0:T(8,128)(2,1)S(1)}, u32[]{:S(2)}, u32[]{:S(2)}) collective-permute-start(bf16[128,3584]{1,0:T(8,128)(2,1)} %get-tuple-element.44), channel_id=1, source_target_pairs={{0,32},{32,64},{64,96},{96,0},{1,33},{33,65},{65,97},{97,1},{2,34}... | collective-permute-start | bytes 2752520 | tf_op jit(solution)/shard_map/ppermute | solution.py:30
  112.1 42.3 %collective-permute-start.8 = (bf16[128,3584]{1,0:T(8,128)(2,1)}, bf16[128,3584]{1,0:T(8,128)(2,1)}, u32[]{:S(2)}, u32[]{:S(2)}) collective-permute-start(bf16[128,3584]{1,0:T(8,128)(2,1)} %get-tuple-element.45), channel_id=1, source_target_pairs={{0,64},{32,96},{64,0},{96,32},{1,65},{33,97},{65,1},{97,33},{2,66}... | collective-permute-start | bytes 2752520 | tf_op jit(solution)/shard_map/ppermute | solution.py:30
  115.3 39.2 %collective-permute-start.9 = (bf16[128,3584]{1,0:T(8,128)(2,1)}, bf16[128,3584]{1,0:T(8,128)(2,1)}, u32[]{:S(2)}, u32[]{:S(2)}) collective-permute-start(bf16[128,3584]{1,0:T(8,128)(2,1)} %get-tuple-element.46), channel_id=1, source_target_pairs={{0,96},{32,0},{64,32},{96,64},{1,97},{33,1},{65,33},{97,65},{2,98}... | collective-permute-start | bytes 2752520 | tf_op jit(solution)/shard_map/ppermute | solution.py:30
  123.0 35.7 %all-to-all-start.2 = ((bf16[4,32,3584]{2,1,0:T(8,128)(2,1)}), bf16[4,32,3584]{2,1,0:T(8,128)(2,1)}, u32[]{:S(2)}, u32[]{:S(2)}) async-start(bf16[4,32,3584]{2,1,0:T(8,128)(2,1)} %bitcast.34), calls=%async_computation.2 | async-start | bytes 1835008 | tf_op jit(solution)/shard_map/all_to_all | solution.py:524
  154.5 6.2 %copy-start.11 = (bf16[1,3584]{1,0:T(2,128)(2,1)S(1)}, bf16[1,3584]{1,0:T(2,128)(2,1)}, u32[]{:S(2)}) copy-start(bf16[1,3584]{1,0:T(2,128)(2,1)} %copy-done.10) | copy-start | bytes 21508
  (6 other events, 4.4 us)

commit v4 on v3

--- a/solution.py
+++ b/solution.py
@@ -16,7 +16,7 @@
 BLOCK = 16
 TRADED = (64, 128)
 COLUMNS = 512
-VMEM_LIMIT = 60 << 20
+VMEM_LIMIT = 50 << 20
 AHEAD = 3
 CHEAP = pl.CostEstimate(flops=1000, bytes_accessed=1000, transcendentals=0)
 HBM = pl.BlockSpec(memory_space=pltpu.HBM)
@@ -33,7 +33,7 @@
 TOKEN = jax.ShapeDtypeStruct((8, 128), jnp.float32)
 
 
-def ordered_call(kernel, operands, after, out_shape, out_specs, scratch, in_specs=None, aliases=None, limit=60):
+def ordered_call(kernel, operands, after, out_shape, out_specs, scratch, in_specs=None, aliases=None, limit=50):
     after = [t for t in after if t is not None]
     in_specs = in_specs or [HBM] * len(operands)
 
@@ -87,6 +87,7 @@
         [pltpu.VMEM(shape, weight.dtype) for shape in shapes]
         + [pltpu.SemaphoreType.DMA((len(shapes),))] * 2,
         in_specs=[SMEM, HBM],
+        limit=60,
     )
 
 
@@ -184,40 +185,64 @@
     return whole, token
 
 
-def finish_kernel(at, quarter, parts, picks, part, block, *refs):
-    arrived, (straight, _, out, held, rest, reads, writes) = refs[: parts - 1], refs[parts - 1 :]
-    rows = arrived[0].shape[0]
-    moves = []
-    share = rest.shape[1]
-    for i in range(parts):
-        first = out.shape[1] - (parts - i) * share
+def own_kernel(at, quarter, picks, part, block, straight, _, out, held, rest, reads, writes):
+    rows, share = held.shape[0], rest.shape[1]
+    count = rest.shape[0]
+    start = pl.multiple_of(part[0] * quarter + at, 16)
+    moves = [(block.at[picks[0]], held, out.at[0, pl.ds(start, rows)])]
+    for i in range(count):
+        first = out.shape[1] - (count - i) * share
         moves.append(
             (straight.at[pl.ds(i * share, share)], rest.at[i], out.at[0, pl.ds(first, share)])
         )
-    for i, source in enumerate([block.at[picks[0]], *arrived]):
-        origin = lax.rem(part[0] - i + parts, parts)
+    through(moves, reads, writes)
+
+
+def placed_own(picks, part, block, straight, at, quarter, whole, after):
+    _, rows, width = block.shape
+    (whole,), token = ordered_call(
+        functools.partial(own_kernel, at, quarter),
+        [picks, part, block, straight, whole],
+        after,
+        [jax.ShapeDtypeStruct(whole.shape, whole.dtype)],
+        [HBM],
+        [
+            pltpu.VMEM((rows, width), block.dtype),
+            pltpu.VMEM((4, straight.shape[0] // 4, width), block.dtype),
+        ]
+        + [pltpu.SemaphoreType.DMA((5,))] * 2,
+        in_specs=[SMEM, SMEM, ANY, ANY, HBM],
+        aliases={4: 0},
+        limit=16,
+    )
+    return whole, token
+
+
+def others_kernel(at, quarter, part, *refs):
+    *arrived, _, out, held, reads, writes = refs
+    parts = len(arrived) + 1
+    rows = arrived[0].shape[0]
+    moves = []
+    for i, source in enumerate(arrived):
+        origin = lax.rem(part[0] - i - 1 + parts, parts)
         start = pl.multiple_of(origin * quarter + at, 16)
         moves.append((source, held.at[i], out.at[0, pl.ds(start, rows)]))
     through(moves, reads, writes)
 
 
-def finished(picks, part, block, arrived, straight, at, quarter, whole, after):
-    parts = len(arrived) + 1
+def placed_others(part, arrived, at, quarter, whole, after):
     rows, width = arrived[0].shape
-    operands = [picks, part, block, *arrived, straight, whole]
+    count = len(arrived)
     (whole,), _ = ordered_call(
-        functools.partial(finish_kernel, at, quarter, parts),
-        operands,
-        after,
-        [jax.ShapeDtypeStruct(whole.shape, block.dtype)],
+        functools.partial(others_kernel, at, quarter),
+        [part, *arrived, whole],
+        after,
+        [jax.ShapeDtypeStruct(whole.shape, whole.dtype)],
         [HBM],
-        [
-            pltpu.VMEM((parts, rows, width), block.dtype),
-            pltpu.VMEM((parts, straight.shape[0] // parts, width), block.dtype),
-        ]
-        + [pltpu.SemaphoreType.DMA((2 * parts,))] * 2,
-        in_specs=[SMEM, SMEM] + [ANY] * (parts + 1) + [HBM],
-        aliases={len(operands) - 1: 0},
+        [pltpu.VMEM((count, rows, width), whole.dtype)]
+        + [pltpu.SemaphoreType.DMA((count,))] * 2,
+        in_specs=[SMEM] + [ANY] * count + [HBM],
+        aliases={1 + count: 0},
         limit=16,
     )
     return whole
@@ -488,8 +513,8 @@
     mine = lax.dynamic_slice(replica_map, (me,), (1,)) % 2
     picks = lax.psum(jnp.where(jnp.arange(parts) == part, mine, 0), "dp")
     picks = jnp.roll(picks, -part)
-    scale, token = chosen_scale(partner, column_scale, [picks])
-    blocks, token = cut(here, expert_weight, ranges, quarter, [picks, token])
+    scale, token = chosen_scale(partner, column_scale, [outgoing])
+    blocks, token = cut(here, expert_weight, ranges, quarter, [token])
     replica_scale = shifted(scale, "xh", 1)
 
     def traded(j, after):
@@ -498,7 +523,7 @@
 
     far = shifted(received[:, 8:].reshape(N_EP * 8, depth), "c", 1)
     received = received.reshape(N_EP * BLOCK, depth)
-    blocks[0] = gated(blocks[0], [received])
+    blocks[0] = gated(blocks[0], [received, picks])
     crossed = [shifted(block, "xh", 1) for block in blocks]
     where = jnp.stack([me, lax.axis_index("c")]).astype(jnp.int32)
     returned, token = serve(where, received, far, expert_weight, column_scale, [token, picks])
@@ -516,9 +541,10 @@
         picks, here, crossed[0], first, starts[0], quarter, depth, None, [token]
     )
     second, token = traded(1, [token])
-    replica_weight = finished(
-        picks, here, crossed[1], second, straight, starts[1], quarter, whole, [token]
-    )
+    whole, token = placed_own(
+        picks, here, crossed[1], straight, starts[1], quarter, whole, [token]
+    )
+    replica_weight = placed_others(here, second, starts[1], quarter, whole, [token])
 
     partial = mixed(mixes, returned.reshape(-1, width))
     partial = lax.all_to_all(partial.reshape(N_X, steps * rows, width), X, 0, 0, tiled=True)

time: 162 us -> 159 us (0.981)
  local copies, waits for them, and re-layouts: 11.1 us -> 4.12 us
  waiting for transfers between devices: 50.7 us -> 55.1 us
  starting transfers between devices: 33.1 us -> 37 us
  Pallas kernels: 43.9 us -> 41.3 us
  other arithmetic: 5.02 us -> 3.37 us
    ppermute x11, waiting for transfers between devices: 49.4 us -> 55.1 us  [shifted(): lax.ppermute(block, axis, [(i, (i + distance) % count) for i in range(cou...]
    unnamed x35 -> x19, local copies, waits for them, and re-layouts: 7.18 us -> 2.76 us
    ppermute x11, starting transfers between devices: 16.8 us -> 20.6 us  [shifted(): lax.ppermute(block, axis, [(i, (i + distance) % count) for i in range(cou...]
    pallas_call x10 -> x11, Pallas kernels: 22.2 us -> 20.7 us  [ordered_call(): pl.pallas_call(body, out_shape=list(out_shape) + [TOKEN], in_specs=list(i...]
  transfers between devices with their start and end apart: 14 -> 14, of which waited for: 7 -> 7; matrix products, arithmetic and copies ran while one was open for 3% -> 1% of each run, Pallas kernels for 27% -> 26%
where the time goes in v4:
time: 159 us; the launch traced here: 158 us
  waiting for transfers between devices  55.1 us (35%)
  Pallas kernels  41.3 us (26%)
  starting transfers between devices  37 us (23%)
  blocking collectives  9.77 us (6%)
  between operations  4.87 us (3%)
  local copies, waits for them, and re-layouts  4.12 us (3%)
  other arithmetic  3.37 us (2%)
  matrix products  2.91 us (2%)
    ppermute x11, waiting for transfers between devices, shifted(): lax.ppermute(block, axis, [(i, (i + distance) % count) for i in range(cou...  55.1 us
    pallas_call x11, Pallas kernels, ordered_call(): pl.pallas_call(body, out_shape=list(out_shape) + [TOKEN], in_specs=list(i...  20.7 us
    ppermute x11, starting transfers between devices, shifted(): lax.ppermute(block, axis, [(i, (i + distance) % count) for i in range(cou...  20.6 us
    pallas_call x1, Pallas kernels, serve(): pl.pallas_call(serve_kernel, in_specs=[SMEM, WHOLE, WHOLE, HBM, HBM, WHOL...  16.1 us
    psum x1, blocking collectives, local(): picks = lax.psum(jnp.where(jnp.arange(parts) == part, mine, 0), 'dp')  9.77 us
    all_to_all x1, starting transfers between devices, local(): lax.all_to_all(outgoing.reshape(N_EP, BLOCK, depth), EP, 0, 0, tiled=True)  7.4 us
    all_to_all x1, starting transfers between devices, local(): lax.all_to_all(returned.reshape(N_YC, -1, width), ('y', 'c'), 0, 0, tiled...  4.74 us
    pallas_call x1, Pallas kernels, mixed(): pl.pallas_call(mix_kernel, in_specs=[WHOLE, HBM], out_specs=HBM, out_shap...  4.52 us
  transfers between devices with their start and end apart: 14, of which 7 were waited for; matrix products, arithmetic and copies ran while one was open for 1% of the time, Pallas kernels for 26%

profile of v4, /device:TPU:0, one launch (start us, length us, event | category | flops | bytes accessed | tf_op | source)
XLA Modules:
  0.0 158.4 jit_solution(8318087855591828619)
XLA Ops:
  3.9 2.9 %convolution_convert_fusion.refs_2_ = bf16[512,1024]{1,0:T(8,128)(2,1)} fusion(bf16[1,1024]{1,0:T(2,128)(2,1)S(1)} %broadcast_in_dim.40, bf16[256,1024]{1,0:T(8,128)(2,1)} %bitcast.36, s32[264]{0:T(512)S(1)} %pad_add_fusion, s32[512]{0:T(512)S(1)} %iota_select_fusion, bf16[264]{0:T(512)(128)(2,1)S(1)} %pad.7.clone, bf16[264]{0:T(512)(128)(2,1)S(1)} %pad.6.clone), kind=kOutput, calls=%fused_computation | convolution fusion | flops 279646208 | bytes 1579072 | tf_op jit(solution)/shard_map/dot_general | solution.py:511
  6.8 7.4 %all-to-all-start = ((bf16[32,16,1024]{2,1,0:T(8,128)(2,1)}), bf16[32,16,1024]{2,1,0:T(8,128)(2,1)S(1)}, u32[]{:S(2)}, u32[]{:S(2)}) async-start(bf16[32,16,1024]{2,1,0:T(8,128)(2,1)} %bitcast.4), calls=%async_computation | async-start | bytes 2097152 | tf_op jit(solution)/shard_map/all_to_all | solution.py:512
  19.4 3.0 %shard_map.122 = (bf16[2,64,3584]{2,1,0:T(8,128)(2,1)}, bf16[2,128,3584]{2,1,0:T(8,128)(2,1)}, f32[8,128]{1,0:T(8,128)}) custom-call(s32[1]{0:T(128)} %bitcast.8.refs_0_.refs_1_, bf16[2,1024,3584]{2,1,0:T(8,128)(2,1)} %refs_1_.5, f32[8,128]{1,0:T(8,128)} %copy-done.4), custom_call_target="tpu_custom_call" | custom-call | flops 1000 | bytes 1000 | tf_op jit(solution)/shard_map/pallas_call | solution.py:44
  22.5 9.8 %psum.7 = s32[4]{0:T(128)S(1)} all-reduce(s32[4]{0:T(128)S(1)} %compare_select_fusion), channel_id=1, replica_groups=mesh['dp'=4,'xh'=2,'xl'=2,'y'=4,'c'=2] {'dp'}, use_global_device_ids=true, to_apply=%region_2.3 | all-reduce | flops 4 | bytes 32 | tf_op jit(solution)/shard_map/psum | solution.py:514
  32.4 3.3 %collective-permute-start = (bf16[2,64,3584]{2,1,0:T(8,128)(2,1)}, bf16[2,64,3584]{2,1,0:T(8,128)(2,1)S(1)}, u32[]{:S(2)}, u32[]{:S(2)}) collective-permute-start(bf16[2,64,3584]{2,1,0:T(8,128)(2,1)} %get-tuple-element.31), channel_id=1, source_target_pairs={{0,16},{16,0},{1,17},{17,1},{2,18},{18,2},{3,19},{19,3},{4,20},{20... | collective-permute-start | bytes 2752520 | tf_op jit(solution)/shard_map/ppermute | solution.py:30
  37.8 16.1 %shard_map.124 = (bf16[640,3584]{1,0:T(8,128)(2,1)}, f32[8,128]{1,0:T(8,128)S(1)}) custom-call(s32[2]{0:T(128)S(1)} %pad_add_fusion.2.me, bf16[512,1024]{1,0:T(8,128)(2,1)S(1)} %bitcast.31, bf16[256,1024]{1,0:T(8,128)(2,1)S(1)} %collective-permute-done.1.far, bf16[2,2,640,768]{3,2,1,0:T(8,128)(2,1)} %constant.185.clone.order, ...), custom_call_target="tpu_custom_call" | custom-call | flops 1000 | bytes 1000 | tf_op jit(solution)/shard_map/pallas_call | solution.py:357
  55.7 4.7 %all-to-all-start.1 = ((bf16[8,80,3584]{2,1,0:T(8,128)(2,1)}), bf16[8,80,3584]{2,1,0:T(8,128)(2,1)}, u32[]{:S(2)}, u32[]{:S(2)}) async-start(bf16[8,80,3584]{2,1,0:T(8,128)(2,1)} %bitcast.34), calls=%async_computation.1 | async-start | bytes 9175040 | tf_op jit(solution)/shard_map/all_to_all | solution.py:533
  60.4 2.8 %collective-permute-start.3 = (bf16[2,128,3584]{2,1,0:T(8,128)(2,1)}, bf16[2,128,3584]{2,1,0:T(8,128)(2,1)}, u32[]{:S(2)}, u32[]{:S(2)}) collective-permute-start(bf16[2,128,3584]{2,1,0:T(8,128)(2,1)} %get-tuple-element.39), channel_id=1, source_target_pairs={{0,16},{16,0},{1,17},{17,1},{2,18},{18,2},{3,19},{19,3},{4,20},{20... | collective-permute-start | bytes 5505032 | tf_op jit(solution)/shard_map/ppermute | solution.py:30
  63.3 2.5 %shard_map.125 = (bf16[64,3584]{1,0:T(8,128)(2,1)}, bf16[64,3584]{1,0:T(8,128)(2,1)}, bf16[64,3584]{1,0:T(8,128)(2,1)}, f32[8,128]{1,0:T(8,128)S(1)}) custom-call(s32[4]{0:T(128)S(1)} %dynamic_slice.16.refs_2_.refs_1_.refs_0_, bf16[2,64,3584]{2,1,0:T(8,128)(2,1)S(1)} %collective-permute-done.refs_1_.refs_2_, f32[8,128]{1,0:T(8,128)S(1)} %get-tuple-element.33.refs_2_), custom_call_target="tpu_custom_call" | custom-call | flops 1000 | bytes 1000 | tf_op jit(solution)/shard_map/pallas_call | solution.py:44
  66.8 3.3 %collective-permute-start.5 = (bf16[64,3584]{1,0:T(8,128)(2,1)}, bf16[64,3584]{1,0:T(8,128)(2,1)S(1)}, u32[]{:S(2)}, u32[]{:S(2)}) collective-permute-start(bf16[64,3584]{1,0:T(8,128)(2,1)} %get-tuple-element.41), channel_id=1, source_target_pairs={{0,64},{32,96},{64,0},{96,32},{1,65},{33,97},{65,1},{97,33},{2,66}... | collective-permute-start | bytes 1376264 | tf_op jit(solution)/shard_map/ppermute | solution.py:30
  72.4 7.3 %collective-permute-done.4.refs_3_ = bf16[64,3584]{1,0:T(8,128)(2,1)S(1)} collective-permute-done((bf16[64,3584]{1,0:T(8,128)(2,1)}, bf16[64,3584]{1,0:T(8,128)(2,1)S(1)}, u32[]{:S(2)}, u32[]{:S(2)}) %collective-permute-start.4) | collective-permute-done | bytes 458784 | tf_op jit(solution)/shard_map/ppermute | solution.py:30
  79.7 10.9 %collective-permute-done.5.refs_4_ = bf16[64,3584]{1,0:T(8,128)(2,1)S(1)} collective-permute-done((bf16[64,3584]{1,0:T(8,128)(2,1)}, bf16[64,3584]{1,0:T(8,128)(2,1)S(1)}, u32[]{:S(2)}, u32[]{:S(2)}) %collective-permute-start.5) | collective-permute-done | bytes 458784 | tf_op jit(solution)/shard_map/ppermute | solution.py:30
  90.6 2.3 %shard_map.129 = (bf16[256,3584]{1,0:T(8,128)(2,1)}, f32[8,128]{1,0:T(8,128)S(1)}) custom-call(s32[1]{0:T(128)S(6)} %select_n.135.refs_0_, bf16[2,1024,3584]{2,1,0:T(8,128)(2,1)} %refs_1_.5, f32[8,128]{1,0:T(8,128)S(1)} %get-tuple-element.43.refs_2_, bf16[64,3584]{1,0:T(8,128)(2,1)S(1)} %collective-permute-done.4.refs_3_, ...), custom_call_target="tpu_custom_call" | custom-call | flops 1000 | bytes 1000 | tf_op jit(solution)/shard_map/pallas_call | solution.py:44
  95.0 2.9 %shard_map.130 = (bf16[1,1024,3584]{2,1,0:T(8,128)(2,1)}, f32[8,128]{1,0:T(8,128)S(1)}) custom-call(s32[4]{0:T(128)S(1)} %dynamic_slice.16.refs_2_.refs_1_.refs_0_, s32[1]{0:T(128)} %bitcast.8.refs_0_.refs_1_, bf16[2,64,3584]{2,1,0:T(8,128)(2,1)S(1)} %collective-permute-done.refs_1_.refs_2_, bf16[64,3584]{1,0:T(8,128)(2,1)S(1)} %collective-permute-done.4.refs_3_, ...), custom_call_target="tpu_custom_call" | custom-call | flops 1000 | bytes 1000 | tf_op jit(solution)/shard_map/pallas_call | solution.py:44
  97.9 7.3 %collective-permute-done.3.refs_1_.refs_2_ = bf16[2,128,3584]{2,1,0:T(8,128)(2,1)} collective-permute-done((bf16[2,128,3584]{2,1,0:T(8,128)(2,1)}, bf16[2,128,3584]{2,1,0:T(8,128)(2,1)}, u32[]{:S(2)}, u32[]{:S(2)}) %collective-permute-start.3) | collective-permute-done | bytes 1835040 | tf_op jit(solution)/shard_map/ppermute | solution.py:30
  105.2 3.3 %shard_map.131 = (bf16[128,3584]{1,0:T(8,128)(2,1)}, bf16[128,3584]{1,0:T(8,128)(2,1)}, bf16[128,3584]{1,0:T(8,128)(2,1)}, f32[8,128]{1,0:T(8,128)S(1)}) custom-call(s32[4]{0:T(128)S(1)} %dynamic_slice.16.refs_2_.refs_1_.refs_0_, bf16[2,128,3584]{2,1,0:T(8,128)(2,1)} %collective-permute-done.3.refs_1_.refs_2_, f32[8,128]{1,0:T(8,128)S(1)} %get-tuple-element.45.refs_2_), custom_call_target="tpu_custom_call" | custom-call | flops 1000 | bytes 1000 | tf_op jit(solution)/shard_map/pallas_call | solution.py:44
  110.5 4.0 %collective-permute-start.8 = (bf16[128,3584]{1,0:T(8,128)(2,1)}, bf16[128,3584]{1,0:T(8,128)(2,1)S(1)}, u32[]{:S(2)}, u32[]{:S(2)}) collective-permute-start(bf16[128,3584]{1,0:T(8,128)(2,1)} %get-tuple-element.47), channel_id=1, source_target_pairs={{0,64},{32,96},{64,0},{96,32},{1,65},{33,97},{65,1},{97,33},{2,66}... | collective-permute-start | bytes 2752520 | tf_op jit(solution)/shard_map/ppermute | solution.py:30
  115.1 4.5 %shard_map.128 = bf16[128,3584]{1,0:T(8,128)(2,1)} custom-call(bf16[256,640]{1,0:T(8,128)(2,1)S(1)} %copy-done.1, bf16[640,3584]{1,0:T(8,128)(2,1)} %bitcast.14.returned), custom_call_target="tpu_custom_call" | custom-call | flops 1000 | bytes 1000 | tf_op jit(solution)/shard_map/pallas_call | solution.py:459
  119.6 4.2 %all-to-all-start.2 = ((bf16[4,32,3584]{2,1,0:T(8,128)(2,1)}), bf16[4,32,3584]{2,1,0:T(8,128)(2,1)}, u32[]{:S(2)}, u32[]{:S(2)}) async-start(bf16[4,32,3584]{2,1,0:T(8,128)(2,1)} %bitcast.15), calls=%async_computation.2 | async-start | bytes 1835008 | tf_op jit(solution)/shard_map/all_to_all | solution.py:550
  123.8 20.7 %collective-permute-done.10.refs_3_ = bf16[256,3584]{1,0:T(8,128)(2,1)} collective-permute-done((bf16[256,3584]{1,0:T(8,128)(2,1)}, bf16[256,3584]{1,0:T(8,128)(2,1)}, u32[]{:S(2)}, u32[]{:S(2)}) %collective-permute-start.10) | collective-permute-done | bytes 1835040 | tf_op jit(solution)/shard_map/ppermute | solution.py:30
  144.5 3.3 %shard_map.132 = (bf16[1,1024,3584]{2,1,0:T(8,128)(2,1)}, f32[8,128]{1,0:T(8,128)S(1)}) custom-call(s32[4]{0:T(128)S(1)} %dynamic_slice.16.refs_2_.refs_1_.refs_0_, s32[1]{0:T(128)} %bitcast.8.refs_0_.refs_1_, bf16[2,128,3584]{2,1,0:T(8,128)(2,1)} %collective-permute-done.3.refs_1_.refs_2_, ...), custom_call_target="tpu_custom_call", output_to_operand_aliasing={{0}: (4, {})} | custom-call | flops 1000 | bytes 1000 | tf_op jit(solution)/shard_map/pallas_call | solution.py:44
  147.9 5.6 %collective-permute-done.8.refs_2_ = bf16[128,3584]{1,0:T(8,128)(2,1)S(1)} collective-permute-done((bf16[128,3584]{1,0:T(8,128)(2,1)}, bf16[128,3584]{1,0:T(8,128)(2,1)S(1)}, u32[]{:S(2)}, u32[]{:S(2)}) %collective-permute-start.8) | collective-permute-done | bytes 917536 | tf_op jit(solution)/shard_map/ppermute | solution.py:30
  153.5 2.2 %shard_map.133 = (bf16[1,1024,3584]{2,1,0:T(8,128)(2,1)}, f32[8,128]{1,0:T(8,128)}) custom-call(s32[1]{0:T(128)} %bitcast.8.refs_0_.refs_1_, bf16[128,3584]{1,0:T(8,128)(2,1)S(1)} %collective-permute-done.7.refs_1_, bf16[128,3584]{1,0:T(8,128)(2,1)S(1)} %collective-permute-done.8.refs_2_, ...), custom_call_target="tpu_custom_call", output_to_operand_aliasing={{0}: (4, {})} | custom-call | flops 1000 | bytes 1000 | tf_op jit(solution)/shard_map/pallas_call | solution.py:44
  155.8 2.1 %reduce_sum.35 = bf16[32,3584]{1,0:T(8,128)(2,1)} reduce(bf16[4,32,3584]{2,1,0:T(8,128)(2,1)} %all-to-all-done.2, bf16[]{:T(256)} %constant.172.clone.1), dimensions={0}, to_apply=%region_3.4 | reduce | flops 344064 | bytes 1146882 | tf_op jit(solution)/shard_map/reduce_sum | solution.py:551
  (67 shorter events, 17.1 us)
Async XLA Ops:
  3.9 10.4 %copy-start.7 = (s32[32]{0:T(128)S(1)}, s32[32]{0:T(128)}, u32[]{:S(2)}) copy-start(s32[32]{0:T(128)} %param.15) | copy-start | bytes 388
  3.9 12.9 %copy-start.2 = (bf16[2,3584]{1,0:T(2,128)(2,1)S(1)}, bf16[2,3584]{1,0:T(2,128)(2,1)}, u32[]{:S(2)}) copy-start(bf16[2,3584]{1,0:T(2,128)(2,1)} %scale.1) | copy-start | bytes 43012
  6.8 25.6 %all-to-all-start = ((bf16[32,16,1024]{2,1,0:T(8,128)(2,1)}), bf16[32,16,1024]{2,1,0:T(8,128)(2,1)S(1)}, u32[]{:S(2)}, u32[]{:S(2)}) async-start(bf16[32,16,1024]{2,1,0:T(8,128)(2,1)} %bitcast.4), calls=%async_computation | async-start | bytes 2097152 | tf_op jit(solution)/shard_map/all_to_all | solution.py:512
  16.8 0.6 copy-start.4
  22.4 15.3 %copy-start.3 = (f32[8,128]{1,0:T(8,128)S(1)}, f32[8,128]{1,0:T(8,128)}, u32[]{:S(2)}) copy-start(f32[8,128]{1,0:T(8,128)} %get-tuple-element.32.refs_0_) | copy-start | bytes 12292
  32.4 23.3 %collective-permute-start = (bf16[2,64,3584]{2,1,0:T(8,128)(2,1)}, bf16[2,64,3584]{2,1,0:T(8,128)(2,1)S(1)}, u32[]{:S(2)}, u32[]{:S(2)}) collective-permute-start(bf16[2,64,3584]{2,1,0:T(8,128)(2,1)} %get-tuple-element.31), channel_id=1, source_target_pairs={{0,16},{16,0},{1,17},{17,1},{2,18},{18,2},{3,19},{19,3},{4,20},{20... | collective-permute-start | bytes 2752520 | tf_op jit(solution)/shard_map/ppermute | solution.py:30
  35.8 2.0 %collective-permute-start.1 = (bf16[256,1024]{1,0:T(8,128)(2,1)S(1)}, bf16[256,1024]{1,0:T(8,128)(2,1)S(1)}, u32[]{:S(2)}, u32[]{:S(2)}) collective-permute-start(bf16[256,1024]{1,0:T(8,128)(2,1)S(1)} %slice_bitcast_fusion), channel_id=1, source_target_pairs={{0,1},{1,0},{2,3},{3,2},{4,5},{5,4},{6,7},{7,6},{8,9},{9,8},{10,11... | collective-permute-start | bytes 1572872 | tf_op jit(solution)/shard_map/ppermute | solution.py:30
  35.9 19.8 %collective-permute-start.2 = (bf16[1,3584]{1,0:T(2,128)(2,1)S(1)}, bf16[1,3584]{1,0:T(2,128)(2,1)S(1)}, u32[]{:S(2)}, u32[]{:S(2)}) collective-permute-start(bf16[1,3584]{1,0:T(2,128)(2,1)S(1)} %get-tuple-element.37), channel_id=1, source_target_pairs={{0,16},{16,0},{1,17},{17,1},{2,18},{18,2},{3,19},{19,3},{4,20},{20... | collective-permute-start | bytes 21512 | tf_op jit(solution)/shard_map/ppermute | solution.py:30
  55.7 15.5 %copy-start.5 = (f32[1,640]{1,0:T(1,128)S(1)}, f32[1,640]{1,0:T(1,128)}, u32[]{:S(2)}) copy-start(f32[1,640]{1,0:T(1,128)} %constant.186.clone) | copy-start | bytes 7684
  55.7 15.5 %copy-start.6 = (f32[1,640]{1,0:T(1,128)S(1)}, f32[1,640]{1,0:T(1,128)}, u32[]{:S(2)}) copy-start(f32[1,640]{1,0:T(1,128)} %constant.187.clone) | copy-start | bytes 7684
  55.7 59.4 %all-to-all-start.1 = ((bf16[8,80,3584]{2,1,0:T(8,128)(2,1)}), bf16[8,80,3584]{2,1,0:T(8,128)(2,1)}, u32[]{:S(2)}, u32[]{:S(2)}) async-start(bf16[8,80,3584]{2,1,0:T(8,128)(2,1)} %bitcast.34), calls=%async_computation.1 | async-start | bytes 9175040 | tf_op jit(solution)/shard_map/all_to_all | solution.py:533
  60.4 44.7 %collective-permute-start.3 = (bf16[2,128,3584]{2,1,0:T(8,128)(2,1)}, bf16[2,128,3584]{2,1,0:T(8,128)(2,1)}, u32[]{:S(2)}, u32[]{:S(2)}) collective-permute-start(bf16[2,128,3584]{2,1,0:T(8,128)(2,1)} %get-tuple-element.39), channel_id=1, source_target_pairs={{0,16},{16,0},{1,17},{17,1},{2,18},{18,2},{3,19},{19,3},{4,20},{20... | collective-permute-start | bytes 5505032 | tf_op jit(solution)/shard_map/ppermute | solution.py:30
  65.7 13.9 %collective-permute-start.4 = (bf16[64,3584]{1,0:T(8,128)(2,1)}, bf16[64,3584]{1,0:T(8,128)(2,1)S(1)}, u32[]{:S(2)}, u32[]{:S(2)}) collective-permute-start(bf16[64,3584]{1,0:T(8,128)(2,1)} %get-tuple-element.40), channel_id=1, source_target_pairs={{0,32},{32,64},{64,96},{96,0},{1,33},{33,65},{65,97},{97,1},{2,34}... | collective-permute-start | bytes 1376264 | tf_op jit(solution)/shard_map/ppermute | solution.py:30
  66.8 23.7 %collective-permute-start.5 = (bf16[64,3584]{1,0:T(8,128)(2,1)}, bf16[64,3584]{1,0:T(8,128)(2,1)S(1)}, u32[]{:S(2)}, u32[]{:S(2)}) collective-permute-start(bf16[64,3584]{1,0:T(8,128)(2,1)} %get-tuple-element.41), channel_id=1, source_target_pairs={{0,64},{32,96},{64,0},{96,32},{1,65},{33,97},{65,1},{97,33},{2,66}... | collective-permute-start | bytes 1376264 | tf_op jit(solution)/shard_map/ppermute | solution.py:30
  70.1 20.5 %collective-permute-start.6 = (bf16[64,3584]{1,0:T(8,128)(2,1)}, bf16[64,3584]{1,0:T(8,128)(2,1)S(1)}, u32[]{:S(2)}, u32[]{:S(2)}) collective-permute-start(bf16[64,3584]{1,0:T(8,128)(2,1)} %get-tuple-element.42), channel_id=1, source_target_pairs={{0,96},{32,0},{64,32},{96,64},{1,97},{33,1},{65,33},{97,65},{2,98}... | collective-permute-start | bytes 1376264 | tf_op jit(solution)/shard_map/ppermute | solution.py:30
  72.4 20.5 %copy-start = (bf16[256,640]{1,0:T(8,128)(2,1)}, bf16[256,640]{1,0:T(8,128)(2,1)S(1)}, u32[]{:S(2)}) copy-start(bf16[256,640]{1,0:T(8,128)(2,1)S(1)} %get-tuple-element.35.mixes) | copy-start | bytes 983044
  92.9 51.6 %collective-permute-start.10 = (bf16[256,3584]{1,0:T(8,128)(2,1)}, bf16[256,3584]{1,0:T(8,128)(2,1)}, u32[]{:S(2)}, u32[]{:S(2)}) collective-permute-start(bf16[256,3584]{1,0:T(8,128)(2,1)} %get-tuple-element.49), channel_id=1, source_target_pairs={{0,16},{16,0},{1,17},{17,1},{2,18},{18,2},{3,19},{19,3},{4,20},{20... | collective-permute-start | bytes 5505032 | tf_op jit(solution)/shard_map/ppermute | solution.py:30
  97.9 17.2 %copy-start.1 = (bf16[256,640]{1,0:T(8,128)(2,1)S(1)}, bf16[256,640]{1,0:T(8,128)(2,1)}, u32[]{:S(2)}) copy-start(bf16[256,640]{1,0:T(8,128)(2,1)} %copy-done) | copy-start | bytes 983044
  108.5 39.4 %collective-permute-start.7 = (bf16[128,3584]{1,0:T(8,128)(2,1)}, bf16[128,3584]{1,0:T(8,128)(2,1)S(1)}, u32[]{:S(2)}, u32[]{:S(2)}) collective-permute-start(bf16[128,3584]{1,0:T(8,128)(2,1)} %get-tuple-element.46), channel_id=1, source_target_pairs={{0,32},{32,64},{64,96},{96,0},{1,33},{33,65},{65,97},{97,1},{2,34}... | collective-permute-start | bytes 2752520 | tf_op jit(solution)/shard_map/ppermute | solution.py:30
  110.5 43.0 %collective-permute-start.8 = (bf16[128,3584]{1,0:T(8,128)(2,1)}, bf16[128,3584]{1,0:T(8,128)(2,1)S(1)}, u32[]{:S(2)}, u32[]{:S(2)}) collective-permute-start(bf16[128,3584]{1,0:T(8,128)(2,1)} %get-tuple-element.47), channel_id=1, source_target_pairs={{0,64},{32,96},{64,0},{96,32},{1,65},{33,97},{65,1},{97,33},{2,66}... | collective-permute-start | bytes 2752520 | tf_op jit(solution)/shard_map/ppermute | solution.py:30
  114.4 39.1 %collective-permute-start.9 = (bf16[128,3584]{1,0:T(8,128)(2,1)}, bf16[128,3584]{1,0:T(8,128)(2,1)S(1)}, u32[]{:S(2)}, u32[]{:S(2)}) collective-permute-start(bf16[128,3584]{1,0:T(8,128)(2,1)} %get-tuple-element.48), channel_id=1, source_target_pairs={{0,96},{32,0},{64,32},{96,64},{1,97},{33,1},{65,33},{97,65},{2,98}... | collective-permute-start | bytes 2752520 | tf_op jit(solution)/shard_map/ppermute | solution.py:30
  119.6 36.2 %all-to-all-start.2 = ((bf16[4,32,3584]{2,1,0:T(8,128)(2,1)}), bf16[4,32,3584]{2,1,0:T(8,128)(2,1)}, u32[]{:S(2)}, u32[]{:S(2)}) async-start(bf16[4,32,3584]{2,1,0:T(8,128)(2,1)} %bitcast.15), calls=%async_computation.2 | async-start | bytes 1835008 | tf_op jit(solution)/shard_map/all_to_all | solution.py:550

commit v5 on v4

--- a/solution.py
+++ b/solution.py
@@ -541,14 +541,14 @@
         picks, here, crossed[0], first, starts[0], quarter, depth, None, [token]
     )
     second, token = traded(1, [token])
-    whole, token = placed_own(
-        picks, here, crossed[1], straight, starts[1], quarter, whole, [token]
-    )
-    replica_weight = placed_others(here, second, starts[1], quarter, whole, [token])
-
     partial = mixed(mixes, returned.reshape(-1, width))
     partial = lax.all_to_all(partial.reshape(N_X, steps * rows, width), X, 0, 0, tiled=True)
     combined = jnp.sum(partial.astype(jnp.float32), axis=0).astype(jnp.bfloat16)
+    whole, token = placed_own(
+        picks, here, crossed[1], straight, starts[1], quarter, whole, [token]
+    )
+    replica_weight = placed_others(here, second, starts[1], quarter, whole, [token, combined])
+
     return combined.reshape(steps, rows, width), replica_weight, replica_scale
 
 

time: 159 us -> 159 us (level)
    ppermute x11, waiting for transfers between devices: 55.1 us -> 49.1 us  [shifted(): lax.ppermute(block, axis, [(i, (i + distance) % count) for i in range(cou...]
    all_to_all x1, waiting for transfers between devices: 0.01 us -> 5.87 us  [local(): lax.all_to_all(partial.reshape(N_X, steps * rows, width), X, 0, 0, tiled=...]
  transfers between devices with their start and end apart: 14 -> 14, of which waited for: 7 -> 7; matrix products, arithmetic and copies ran while one was open for 1% -> 2% of each run, Pallas kernels for 26% -> 25%
where the time goes in v5:
time: 159 us; the launch traced here: 158 us
  waiting for transfers between devices  54.9 us (35%)
  Pallas kernels  41.8 us (26%)
  starting transfers between devices  36.9 us (23%)
  blocking collectives  9.77 us (6%)
  between operations  4.9 us (3%)
  local copies, waits for them, and re-layouts  4.13 us (3%)
  matrix products  2.91 us (2%)
  other arithmetic  2.66 us (2%)
    ppermute x11, waiting for transfers between devices, shifted(): lax.ppermute(block, axis, [(i, (i + distance) % count) for i in range(cou...  49.1 us
    pallas_call x11, Pallas kernels, ordered_call(): pl.pallas_call(body, out_shape=list(out_shape) + [TOKEN], in_specs=list(i...  21.3 us
    ppermute x11, starting transfers between devices, shifted(): lax.ppermute(block, axis, [(i, (i + distance) % count) for i in range(cou...  20.5 us
    pallas_call x1, Pallas kernels, serve(): pl.pallas_call(serve_kernel, in_specs=[SMEM, WHOLE, WHOLE, HBM, HBM, WHOL...  16 us
    psum x1, blocking collectives, local(): picks = lax.psum(jnp.where(jnp.arange(parts) == part, mine, 0), 'dp')  9.77 us
    all_to_all x1, starting transfers between devices, local(): lax.all_to_all(outgoing.reshape(N_EP, BLOCK, depth), EP, 0, 0, tiled=True)  7.4 us
    all_to_all x1, waiting for transfers between devices, local(): lax.all_to_all(partial.reshape(N_X, steps * rows, width), X, 0, 0, tiled=...  5.87 us
    all_to_all x1, starting transfers between devices, local(): lax.all_to_all(returned.reshape(N_YC, -1, width), ('y', 'c'), 0, 0, tiled...  4.74 us
  transfers between devices with their start and end apart: 14, of which 7 were waited for; matrix products, arithmetic and copies ran while one was open for 2% of the time, Pallas kernels for 25%

profile of v5, /device:TPU:0, one launch (start us, length us, event | category | flops | bytes accessed | tf_op | source)
XLA Modules:
  0.0 158.0 jit_solution(2376857829855793780)
XLA Ops:
  3.9 2.9 %convolution_convert_fusion.refs_2_ = bf16[512,1024]{1,0:T(8,128)(2,1)} fusion(bf16[1,1024]{1,0:T(2,128)(2,1)S(1)} %broadcast_in_dim.40, bf16[256,1024]{1,0:T(8,128)(2,1)} %bitcast.36, s32[264]{0:T(512)S(1)} %pad_add_fusion, s32[512]{0:T(512)S(1)} %iota_select_fusion, bf16[264]{0:T(512)(128)(2,1)S(1)} %pad.7.clone, bf16[264]{0:T(512)(128)(2,1)S(1)} %pad.6.clone), kind=kOutput, calls=%fused_computation | convolution fusion | flops 279646208 | bytes 1579072 | tf_op jit(solution)/shard_map/dot_general | solution.py:511
  6.8 7.4 %all-to-all-start = ((bf16[32,16,1024]{2,1,0:T(8,128)(2,1)}), bf16[32,16,1024]{2,1,0:T(8,128)(2,1)S(1)}, u32[]{:S(2)}, u32[]{:S(2)}) async-start(bf16[32,16,1024]{2,1,0:T(8,128)(2,1)} %bitcast.4), calls=%async_computation | async-start | bytes 2097152 | tf_op jit(solution)/shard_map/all_to_all | solution.py:512
  19.4 3.1 %shard_map.122 = (bf16[2,64,3584]{2,1,0:T(8,128)(2,1)}, bf16[2,128,3584]{2,1,0:T(8,128)(2,1)}, f32[8,128]{1,0:T(8,128)}) custom-call(s32[1]{0:T(128)} %bitcast.8.refs_0_.refs_1_, bf16[2,1024,3584]{2,1,0:T(8,128)(2,1)} %refs_1_.5, f32[8,128]{1,0:T(8,128)} %copy-done.5), custom_call_target="tpu_custom_call" | custom-call | flops 1000 | bytes 1000 | tf_op jit(solution)/shard_map/pallas_call | solution.py:44
  22.5 9.8 %psum.7 = s32[4]{0:T(128)S(1)} all-reduce(s32[4]{0:T(128)S(1)} %compare_select_fusion), channel_id=1, replica_groups=mesh['dp'=4,'xh'=2,'xl'=2,'y'=4,'c'=2] {'dp'}, use_global_device_ids=true, to_apply=%region_2.3 | all-reduce | flops 4 | bytes 32 | tf_op jit(solution)/shard_map/psum | solution.py:514
  32.4 3.3 %collective-permute-start = (bf16[2,64,3584]{2,1,0:T(8,128)(2,1)}, bf16[2,64,3584]{2,1,0:T(8,128)(2,1)S(1)}, u32[]{:S(2)}, u32[]{:S(2)}) collective-permute-start(bf16[2,64,3584]{2,1,0:T(8,128)(2,1)} %get-tuple-element.31), channel_id=1, source_target_pairs={{0,16},{16,0},{1,17},{17,1},{2,18},{18,2},{3,19},{19,3},{4,20},{20... | collective-permute-start | bytes 2752520 | tf_op jit(solution)/shard_map/ppermute | solution.py:30
  37.8 16.0 %shard_map.124 = (bf16[640,3584]{1,0:T(8,128)(2,1)}, f32[8,128]{1,0:T(8,128)S(1)}) custom-call(s32[2]{0:T(128)S(1)} %pad_add_fusion.2.me, bf16[512,1024]{1,0:T(8,128)(2,1)S(1)} %bitcast.31, bf16[256,1024]{1,0:T(8,128)(2,1)S(1)} %collective-permute-done.1.far, bf16[2,2,640,768]{3,2,1,0:T(8,128)(2,1)} %constant.185.clone.order, ...), custom_call_target="tpu_custom_call" | custom-call | flops 1000 | bytes 1000 | tf_op jit(solution)/shard_map/pallas_call | solution.py:357
  55.7 4.7 %all-to-all-start.1 = ((bf16[8,80,3584]{2,1,0:T(8,128)(2,1)}), bf16[8,80,3584]{2,1,0:T(8,128)(2,1)}, u32[]{:S(2)}, u32[]{:S(2)}) async-start(bf16[8,80,3584]{2,1,0:T(8,128)(2,1)} %bitcast.35), calls=%async_computation.1 | async-start | bytes 9175040 | tf_op jit(solution)/shard_map/all_to_all | solution.py:533
  60.4 2.8 %collective-permute-start.3 = (bf16[2,128,3584]{2,1,0:T(8,128)(2,1)}, bf16[2,128,3584]{2,1,0:T(8,128)(2,1)}, u32[]{:S(2)}, u32[]{:S(2)}) collective-permute-start(bf16[2,128,3584]{2,1,0:T(8,128)(2,1)} %get-tuple-element.39), channel_id=1, source_target_pairs={{0,16},{16,0},{1,17},{17,1},{2,18},{18,2},{3,19},{19,3},{4,20},{20... | collective-permute-start | bytes 5505032 | tf_op jit(solution)/shard_map/ppermute | solution.py:30
  63.3 2.5 %shard_map.125 = (bf16[64,3584]{1,0:T(8,128)(2,1)}, bf16[64,3584]{1,0:T(8,128)(2,1)}, bf16[64,3584]{1,0:T(8,128)(2,1)}, f32[8,128]{1,0:T(8,128)S(1)}) custom-call(s32[4]{0:T(128)S(1)} %dynamic_slice.16.refs_2_.refs_1_.refs_0_, bf16[2,64,3584]{2,1,0:T(8,128)(2,1)S(1)} %collective-permute-done.refs_1_.refs_2_, f32[8,128]{1,0:T(8,128)S(1)} %get-tuple-element.33.refs_2_), custom_call_target="tpu_custom_call" | custom-call | flops 1000 | bytes 1000 | tf_op jit(solution)/shard_map/pallas_call | solution.py:44
  66.9 3.3 %collective-permute-start.5 = (bf16[64,3584]{1,0:T(8,128)(2,1)}, bf16[64,3584]{1,0:T(8,128)(2,1)S(1)}, u32[]{:S(2)}, u32[]{:S(2)}) collective-permute-start(bf16[64,3584]{1,0:T(8,128)(2,1)} %get-tuple-element.41), channel_id=1, source_target_pairs={{0,64},{32,96},{64,0},{96,32},{1,65},{33,97},{65,1},{97,33},{2,66}... | collective-permute-start | bytes 1376264 | tf_op jit(solution)/shard_map/ppermute | solution.py:30
  72.4 7.3 %collective-permute-done.4.refs_3_ = bf16[64,3584]{1,0:T(8,128)(2,1)S(1)} collective-permute-done((bf16[64,3584]{1,0:T(8,128)(2,1)}, bf16[64,3584]{1,0:T(8,128)(2,1)S(1)}, u32[]{:S(2)}, u32[]{:S(2)}) %collective-permute-start.4) | collective-permute-done | bytes 458784 | tf_op jit(solution)/shard_map/ppermute | solution.py:30
  79.7 10.9 %collective-permute-done.5.refs_4_ = bf16[64,3584]{1,0:T(8,128)(2,1)S(1)} collective-permute-done((bf16[64,3584]{1,0:T(8,128)(2,1)}, bf16[64,3584]{1,0:T(8,128)(2,1)S(1)}, u32[]{:S(2)}, u32[]{:S(2)}) %collective-permute-start.5) | collective-permute-done | bytes 458784 | tf_op jit(solution)/shard_map/ppermute | solution.py:30
  90.6 2.3 %shard_map.129 = (bf16[256,3584]{1,0:T(8,128)(2,1)}, f32[8,128]{1,0:T(8,128)S(1)}) custom-call(s32[1]{0:T(128)S(6)} %select_n.135.refs_0_, bf16[2,1024,3584]{2,1,0:T(8,128)(2,1)} %refs_1_.5, f32[8,128]{1,0:T(8,128)S(1)} %get-tuple-element.43.refs_2_, bf16[64,3584]{1,0:T(8,128)(2,1)S(1)} %collective-permute-done.4.refs_3_, ...), custom_call_target="tpu_custom_call" | custom-call | flops 1000 | bytes 1000 | tf_op jit(solution)/shard_map/pallas_call | solution.py:44
  92.9 2.1 %collective-permute-start.10 = (bf16[256,3584]{1,0:T(8,128)(2,1)}, bf16[256,3584]{1,0:T(8,128)(2,1)}, u32[]{:S(2)}, u32[]{:S(2)}) collective-permute-start(bf16[256,3584]{1,0:T(8,128)(2,1)} %get-tuple-element.49), channel_id=1, source_target_pairs={{0,16},{16,0},{1,17},{17,1},{2,18},{18,2},{3,19},{19,3},{4,20},{20... | collective-permute-start | bytes 5505032 | tf_op jit(solution)/shard_map/ppermute | solution.py:30
  95.0 2.9 %shard_map.130 = (bf16[1,1024,3584]{2,1,0:T(8,128)(2,1)}, f32[8,128]{1,0:T(8,128)S(1)}) custom-call(s32[4]{0:T(128)S(1)} %dynamic_slice.16.refs_2_.refs_1_.refs_0_, s32[1]{0:T(128)} %bitcast.8.refs_0_.refs_1_, bf16[2,64,3584]{2,1,0:T(8,128)(2,1)S(1)} %collective-permute-done.refs_1_.refs_2_, bf16[64,3584]{1,0:T(8,128)(2,1)S(1)} %collective-permute-done.4.refs_3_, ...), custom_call_target="tpu_custom_call" | custom-call | flops 1000 | bytes 1000 | tf_op jit(solution)/shard_map/pallas_call | solution.py:44
  97.9 7.2 %collective-permute-done.3.refs_1_.refs_2_ = bf16[2,128,3584]{2,1,0:T(8,128)(2,1)} collective-permute-done((bf16[2,128,3584]{2,1,0:T(8,128)(2,1)}, bf16[2,128,3584]{2,1,0:T(8,128)(2,1)}, u32[]{:S(2)}, u32[]{:S(2)}) %collective-permute-start.3) | collective-permute-done | bytes 1835040 | tf_op jit(solution)/shard_map/ppermute | solution.py:30
  105.2 3.9 %shard_map.131 = (bf16[128,3584]{1,0:T(8,128)(2,1)}, bf16[128,3584]{1,0:T(8,128)(2,1)}, bf16[128,3584]{1,0:T(8,128)(2,1)}, f32[8,128]{1,0:T(8,128)S(1)}) custom-call(s32[4]{0:T(128)S(1)} %dynamic_slice.16.refs_2_.refs_1_.refs_0_, bf16[2,128,3584]{2,1,0:T(8,128)(2,1)} %collective-permute-done.3.refs_1_.refs_2_, f32[8,128]{1,0:T(8,128)S(1)} %get-tuple-element.45.refs_2_), custom_call_target="tpu_custom_call" | custom-call | flops 1000 | bytes 1000 | tf_op jit(solution)/shard_map/pallas_call | solution.py:44
  111.0 3.4 %collective-permute-start.8 = (bf16[128,3584]{1,0:T(8,128)(2,1)}, bf16[128,3584]{1,0:T(8,128)(2,1)S(1)}, u32[]{:S(2)}, u32[]{:S(2)}) collective-permute-start(bf16[128,3584]{1,0:T(8,128)(2,1)} %get-tuple-element.47), channel_id=1, source_target_pairs={{0,64},{32,96},{64,0},{96,32},{1,65},{33,97},{65,1},{97,33},{2,66}... | collective-permute-start | bytes 2752520 | tf_op jit(solution)/shard_map/ppermute | solution.py:30
  115.5 4.5 %shard_map.128 = bf16[128,3584]{1,0:T(8,128)(2,1)} custom-call(bf16[256,640]{1,0:T(8,128)(2,1)S(1)} %copy-done.2, bf16[640,3584]{1,0:T(8,128)(2,1)} %bitcast.14.returned), custom_call_target="tpu_custom_call" | custom-call | flops 1000 | bytes 1000 | tf_op jit(solution)/shard_map/pallas_call | solution.py:459
  120.0 4.2 %all-to-all-start.2 = ((bf16[4,32,3584]{2,1,0:T(8,128)(2,1)}), bf16[4,32,3584]{2,1,0:T(8,128)(2,1)}, u32[]{:S(2)}, u32[]{:S(2)}) async-start(bf16[4,32,3584]{2,1,0:T(8,128)(2,1)} %bitcast.15), calls=%async_computation.2 | async-start | bytes 1835008 | tf_op jit(solution)/shard_map/all_to_all | solution.py:545
  124.3 20.3 %collective-permute-done.10.refs_3_ = bf16[256,3584]{1,0:T(8,128)(2,1)} collective-permute-done((bf16[256,3584]{1,0:T(8,128)(2,1)}, bf16[256,3584]{1,0:T(8,128)(2,1)}, u32[]{:S(2)}, u32[]{:S(2)}) %collective-permute-start.10) | collective-permute-done | bytes 1835040 | tf_op jit(solution)/shard_map/ppermute | solution.py:30
  144.5 3.3 %shard_map.132 = (bf16[1,1024,3584]{2,1,0:T(8,128)(2,1)}, f32[8,128]{1,0:T(8,128)S(1)}) custom-call(s32[4]{0:T(128)S(1)} %dynamic_slice.16.refs_2_.refs_1_.refs_0_, s32[1]{0:T(128)} %bitcast.8.refs_0_.refs_1_, bf16[2,128,3584]{2,1,0:T(8,128)(2,1)} %collective-permute-done.3.refs_1_.refs_2_, ...), custom_call_target="tpu_custom_call", output_to_operand_aliasing={{0}: (4, {})} | custom-call | flops 1000 | bytes 1000 | tf_op jit(solution)/shard_map/pallas_call | solution.py:44
  147.9 5.9 %all-to-all-done.2 = bf16[4,32,3584]{2,1,0:T(8,128)(2,1)} async-done(((bf16[4,32,3584]{2,1,0:T(8,128)(2,1)}), bf16[4,32,3584]{2,1,0:T(8,128)(2,1)}, u32[]{:S(2)}, u32[]{:S(2)}) %all-to-all-start.2) | async-done | bytes 917536 | tf_op jit(solution)/shard_map/all_to_all | solution.py:545
  155.1 2.3 %shard_map.133 = (bf16[1,1024,3584]{2,1,0:T(8,128)(2,1)}, f32[8,128]{1,0:T(8,128)}) custom-call(s32[1]{0:T(128)} %bitcast.8.refs_0_.refs_1_, bf16[128,3584]{1,0:T(8,128)(2,1)S(1)} %collective-permute-done.7.refs_1_, bf16[128,3584]{1,0:T(8,128)(2,1)S(1)} %collective-permute-done.8.refs_2_, ...), custom_call_target="tpu_custom_call", output_to_operand_aliasing={{0}: (4, {})} | custom-call | flops 1000 | bytes 1000 | tf_op jit(solution)/shard_map/pallas_call | solution.py:44
  (69 shorter events, 16.8 us)
Async XLA Ops:
  3.9 10.4 %copy-start.8 = (s32[32]{0:T(128)S(1)}, s32[32]{0:T(128)}, u32[]{:S(2)}) copy-start(s32[32]{0:T(128)} %param.15) | copy-start | bytes 388
  3.9 12.9 %copy-start.3 = (bf16[2,3584]{1,0:T(2,128)(2,1)S(1)}, bf16[2,3584]{1,0:T(2,128)(2,1)}, u32[]{:S(2)}) copy-start(bf16[2,3584]{1,0:T(2,128)(2,1)} %scale.1) | copy-start | bytes 43012
  6.8 25.6 %all-to-all-start = ((bf16[32,16,1024]{2,1,0:T(8,128)(2,1)}), bf16[32,16,1024]{2,1,0:T(8,128)(2,1)S(1)}, u32[]{:S(2)}, u32[]{:S(2)}) async-start(bf16[32,16,1024]{2,1,0:T(8,128)(2,1)} %bitcast.4), calls=%async_computation | async-start | bytes 2097152 | tf_op jit(solution)/shard_map/all_to_all | solution.py:512
  16.8 0.6 copy-start.5
  22.5 15.3 %copy-start.4 = (f32[8,128]{1,0:T(8,128)S(1)}, f32[8,128]{1,0:T(8,128)}, u32[]{:S(2)}) copy-start(f32[8,128]{1,0:T(8,128)} %get-tuple-element.32.refs_0_) | copy-start | bytes 12292
  32.4 23.3 %collective-permute-start = (bf16[2,64,3584]{2,1,0:T(8,128)(2,1)}, bf16[2,64,3584]{2,1,0:T(8,128)(2,1)S(1)}, u32[]{:S(2)}, u32[]{:S(2)}) collective-permute-start(bf16[2,64,3584]{2,1,0:T(8,128)(2,1)} %get-tuple-element.31), channel_id=1, source_target_pairs={{0,16},{16,0},{1,17},{17,1},{2,18},{18,2},{3,19},{19,3},{4,20},{20... | collective-permute-start | bytes 2752520 | tf_op jit(solution)/shard_map/ppermute | solution.py:30
  35.8 2.0 %collective-permute-start.1 = (bf16[256,1024]{1,0:T(8,128)(2,1)S(1)}, bf16[256,1024]{1,0:T(8,128)(2,1)S(1)}, u32[]{:S(2)}, u32[]{:S(2)}) collective-permute-start(bf16[256,1024]{1,0:T(8,128)(2,1)S(1)} %slice_bitcast_fusion), channel_id=1, source_target_pairs={{0,1},{1,0},{2,3},{3,2},{4,5},{5,4},{6,7},{7,6},{8,9},{9,8},{10,11... | collective-permute-start | bytes 1572872 | tf_op jit(solution)/shard_map/ppermute | solution.py:30
  35.9 19.8 %collective-permute-start.2 = (bf16[1,3584]{1,0:T(2,128)(2,1)S(1)}, bf16[1,3584]{1,0:T(2,128)(2,1)S(1)}, u32[]{:S(2)}, u32[]{:S(2)}) collective-permute-start(bf16[1,3584]{1,0:T(2,128)(2,1)S(1)} %get-tuple-element.37), channel_id=1, source_target_pairs={{0,16},{16,0},{1,17},{17,1},{2,18},{18,2},{3,19},{19,3},{4,20},{20... | collective-permute-start | bytes 21512 | tf_op jit(solution)/shard_map/ppermute | solution.py:30
  55.7 15.5 %copy-start.6 = (f32[1,640]{1,0:T(1,128)S(1)}, f32[1,640]{1,0:T(1,128)}, u32[]{:S(2)}) copy-start(f32[1,640]{1,0:T(1,128)} %constant.186.clone) | copy-start | bytes 7684
  55.7 15.5 %copy-start.7 = (f32[1,640]{1,0:T(1,128)S(1)}, f32[1,640]{1,0:T(1,128)}, u32[]{:S(2)}) copy-start(f32[1,640]{1,0:T(1,128)} %constant.187.clone) | copy-start | bytes 7684
  55.7 59.9 %all-to-all-start.1 = ((bf16[8,80,3584]{2,1,0:T(8,128)(2,1)}), bf16[8,80,3584]{2,1,0:T(8,128)(2,1)}, u32[]{:S(2)}, u32[]{:S(2)}) async-start(bf16[8,80,3584]{2,1,0:T(8,128)(2,1)} %bitcast.35), calls=%async_computation.1 | async-start | bytes 9175040 | tf_op jit(solution)/shard_map/all_to_all | solution.py:533
  60.4 44.7 %collective-permute-start.3 = (bf16[2,128,3584]{2,1,0:T(8,128)(2,1)}, bf16[2,128,3584]{2,1,0:T(8,128)(2,1)}, u32[]{:S(2)}, u32[]{:S(2)}) collective-permute-start(bf16[2,128,3584]{2,1,0:T(8,128)(2,1)} %get-tuple-element.39), channel_id=1, source_target_pairs={{0,16},{16,0},{1,17},{17,1},{2,18},{18,2},{3,19},{19,3},{4,20},{20... | collective-permute-start | bytes 5505032 | tf_op jit(solution)/shard_map/ppermute | solution.py:30
  65.8 13.9 %collective-permute-start.4 = (bf16[64,3584]{1,0:T(8,128)(2,1)}, bf16[64,3584]{1,0:T(8,128)(2,1)S(1)}, u32[]{:S(2)}, u32[]{:S(2)}) collective-permute-start(bf16[64,3584]{1,0:T(8,128)(2,1)} %get-tuple-element.40), channel_id=1, source_target_pairs={{0,32},{32,64},{64,96},{96,0},{1,33},{33,65},{65,97},{97,1},{2,34}... | collective-permute-start | bytes 1376264 | tf_op jit(solution)/shard_map/ppermute | solution.py:30
  66.9 23.7 %collective-permute-start.5 = (bf16[64,3584]{1,0:T(8,128)(2,1)}, bf16[64,3584]{1,0:T(8,128)(2,1)S(1)}, u32[]{:S(2)}, u32[]{:S(2)}) collective-permute-start(bf16[64,3584]{1,0:T(8,128)(2,1)} %get-tuple-element.41), channel_id=1, source_target_pairs={{0,64},{32,96},{64,0},{96,32},{1,65},{33,97},{65,1},{97,33},{2,66}... | collective-permute-start | bytes 1376264 | tf_op jit(solution)/shard_map/ppermute | solution.py:30
  70.1 20.5 %collective-permute-start.6 = (bf16[64,3584]{1,0:T(8,128)(2,1)}, bf16[64,3584]{1,0:T(8,128)(2,1)S(1)}, u32[]{:S(2)}, u32[]{:S(2)}) collective-permute-start(bf16[64,3584]{1,0:T(8,128)(2,1)} %get-tuple-element.42), channel_id=1, source_target_pairs={{0,96},{32,0},{64,32},{96,64},{1,97},{33,1},{65,33},{97,65},{2,98}... | collective-permute-start | bytes 1376264 | tf_op jit(solution)/shard_map/ppermute | solution.py:30
  72.4 20.5 %copy-start.1 = (bf16[256,640]{1,0:T(8,128)(2,1)}, bf16[256,640]{1,0:T(8,128)(2,1)S(1)}, u32[]{:S(2)}) copy-start(bf16[256,640]{1,0:T(8,128)(2,1)S(1)} %get-tuple-element.35.mixes) | copy-start | bytes 983044
  92.9 51.6 %collective-permute-start.10 = (bf16[256,3584]{1,0:T(8,128)(2,1)}, bf16[256,3584]{1,0:T(8,128)(2,1)}, u32[]{:S(2)}, u32[]{:S(2)}) collective-permute-start(bf16[256,3584]{1,0:T(8,128)(2,1)} %get-tuple-element.49), channel_id=1, source_target_pairs={{0,16},{16,0},{1,17},{17,1},{2,18},{18,2},{3,19},{19,3},{4,20},{20... | collective-permute-start | bytes 5505032 | tf_op jit(solution)/shard_map/ppermute | solution.py:30
  97.9 17.6 %copy-start.2 = (bf16[256,640]{1,0:T(8,128)(2,1)S(1)}, bf16[256,640]{1,0:T(8,128)(2,1)}, u32[]{:S(2)}) copy-start(bf16[256,640]{1,0:T(8,128)(2,1)} %copy-done.1) | copy-start | bytes 983044
  109.0 46.1 %collective-permute-start.7 = (bf16[128,3584]{1,0:T(8,128)(2,1)}, bf16[128,3584]{1,0:T(8,128)(2,1)S(1)}, u32[]{:S(2)}, u32[]{:S(2)}) collective-permute-start(bf16[128,3584]{1,0:T(8,128)(2,1)} %get-tuple-element.46), channel_id=1, source_target_pairs={{0,32},{32,64},{64,96},{96,0},{1,33},{33,65},{65,97},{97,1},{2,34}... | collective-permute-start | bytes 2752520 | tf_op jit(solution)/shard_map/ppermute | solution.py:30
  111.0 44.1 %collective-permute-start.8 = (bf16[128,3584]{1,0:T(8,128)(2,1)}, bf16[128,3584]{1,0:T(8,128)(2,1)S(1)}, u32[]{:S(2)}, u32[]{:S(2)}) collective-permute-start(bf16[128,3584]{1,0:T(8,128)(2,1)} %get-tuple-element.47), channel_id=1, source_target_pairs={{0,64},{32,96},{64,0},{96,32},{1,65},{33,97},{65,1},{97,33},{2,66}... | collective-permute-start | bytes 2752520 | tf_op jit(solution)/shard_map/ppermute | solution.py:30
  114.5 40.7 %collective-permute-start.9 = (bf16[128,3584]{1,0:T(8,128)(2,1)}, bf16[128,3584]{1,0:T(8,128)(2,1)S(1)}, u32[]{:S(2)}, u32[]{:S(2)}) collective-permute-start(bf16[128,3584]{1,0:T(8,128)(2,1)} %get-tuple-element.48), channel_id=1, source_target_pairs={{0,96},{32,0},{64,32},{96,64},{1,97},{33,1},{65,33},{97,65},{2,98}... | collective-permute-start | bytes 2752520 | tf_op jit(solution)/shard_map/ppermute | solution.py:30
  120.0 33.7 %all-to-all-start.2 = ((bf16[4,32,3584]{2,1,0:T(8,128)(2,1)}), bf16[4,32,3584]{2,1,0:T(8,128)(2,1)}, u32[]{:S(2)}, u32[]{:S(2)}) async-start(bf16[4,32,3584]{2,1,0:T(8,128)(2,1)} %bitcast.15), calls=%async_computation.2 | async-start | bytes 1835008 | tf_op jit(solution)/shard_map/all_to_all | solution.py:545
  155.1 2.3 %copy-start = (bf16[32,3584]{1,0:T(8,128)(2,1)}, bf16[32,3584]{1,0:T(8,128)(2,1)S(1)}, u32[]{:S(2)}) copy-start(bf16[32,3584]{1,0:T(8,128)(2,1)S(1)} %reduce_sum.35.refs_6_) | copy-start | bytes 688132
